TPU v7x, 128 devices: a whole 4x4x4 slice. The times are simulated.
128 devices in a mesh: dom: 32 (over y, z, core), feat: 4 (over x).
Axes of the slice: x: 4, y: 4, z: 4, core: 2. Of those that a mesh axis runs over, the one named last changes fastest.
Arguments:
- features: bfloat16 [262144, 128], P('dom'), may hold values from -6 to 6
- weight: bfloat16 [128, 256], P(None, 'feat'), may hold values from -0.5 to 0.5
- attention: float32 [2, 4, 64], P(None, 'feat')
- bias: float32 [256], P('feat'), may hold values from -3 to 3
- cotangent: bfloat16 [256, 262144], P('feat', 'dom'), may hold values from -0.01171875 to 0.01171875
- local_pairs: int32 [2048, 5], P('dom'), may hold values from 0 to 63, as said below
- local_counts: int32 [2048, 5, 128], P('dom'), may hold values from 0 to 6
- remote_pairs: int32 [2048, 3], P('dom'), may hold values from 0 to 63, as said below
- remote_counts: int32 [2048, 3, 128], P('dom'), may hold values from 0 to 6
- send_rows: int32 [32, 32, 256], P('dom'), may hold values from 0 to 8191
- send_counts: int32 [32, 32], replicated, may hold values from 1 to 256
Outputs:
- output: bfloat16 [256, 262144], P('feat', 'dom')
- grad_weight: float32 [128, 256], P(None, 'feat')
- grad_attention: float32 [2, 4, 64], P(None, 'feat')
- grad_bias: float32 [256], P('feat')
Inputs may be any that keep to these rules, and one draw needn't show every extreme that they name: `local_pairs`: the 5 blocks of a row are different. `remote_pairs`: the 3 entries of a row are different.
All inputs are finite; a program needn't handle non-finite values.
Results may differ from a plain program's by a relative error of at most 0.0035.
The roundings to bfloat16 on the way count: a program that leaves them out, or rounds other values in their place, can miss the bound.
Values may be sent and summed in bfloat16 or wider, within the bound.
No kernel may reach another device: no remote copies, remote signals or barrier semaphores. Data moves between devices by JAX's collectives and lax.ppermute only.
A program may use at most 64 MiB of HBM per device.

v0:
```python
import jax
import jax.numpy as jnp
from jax import lax
from jax.sharding import PartitionSpec as P

BLK = 128
PEER_BLOCKS = 2


def leaky_relu(values):
    return jnp.where(values > 0, values, 0.2 * values)


def slope_of(values):
    return jnp.where(values > 0, 1.0, 0.2)


def per_device(
    features,
    weight,
    attention,
    bias,
    cotangent,
    local_pairs,
    local_counts,
    remote_pairs,
    remote_counts,
    send_rows,
    send_counts,
):
    node_count, in_width = features.shape
    out_width = weight.shape[1]
    head_count = attention.shape[1]
    head_width = out_width // head_count
    block_count = node_count // BLK
    peer_count = lax.axis_size("dom")
    capacity = PEER_BLOCKS * BLK
    halo_count = peer_count * PEER_BLOCKS
    offsets = jnp.arange(BLK, dtype=jnp.int32)
    band = (offsets[None, None, None, :] - offsets[None, None, :, None]) % BLK
    own_blocks = jnp.einsum(
        "bcf,fo->boc",
        features.reshape(block_count, BLK, in_width),
        weight,
        preferred_element_type=jnp.float32,
    ).astype(jnp.bfloat16)
    row_lists = send_rows[0]
    flat_rows = row_lists.reshape(-1)
    incoming = lax.dynamic_index_in_dim(send_counts, lax.axis_index("dom"), 1, False)
    recv_live = (jnp.arange(capacity, dtype=jnp.int32)[None, :] < incoming[:, None]).reshape(
        halo_count, BLK
    )
    flat_proj = own_blocks.transpose(1, 0, 2).reshape(out_width, node_count)
    outgoing = flat_proj[:, flat_rows].reshape(out_width, peer_count, capacity).transpose(1, 0, 2)
    halo_proj = lax.all_to_all(outgoing, "dom", split_axis=0, concat_axis=0, tiled=True)
    halo_blocks = (
        halo_proj.reshape(peer_count, out_width, PEER_BLOCKS, BLK)
        .transpose(0, 2, 1, 3)
        .reshape(halo_count, out_width, BLK)
    )
    table = jnp.concatenate([own_blocks, halo_blocks], 0).reshape(
        block_count + halo_count, head_count, head_width, BLK
    )
    table_float = table.astype(jnp.float32)
    score_src = jnp.sum(table_float * attention[0][None, :, :, None], axis=2)
    score_dst = jnp.sum(table_float[:block_count] * attention[1][None, :, :, None], axis=2)
    live_table = jnp.concatenate([jnp.ones((block_count, BLK), bool), recv_live], 0)
    pair_table = jnp.concatenate([local_pairs, remote_pairs + block_count], 1)
    count_table = jnp.concatenate([local_counts, remote_counts], 1)
    upstream = cotangent.reshape(head_count, head_width, block_count, BLK).transpose(2, 0, 1, 3)
    bias_heads = bias.reshape(head_count, head_width)
    batch_blocks = 4

    def one_turn(carry, turn_index):
        grad_rows, grad_scores = carry
        lead = turn_index * batch_blocks
        chosen = lax.dynamic_slice_in_dim(pair_table, lead, batch_blocks, 0)
        edge_counts = lax.dynamic_slice_in_dim(count_table, lead, batch_blocks, 0)
        source_proj = table[chosen]
        source_scores = score_src[chosen]
        source_live = live_table[chosen]
        valid = (band < edge_counts[..., None]) & source_live[:, :, None, :]
        valid = valid.transpose(0, 2, 1, 3)[:, None]
        dst_scores = lax.dynamic_slice_in_dim(score_dst, lead, batch_blocks, 0)
        self_scores = lax.dynamic_slice_in_dim(score_src, lead, batch_blocks, 0)
        self_proj = lax.dynamic_slice_in_dim(table_float, lead, batch_blocks, 0)
        grad_out = lax.dynamic_slice_in_dim(upstream, lead, batch_blocks, 0)
        grad_float = grad_out.astype(jnp.float32)
        pre_logit = (
            dst_scores[:, :, :, None, None] + source_scores.transpose(0, 2, 1, 3)[:, :, None, :, :]
        )
        logits = leaky_relu(pre_logit)
        pre_self = dst_scores + self_scores
        logit_self = leaky_relu(pre_self)
        highest = jnp.maximum(jnp.max(jnp.where(valid, logits, -jnp.inf), axis=(3, 4)), logit_self)
        raised = jnp.where(valid, jnp.exp(logits - highest[..., None, None]), 0.0)
        raised_self = jnp.exp(logit_self - highest)
        denom = jnp.sum(raised, axis=(3, 4)) + raised_self
        weights_low = raised.astype(jnp.bfloat16)
        summed = jnp.einsum(
            "ghrps,gphds->ghdr", weights_low, source_proj, preferred_element_type=jnp.float32
        )
        aggregate = (summed + raised_self[:, :, None, :] * self_proj) / denom[:, :, None, :]
        out_block = (aggregate + bias_heads[None, :, :, None]).astype(jnp.bfloat16)
        share = raised / denom[..., None, None]
        share_self = raised_self / denom
        grad_share = jnp.einsum(
            "ghdr,gphds->ghrps", grad_out, source_proj, preferred_element_type=jnp.float32
        )
        inner = jnp.sum(grad_float * aggregate, axis=2)
        grad_share_self = jnp.sum(grad_float * self_proj, axis=2)
        grad_pre = share * (grad_share - inner[..., None, None]) * slope_of(pre_logit)
        grad_pre_self = share_self * (grad_share_self - inner) * slope_of(pre_self)
        grad_dst_block = jnp.sum(grad_pre, axis=(3, 4)) + grad_pre_self
        grad_src_block = jnp.sum(grad_pre, axis=2).transpose(0, 2, 1, 3)
        grad_sources = jnp.einsum(
            "ghrps,ghdr->gphds",
            share.astype(jnp.bfloat16),
            grad_out,
            preferred_element_type=jnp.float32,
        )
        own_index = lead + jnp.arange(batch_blocks, dtype=jnp.int32)
        grad_rows = grad_rows.at[chosen].add(grad_sources)
        grad_rows = grad_rows.at[own_index].add(share_self[:, :, None, :] * grad_float)
        grad_scores = grad_scores.at[chosen].add(grad_src_block)
        grad_scores = grad_scores.at[own_index].add(grad_pre_self)
        return ((grad_rows, grad_scores), (out_block, grad_dst_block))

    start = (jnp.zeros(table.shape, jnp.float32), jnp.zeros(score_src.shape, jnp.float32))
    turn_count = block_count // batch_blocks
    (grad_rows, grad_src), (out_blocks, grad_dst) = lax.scan(
        one_turn, start, jnp.arange(turn_count, dtype=jnp.int32)
    )
    output = (
        out_blocks.reshape(block_count, head_count, head_width, BLK)
        .transpose(1, 2, 0, 3)
        .reshape(out_width, node_count)
    )
    grad_dst = grad_dst.reshape(block_count, head_count, BLK)
    source_side = attention[0][None, :, :, None]
    target_side = attention[1][None, :, :, None]
    grad_own = (
        grad_rows[:block_count]
        + grad_src[:block_count][:, :, None, :] * source_side
        + grad_dst[:, :, None, :] * target_side
    )
    grad_far = grad_rows[block_count:] + grad_src[block_count:][:, :, None, :] * source_side
    grad_far = (
        grad_far.reshape(peer_count, PEER_BLOCKS, out_width, BLK)
        .transpose(0, 2, 1, 3)
        .reshape(peer_count, out_width, capacity)
    )
    attention_src = jnp.einsum(
        "thc,thdc->hd", grad_src, table_float, precision=lax.Precision.HIGHEST
    )
    attention_dst = jnp.einsum(
        "bhc,bhdc->hd", grad_dst, table_float[:block_count], precision=lax.Precision.HIGHEST
    )
    grad_node_rows = grad_own.transpose(0, 3, 1, 2).reshape(node_count, out_width)
    returned = lax.all_to_all(grad_far, "dom", split_axis=0, concat_axis=0, tiled=True)
    grad_node_rows = grad_node_rows.at[flat_rows].add(
        returned.transpose(0, 2, 1).reshape(peer_count * capacity, out_width)
    )
    grad_weight = jnp.dot(
        features.astype(jnp.float32).T, grad_node_rows, precision=lax.Precision.HIGHEST
    )
    grad_bias = jnp.sum(cotangent.astype(jnp.float32), axis=1)
    summed_grads = lax.psum(
        (grad_weight, jnp.stack([attention_src, attention_dst]), grad_bias), "dom"
    )
    return (output, summed_grads[0], summed_grads[1], summed_grads[2])


def solution(mesh):
    return jax.shard_map(
        per_device,
        mesh=mesh,
        in_specs=(
            P("dom", None),
            P(None, "feat"),
            P(None, "feat", None),
            P("feat"),
            P("feat", "dom"),
            P("dom", None),
            P("dom", None, None),
            P("dom", None),
            P("dom", None, None),
            P("dom", None, None),
            P(),
        ),
        out_specs=(P("feat", "dom"), P(None, "feat"), P(None, "feat", None), P("feat")),
        check_vma=False,
    )
```

profile of v0, /device:TPU:1, one launch (start us, length us, event | category | flops | bytes accessed | tf_op | source)
XLA Modules:
  0.0 1170.7 jit_solution(15256411911419019861)
XLA Ops:
  6.3 29.9 %gather_fusion.3 = bf16[8192,64]{1,0:T(8,128)(2,1)} fusion(bf16[64,8192]{0,1:T(8,128)(2,1)} %bitcast.246, s32[8192]{0:T(1024)S(1)} %broadcast_clamp_fusion), kind=kCustom, calls=%fused_computation.3 | custom fusion | bytes 2129920 | tf_op jit(solution)/shard_map/gather | solution.py:54
  38.9 9.8 all-to-all-start
  73.9 878.2 %while.18 = (s32[]{:T(128)}, f32[128,1,64,128]{3,2,0,1:T(8,128)}, f32[128,1,128]{2,0,1:T(8,128)}, bf16[16,4,1,64,128]{4,3,1,2,0:T(8,128)(2,1)}, f32[16,4,1,128]{...) while((s32[]{:T(128)}, f32[128,1,64,128]{3,2,0,1:T(8,128)}, ...), condition=%wide.region_13.14_spmd.clone.clone, body=%wide.region_2.13_spmd.clone.clone.sunk | while | flops 228931200 | bytes 11342872 | solution.py:131
  80.4 9.3 select_reduce_fusion.4
  91.7 9.5 select_reduce_fusion.5
  135.3 9.3 select_reduce_fusion.4
  146.6 9.5 select_reduce_fusion.5
  190.2 9.3 select_reduce_fusion.4
  201.5 9.5 select_reduce_fusion.5
  245.1 9.3 select_reduce_fusion.4
  256.4 9.5 select_reduce_fusion.5
  300.0 9.3 select_reduce_fusion.4
  311.3 9.5 select_reduce_fusion.5
  354.9 9.3 select_reduce_fusion.4
  366.2 9.5 select_reduce_fusion.5
  409.8 9.3 select_reduce_fusion.4
  421.0 9.5 select_reduce_fusion.5
  464.6 9.3 select_reduce_fusion.4
  475.9 9.5 select_reduce_fusion.5
  519.5 9.3 select_reduce_fusion.4
  530.8 9.5 select_reduce_fusion.5
  574.4 9.3 select_reduce_fusion.4
  585.7 9.5 select_reduce_fusion.5
  640.6 9.5 select_reduce_fusion.5
  695.5 9.5 select_reduce_fusion.5
  750.3 9.5 select_reduce_fusion.5
  805.2 9.5 select_reduce_fusion.5
  860.1 9.5 select_reduce_fusion.5
  915.0 9.5 select_reduce_fusion.5
  980.8 16.6 %all-to-all-done.1 = f32[32,64,256]{2,1,0:T(8,128)} async-done(((f32[32,64,256]{2,1,0:T(8,128)}), f32[32,64,256]{2,1,0:T(8,128)}, u32[]{:S(2)}, u32[]{:S(2)}) %all-to-all-start.1) | async-done | bytes 2097184 | tf_op jit(solution)/shard_map/all_to_all | solution.py:160
  1001.3 44.0 %scatter_fusion.2 = f32[8192,64]{1,0:T(8,128)} fusion(f32[8192,64]{1,0:T(8,128)} %bitcast.245, s32[8192]{0:T(1024)S(1)} %bitcast.284, f32[8192,64]{1,0:T(8,128)} %bitcast.254), kind=kCustom, calls=%fused_computation.8 | custom fusion | flops 524288 | bytes 6324224 | tf_op jit(solution)/shard_map/scatter-add | solution.py:161
  1051.0 119.7 %all-reduce.1 = (f32[128,64]{0,1:T(8,128)}, f32[2,1,64]{2,1,0:T(1,128)}, f32[64]{0:T(128)}) all-reduce(f32[128,64]{0,1:T(8,128)S(1)} %convolution_bitcast_fusion.1, f32[2,1,64]{2,1,0:T(1,128)S(1)} %pad_maximum_fusion.5, f32[64]{0:T(128)S(1)} %convert_reduce_fusion), channel_id=1, replica_groups=mesh['dom'=32,'feat'=4] {'dom'}, use_global_device_ids=true, to_apply=%region_15.16 | all-reduce | flops 8384 | bytes 67072 | tf_op jit(solution)/shard_map/psum | solution.py:168
  (1154 shorter events, 690.8 us)
Async XLA Ops:
  36.2 12.5 %copy-start.28 = (s32[32,32]{1,0:T(8,128)S(1)}, s32[32,32]{1,0:T(8,128)}, u32[]{:S(2)}) copy-start(s32[32,32]{1,0:T(8,128)} %param.23) | copy-start | bytes 12292
  38.9 14.7 %copy-start.32 = (s32[64,3]{0,1:T(4,128)S(1)}, s32[64,3]{0,1:T(4,128)}, u32[]{:S(2)}) copy-start(s32[64,3]{0,1:T(4,128)} %param.20) | copy-start | bytes 2308
  38.9 14.7 %copy-start.31 = (s32[64,5]{0,1:T(8,128)S(1)}, s32[64,5]{0,1:T(8,128)}, u32[]{:S(2)}) copy-start(s32[64,5]{0,1:T(8,128)} %param.18) | copy-start | bytes 3844
  38.9 26.8 %all-to-all-start = ((bf16[32,64,256]{2,1,0:T(8,128)(2,1)}), bf16[32,64,256]{2,1,0:T(8,128)(2,1)}, u32[]{:S(2)}, u32[]{:S(2)}) async-start(bf16[32,64,256]{2,1,0:T(8,128)(2,1)} %bitcast.267), calls=%async_computation | async-start | bytes 2097152 | tf_op jit(solution)/shard_map/all_to_all | solution.py:55
  55.8 11.4 copy-start.29
  55.8 12.6 %copy-start.30 = (f32[64]{0:T(128)}, f32[64]{0:T(128)S(1)}, u32[]{:S(2)}) copy-start(f32[64]{0:T(128)S(1)} %get-tuple-element.307) | copy-start | bytes 772
  91.0 10.2 copy-start.9
  91.7 10.3 copy-start.23
  145.9 10.2 copy-start.9
  146.6 10.3 copy-start.23
  200.8 10.2 copy-start.9
  201.5 10.3 copy-start.23
  255.7 10.2 copy-start.9
  256.4 10.3 copy-start.23
  310.6 10.2 copy-start.9
  311.3 10.3 copy-start.23
  365.5 10.2 copy-start.9
  366.2 10.3 copy-start.23
  420.4 10.2 copy-start.9
  421.0 10.3 copy-start.23
  475.2 10.2 copy-start.9
  475.9 10.3 copy-start.23
  530.8 10.3 copy-start.23
  585.0 10.2 copy-start.9
  585.7 10.3 copy-start.23
  640.6 10.3 copy-start.23
  695.5 10.3 copy-start.23
  750.3 10.3 copy-start.23
  805.2 10.3 copy-start.23
  860.1 10.3 copy-start.23
  915.0 10.3 copy-start.23
  964.4 33.0 %all-to-all-start.1 = ((f32[32,64,256]{2,1,0:T(8,128)}), f32[32,64,256]{2,1,0:T(8,128)}, u32[]{:S(2)}, u32[]{:S(2)}) async-start(f32[32,64,256]{2,1,0:T(8,128)} %reshape.372), calls=%async_computation.1 | async-start | bytes 4194304 | tf_op jit(solution)/shard_map/all_to_all | solution.py:160
  (320 other events, 1317.0 us)
where the time goes:
time: 1190 us; the launch traced here: 1170 us
  other arithmetic  623 us (52%)
  local copies, waits for them, and re-layouts  216 us (18%)
  matrix products  158 us (13%)
  blocking collectives  120 us (10%)
  waiting for transfers between devices  24.2 us (2%)
  starting transfers between devices  14.5 us (1%)
  loops' own time  13.5 us (1%)
    reduce_sum x16, other arithmetic, one_turn(): denom = jnp.sum(raised, axis=(3, 4)) + raised_self  152 us
    reduce_max x16, other arithmetic, one_turn(): jnp.max(jnp.where(valid, logits, -jnp.inf), axis=(3, 4))  149 us
    psum x1, blocking collectives, per_device(): lax.psum((grad_weight, jnp.stack([attention_src, attention_dst]), grad_bi...  120 us
    scatter-add x16, other arithmetic, one_turn(): grad_rows = grad_rows.at[chosen].add(grad_sources)  87.3 us
    dot_general x16, matrix products, one_turn(): jnp.einsum('ghrps,ghdr->gphds', share.astype(jnp.bfloat16), grad_out, pre...  55 us
    gather x16, local copies, waits for them, and re-layouts, one_turn(): source_proj = table[chosen]  49.8 us
    dot_general x16, matrix products, one_turn(): jnp.einsum('ghrps,gphds->ghdr', weights_low, source_proj, preferred_eleme...  47.5 us
    dot_general x16, matrix products, one_turn(): jnp.einsum('ghdr,gphds->ghrps', grad_out, source_proj, preferred_element_...  45.6 us
  transfers between devices with their start and end apart: 2, of which 2 were waited for; matrix products, arithmetic and copies ran while one was open for 2% of the time, Pallas kernels for 0%

commit v1 on v0

v1 whole, which is shorter than its diff:
```python
import jax
import jax.numpy as jnp
from jax import lax
from jax.experimental import pallas as pl
from jax.experimental.pallas import tpu as pltpu
from jax.sharding import PartitionSpec as P

BLK = 128
PEER_BLOCKS = 2
SUB = 8
LOW = jnp.bfloat16
WIDE = jnp.float32
VMEM_LIMIT = 56 * 1024 * 1024
SCRATCH_TURNS = 2
GATHER_STEP = 32


def gather_kernel(rows_ref, live_ref, features_ref, out_ref, wide_ref, stage_ref):
    node_count = features_ref.shape[0]
    peer_count, capacity = rows_ref.shape
    step_count = capacity // GATHER_STEP

    def widen(turn, carry):
        lead = pl.multiple_of(turn * BLK, BLK)
        wide_ref[pl.ds(lead, BLK), :] = features_ref[pl.ds(lead, BLK), :].astype(WIDE)
        return carry

    lax.fori_loop(0, node_count // BLK, widen, 0)

    def one_peer(peer, carry):
        busy = (live_ref[peer] + GATHER_STEP - 1) // GATHER_STEP

        def fetch(step, inner):
            lead = pl.multiple_of(peer * capacity + step * GATHER_STEP, GATHER_STEP)
            for slot in range(GATHER_STEP):
                row = rows_ref[peer, step * GATHER_STEP + slot]
                stage_ref[pl.ds(lead + slot, 1), :] = wide_ref[pl.ds(row, 1), :]
            return inner

        def blank(step, inner):
            lead = pl.multiple_of(peer * capacity + step * GATHER_STEP, GATHER_STEP)
            stage_ref[pl.ds(lead, GATHER_STEP), :] = jnp.zeros((GATHER_STEP, stage_ref.shape[1]), WIDE)
            return inner

        lax.fori_loop(0, busy, fetch, 0)
        lax.fori_loop(busy, step_count, blank, 0)
        return carry

    lax.fori_loop(0, peer_count, one_peer, 0)

    def narrow(turn, carry):
        lead = pl.multiple_of(turn * BLK, BLK)
        out_ref[pl.ds(lead, BLK), :] = stage_ref[pl.ds(lead, BLK), :].astype(LOW)
        return carry

    lax.fori_loop(0, peer_count * capacity // BLK, narrow, 0)


def spread(row):
    return jnp.broadcast_to(row, (SUB, BLK))


def layer_kernel(
    incoming_ref,
    local_pairs_ref,
    remote_pairs_ref,
    own_ref,
    halo_ref,
    weight_ref,
    consts_ref,
    cotangent_ref,
    local_counts_ref,
    remote_counts_ref,
    out_ref,
    shares_ref,
    proj_ref,
    projt_ref,
    score_ref,
    self_score_ref,
    dst_score_ref,
    grad_ref,
    grad_src_ref,
    grad_self_ref,
    grad_dst_ref,
    mask_ref,
    weights_ref,
    share_ref,
):
    block_count = own_ref.shape[0] // BLK
    halo_count = halo_ref.shape[0] // BLK
    local_count = local_pairs_ref.shape[1]
    remote_count = remote_pairs_ref.shape[1]
    pair_count = local_count + remote_count
    head_width = weight_ref.shape[1]

    sub_index = lax.broadcasted_iota(jnp.int32, (SUB, BLK), 0)
    lane_index = lax.broadcasted_iota(jnp.int32, (SUB, BLK), 1)
    step_index = (sub_index - lane_index) & (SUB - 1)
    tile_index = ((lane_index + step_index) & (BLK - 1)) // SUB
    home = (lane_index & (SUB - 1)) == sub_index
    row_all = lax.broadcasted_iota(jnp.int32, (BLK, BLK), 0)
    lane_all = lax.broadcasted_iota(jnp.int32, (BLK, BLK), 1)
    mask_ref[...] = jnp.where(((row_all - lane_all) & (BLK - 1)) < SUB, 1.0, 0.0).astype(LOW)

    weight = weight_ref[...]
    weight_turned = weight.astype(WIDE).T.astype(LOW)

    def project(rows, index):
        proj_ref[index] = jnp.dot(rows, weight, preferred_element_type=WIDE).astype(LOW)
        turned = lax.dot_general(
            weight_turned, rows, (((1,), (1,)), ((), ())), preferred_element_type=WIDE
        ).astype(LOW)
        projt_ref[index] = turned
        return turned.astype(WIDE)

    def skew(row):
        placed = jnp.where(home, spread(row), 0.0)
        placed = placed + pltpu.roll(placed, BLK - 1, 1)
        placed = placed + pltpu.roll(placed, BLK - 2, 1)
        return placed + pltpu.roll(placed, BLK - 4, 1)

    def unskew(tile):
        tile = tile + pltpu.roll(tile, 1, 1)
        tile = tile + pltpu.roll(tile, 2, 1)
        tile = tile + pltpu.roll(tile, 4, 1)
        return jnp.sum(jnp.where(home, tile, 0.0), axis=0, keepdims=True)

    def clear(index):
        grad_src_ref[index] = jnp.zeros((SUB, BLK), WIDE)
        grad_ref[index] = jnp.zeros((head_width, BLK), WIDE)

    def own_table(block, carry):
        rows = own_ref[pl.ds(pl.multiple_of(block * BLK, BLK), BLK), :]
        turned = project(rows, block)
        source = jnp.sum(turned * consts_ref[0], axis=0, keepdims=True)
        target = jnp.sum(turned * consts_ref[1], axis=0, keepdims=True)
        score_ref[block] = skew(source)
        self_score_ref[block] = spread(source)
        dst_score_ref[block] = spread(target)
        clear(block)
        return carry

    lax.fori_loop(0, block_count, own_table, 0)

    def halo_table(block, carry):
        rows = halo_ref[pl.ds(pl.multiple_of(block * BLK, BLK), BLK), :]
        turned = project(rows, block_count + block)
        source = jnp.sum(turned * consts_ref[0], axis=0, keepdims=True)
        slot = (block % PEER_BLOCKS) * BLK + lane_index[:1]
        live = slot < incoming_ref[block // PEER_BLOCKS]
        score_ref[block_count + block] = skew(jnp.where(live, source, -jnp.inf))
        clear(block_count + block)
        return carry

    lax.fori_loop(0, halo_count, halo_table, 0)

    def leaky(values):
        return jnp.maximum(values, 0.2 * values)

    def widen_band(tile, target_ref, turn, pair):
        doubled = jnp.concatenate([tile, tile], 0).astype(LOW)
        for part in range(BLK // (2 * SUB)):
            lead = pair * BLK + part * 2 * SUB
            target_ref[turn, lead : lead + 2 * SUB, :] = (
                doubled * mask_ref[part * 2 * SUB : (part + 1) * 2 * SUB, :]
            )

    def one_block(block, turn):
        nodes = pl.ds(pl.multiple_of(block * BLK, BLK), BLK)
        upstream = cotangent_ref[:, nodes]
        upstream_wide = upstream.astype(WIDE)
        chosen = [local_pairs_ref[block, k] for k in range(local_count)]
        chosen += [remote_pairs_ref[block, k] + block_count for k in range(remote_count)]
        counts = [local_counts_ref[block, k : k + 1, :] for k in range(local_count)]
        counts += [remote_counts_ref[block, k : k + 1, :] for k in range(remote_count)]
        target_score = dst_score_ref[block]
        pre_self = target_score + self_score_ref[block]
        logit_self = leaky(pre_self)
        pre = [target_score + score_ref[index] for index in chosen]
        logits = [
            jnp.where(step_index < spread(count), leaky(value), -jnp.inf)
            for value, count in zip(pre, counts)
        ]
        top = logits[0]
        for logit in logits[1:]:
            top = jnp.maximum(top, logit)
        top = jnp.maximum(spread(jnp.max(top, axis=0, keepdims=True)), logit_self)
        raised = [jnp.exp(logit - top) for logit in logits]
        raised_self = jnp.exp(logit_self - top)
        denom = raised[0]
        for value in raised[1:]:
            denom = denom + value
        denom = spread(jnp.sum(denom, axis=0, keepdims=True)) + raised_self
        scale = 1.0 / denom
        share = [value * scale for value in raised]
        share_self = raised_self * scale
        for pair in range(pair_count):
            widen_band(raised[pair], weights_ref, turn, pair)
            widen_band(share[pair], share_ref, turn, pair)
        sources = jnp.concatenate([projt_ref[index] for index in chosen], 1)
        summed = jnp.dot(sources, weights_ref[turn], preferred_element_type=WIDE)
        self_wide = projt_ref[block].astype(WIDE)
        aggregate = (summed + raised_self[:1] * self_wide) * scale[:1]
        out_ref[:, nodes] = (aggregate + consts_ref[2]).astype(LOW)
        inner = spread(jnp.sum(upstream_wide * aggregate, axis=0, keepdims=True))
        grad_share_self = spread(jnp.sum(upstream_wide * self_wide, axis=0, keepdims=True))
        grad_self = share_self * (grad_share_self - inner) * jnp.where(pre_self > 0, 1.0, 0.2)
        total = None
        for pair in range(pair_count):
            product = jnp.dot(proj_ref[chosen[pair]], upstream, preferred_element_type=WIDE)
            grad_share = product[:SUB]
            for part in range(1, BLK // SUB):
                grad_share = jnp.where(
                    tile_index == part, product[part * SUB : (part + 1) * SUB], grad_share
                )
            grad_pre = share[pair] * (grad_share - inner) * jnp.where(pre[pair] > 0, 1.0, 0.2)
            grad_src_ref[chosen[pair]] += grad_pre
            total = grad_pre if total is None else total + grad_pre
        grad_self_ref[block] = grad_self
        grad_dst_ref[block] = spread(jnp.sum(total, axis=0, keepdims=True)) + grad_self
        grad_sources = lax.dot_general(
            upstream, share_ref[turn], (((1,), (1,)), ((), ())), preferred_element_type=WIDE
        )
        for pair in range(pair_count):
            grad_ref[chosen[pair]] += grad_sources[:, pair * BLK : (pair + 1) * BLK]
        grad_ref[block] += share_self[:1] * upstream_wide

    def one_turn(turn, carry):
        for part in range(SCRATCH_TURNS):
            one_block(turn * SCRATCH_TURNS + part, part)
        return carry

    lax.fori_loop(0, block_count // SCRATCH_TURNS, one_turn, 0)

    def finish(index, rows, own, carry):
        grad_weight, from_src, from_dst = carry
        parts = []
        for part in range(2):
            at = index * 2 + part
            table = at if own else at + block_count
            turned = projt_ref[table].astype(WIDE)
            source = unskew(grad_src_ref[table])
            if own:
                source = source + grad_self_ref[at][:1]
            grad = grad_ref[table] + consts_ref[0] * source
            from_src = from_src + turned * source
            if own:
                target = grad_dst_ref[at][:1]
                grad = grad + consts_ref[1] * target
                from_dst = from_dst + turned * target
            high = grad.astype(LOW)
            low = (grad - high.astype(WIDE)).astype(LOW)
            parts.append(jnp.concatenate([high, low], 0))
        grad_weight = grad_weight + jnp.dot(
            jnp.concatenate(parts, 1), rows, preferred_element_type=WIDE
        )
        return grad_weight, from_src, from_dst

    def finish_own(index, carry):
        rows = own_ref[pl.ds(pl.multiple_of(index * 2 * BLK, BLK), 2 * BLK), :]
        carry = finish(index, rows, True, carry[:3]) + carry[3:]
        nodes = pl.ds(pl.multiple_of(index * 2 * BLK, BLK), 2 * BLK)
        cotangent = cotangent_ref[:, nodes].astype(WIDE)
        return carry[:3] + (carry[3] + cotangent[:, :BLK] + cotangent[:, BLK:],)

    def finish_halo(index, carry):
        rows = halo_ref[pl.ds(pl.multiple_of(index * 2 * BLK, BLK), 2 * BLK), :]
        return finish(index, rows, False, carry)

    zero = jnp.zeros((head_width, BLK), WIDE)
    carry = (jnp.zeros((2 * head_width, own_ref.shape[1]), WIDE), zero, zero, zero)
    carry = lax.fori_loop(0, block_count // 2, finish_own, carry)
    grad_bias = carry[3]
    grad_weight, from_src, from_dst = lax.fori_loop(0, halo_count // 2, finish_halo, carry[:3])
    grad_weight = grad_weight[:head_width] + grad_weight[head_width:]
    lanes = lax.broadcasted_iota(jnp.int32, (head_width, BLK), 1)
    extra = jnp.zeros((head_width, BLK), WIDE)
    for place, value in enumerate((from_src, from_dst, grad_bias)):
        extra = jnp.where(lanes == place, jnp.sum(value, axis=1, keepdims=True), extra)
    shares_ref[...] = jnp.zeros(shares_ref.shape, WIDE)
    peers = shares_ref.shape[0]
    each = head_width // peers
    for peer in range(peers):
        shares_ref[peer, :each, :] = grad_weight[peer * each : (peer + 1) * each]
        shares_ref[peer, each : 2 * each, :] = extra[peer * each : (peer + 1) * each]


def vmem():
    return pl.BlockSpec(memory_space=pltpu.VMEM)


def smem():
    return pl.BlockSpec(memory_space=pltpu.SMEM)


def per_device(
    features,
    weight,
    attention,
    bias,
    cotangent,
    local_pairs,
    local_counts,
    remote_pairs,
    remote_counts,
    send_rows,
    send_counts,
):
    node_count, in_width = features.shape
    head_width = weight.shape[1]
    block_count = node_count // BLK
    peer_count = lax.axis_size("dom")
    capacity = PEER_BLOCKS * BLK
    halo_count = peer_count * PEER_BLOCKS
    slots = peer_count * capacity
    table_count = block_count + halo_count
    pair_rows = (local_pairs.shape[1] + remote_pairs.shape[1]) * BLK
    me = lax.axis_index("dom")
    outgoing_live = lax.dynamic_index_in_dim(send_counts, me, 0, False)
    incoming_live = lax.dynamic_index_in_dim(send_counts, me, 1, False)
    outgoing = pl.pallas_call(
        gather_kernel,
        out_shape=jax.ShapeDtypeStruct((slots, in_width), LOW),
        in_specs=[smem(), smem(), vmem()],
        out_specs=vmem(),
        scratch_shapes=[
            pltpu.VMEM((node_count, in_width), WIDE),
            pltpu.VMEM((slots, in_width), WIDE),
        ],
        compiler_params=pltpu.CompilerParams(vmem_limit_bytes=VMEM_LIMIT),
        name="gather_rows",
    )(send_rows[0], outgoing_live, features)
    halo = lax.all_to_all(
        outgoing.reshape(peer_count, capacity, in_width), "dom", 0, 0, tiled=True
    ).reshape(slots, in_width)
    consts = jnp.broadcast_to(
        jnp.concatenate([attention[:, 0], bias[None]], 0)[:, :, None], (3, head_width, BLK)
    )
    output, shares = pl.pallas_call(
        layer_kernel,
        out_shape=(
            jax.ShapeDtypeStruct((head_width, node_count), LOW),
            jax.ShapeDtypeStruct((peer_count, SUB, in_width), WIDE),
        ),
        in_specs=[smem(), smem(), smem()] + [vmem()] * 7,
        out_specs=(vmem(), vmem()),
        scratch_shapes=[
            pltpu.VMEM((table_count, BLK, head_width), LOW),
            pltpu.VMEM((table_count, head_width, BLK), LOW),
            pltpu.VMEM((table_count, SUB, BLK), WIDE),
            pltpu.VMEM((block_count, SUB, BLK), WIDE),
            pltpu.VMEM((block_count, SUB, BLK), WIDE),
            pltpu.VMEM((table_count, head_width, BLK), WIDE),
            pltpu.VMEM((table_count, SUB, BLK), WIDE),
            pltpu.VMEM((block_count, SUB, BLK), WIDE),
            pltpu.VMEM((block_count, SUB, BLK), WIDE),
            pltpu.VMEM((BLK, BLK), LOW),
            pltpu.VMEM((SCRATCH_TURNS, pair_rows, BLK), LOW),
            pltpu.VMEM((SCRATCH_TURNS, pair_rows, BLK), LOW),
        ],
        compiler_params=pltpu.CompilerParams(vmem_limit_bytes=VMEM_LIMIT),
        name="attention_layer",
    )(
        incoming_live,
        local_pairs,
        remote_pairs,
        features,
        halo,
        weight,
        consts,
        cotangent,
        local_counts,
        remote_counts,
    )
    mine = jnp.sum(lax.all_to_all(shares, "dom", 0, 0, tiled=True), axis=0)
    summed = lax.all_to_all(
        jnp.broadcast_to(mine[None], shares.shape), "dom", 0, 0, tiled=True
    )
    each = head_width // peer_count
    grad_weight = summed[:, :each].reshape(head_width, in_width).T
    extra = summed[:, each : 2 * each, :3].reshape(head_width, 3).T
    return output, grad_weight, extra[:2, None], extra[2]


def solution(mesh):
    return jax.shard_map(
        per_device,
        mesh=mesh,
        in_specs=(
            P("dom", None),
            P(None, "feat"),
            P(None, "feat", None),
            P("feat"),
            P("feat", "dom"),
            P("dom", None),
            P("dom", None, None),
            P("dom", None),
            P("dom", None, None),
            P("dom", None, None),
            P(),
        ),
        out_specs=(P("feat", "dom"), P(None, "feat"), P(None, "feat", None), P("feat")),
        check_vma=False,
    )
```

time: 1190 us -> 181 us (0.15); the launches traced: 1170 us -> 180 us
  other arithmetic: 623 us -> 0.04 us
  local copies, waits for them, and re-layouts: 216 us -> 8.84 us
  matrix products: 158 us -> 0 us
  Pallas kernels: 0 us -> 112 us
  blocking collectives: 120 us -> 23.4 us
  loops' own time: 13.5 us -> 0 us
    scatter-add x65 -> x0, other arithmetic: 232 us -> none  [the longest x16 87.3 us: one_turn(): grad_rows = grad_rows.at[chosen].add(grad_sources)]
    reduce_sum x35 -> x1, other arithmetic: 171 us -> 0.04 us  [per_device(): mine = jnp.sum(lax.all_to_all(shares, 'dom', 0, 0, tiled=True), axis=0)]
    dot_general x52 -> x0, matrix products: 158 us -> none  [the longest x16 55 us: one_turn(): jnp.einsum('ghrps,ghdr->gphds', share.astype(jnp.bfloat16), grad_out, pre...]
    reduce_max x16 -> x0, other arithmetic: 149 us -> none  [one_turn(): jnp.max(jnp.where(valid, logits, -jnp.inf), axis=(3, 4))]
    psum x1 -> x0, blocking collectives: 120 us -> none  [per_device(): lax.psum((grad_weight, jnp.stack([attention_src, attention_dst]), grad_bi...]
    gather x49 -> x0, local copies, waits for them, and re-layouts: 117 us -> none  [the longest x16 49.8 us: one_turn(): source_proj = table[chosen]]
    pallas_call x0 -> x2, Pallas kernels: none -> 112 us  [the longest x1 95.4 us: per_device(): pl.pallas_call(layer_kernel, out_shape=(jax.ShapeDtypeStruct((head_width,...]
    mul x32 -> x0, other arithmetic: 31.7 us -> none  [the longest x16 20.7 us: one_turn(): raised_self[:, :, None, :] * self_proj]
  transfers between devices with their start and end apart: 2 -> 1, of which waited for: 2 -> 1; matrix products, arithmetic and copies ran while one was open for 2% -> 2% of each run, Pallas kernels for 0% -> 0%
where the time goes in v1:
time: 181 us; the launch traced here: 180 us
  Pallas kernels  112 us (62%)
  waiting for transfers between devices  23.9 us (13%)
  blocking collectives  23.4 us (13%)
  starting transfers between devices  10.8 us (6%)
  local copies, waits for them, and re-layouts  8.84 us (5%)
    pallas_call x1, Pallas kernels, per_device(): pl.pallas_call(layer_kernel, out_shape=(jax.ShapeDtypeStruct((head_width,...  95.4 us
    all_to_all x1, waiting for transfers between devices, per_device(): lax.all_to_all(outgoing.reshape(peer_count, capacity, in_width), 'dom', 0...  23.9 us
    pallas_call x1, Pallas kernels, per_device(): pl.pallas_call(gather_kernel, out_shape=jax.ShapeDtypeStruct((slots, in_w...  17 us
    all_to_all x1, blocking collectives, per_device(): mine = jnp.sum(lax.all_to_all(shares, 'dom', 0, 0, tiled=True), axis=0)  12.2 us
    all_to_all x1, blocking collectives, per_device(): lax.all_to_all(jnp.broadcast_to(mine[None], shares.shape), 'dom', 0, 0, t...  11.3 us
    all_to_all x1, starting transfers between devices, per_device(): lax.all_to_all(outgoing.reshape(peer_count, capacity, in_width), 'dom', 0...  10.8 us
    unnamed x23, local copies, waits for them, and re-layouts  4.95 us
  transfers between devices with their start and end apart: 1, of which 1 were waited for; matrix products, arithmetic and copies ran while one was open for 2% of the time, Pallas kernels for 0%

profile of v1, /device:TPU:1, one launch (start us, length us, event | category | flops | bytes accessed | tf_op | source)
XLA Modules:
  0.0 180.0 jit_solution(18419902532917816284)
XLA Ops:
  0.6 0.0 copy-start
  0.6 0.7 copy-done
  1.4 0.5 dynamic-slice_bitcast_fusion.live_ref
  1.9 17.0 %gather_rows.1 = bf16[8192,128]{1,0:T(8,128)(2,1)} custom-call(s32[32,256]{1,0:T(8,128)} %bitcast.20, s32[32]{0:T(128)} %dynamic-slice_bitcast_fusion.live_ref, bf16[8192,128]{1,0:T(8,128)(2,1)} %own_ref.1), custom_call_target="tpu_custom_call" | custom-call | tf_op jit(solution)/shard_map/gather_rows/pallas_call | solution.py:321
  18.8 0.0 copy-start.2
  18.8 0.0 copy-start.4
  18.9 0.0 copy-start.7
  18.9 0.0 copy-start.8
  18.9 10.8 %all-to-all-start = ((bf16[32,256,128]{2,1,0:T(8,128)(2,1)}), bf16[32,256,128]{2,1,0:T(8,128)(2,1)S(1)}, u32[]{:S(2)}, u32[]{:S(2)}) async-start(bf16[32,256,128]{2,1,0:T(8,128)(2,1)} %bitcast.18), calls=%async_computation | async-start | bytes 4194304 | tf_op jit(solution)/shard_map/all_to_all | solution.py:333
  29.7 0.0 copy-done.2
  29.7 0.8 copy.32.local_counts_ref
  30.5 0.0 copy-done.3
  30.5 0.7 copy.33.remote_counts_ref
  31.2 0.0 copy-done.5
  31.2 0.7 copy.29.local_pairs_ref
  31.9 0.0 copy-done.6
  31.9 0.7 copy.30.remote_pairs_ref
  32.7 0.0 copy-done.4
  32.7 0.7 copy.31.weight_ref
  33.4 0.7 dynamic-slice_reduce_fusion.incoming_ref
  34.1 0.0 copy-done.7
  34.1 0.0 copy-done.8
  34.1 23.9 %all-to-all-done = bf16[32,256,128]{2,1,0:T(8,128)(2,1)S(1)} async-done(((bf16[32,256,128]{2,1,0:T(8,128)(2,1)}), bf16[32,256,128]{2,1,0:T(8,128)(2,1)S(1)}, u32[]{:S(2)}, u32[]{:S(2)}) %all-to-all-start) | async-done | bytes 2097184 | tf_op jit(solution)/shard_map/all_to_all | solution.py:333
  58.0 0.9 broadcast_in_dim.9.consts_ref
  58.9 0.5 copy-done.1
  59.4 95.4 %attention_layer.1 = (bf16[64,8192]{1,0:T(8,128)(2,1)}, f32[32,8,128]{2,1,0:T(8,128)}) custom-call(s32[32]{0:T(128)} %dynamic-slice_reduce_fusion.incoming_ref, s32[64,5]{1,0:T(8,128)} %copy.29.local_pairs_ref, s32[64,3]{1,0:T(8,128)} %copy.30.remote_pairs_ref, bf16[8192,128]{1,0:T(8,128)(2,1)} %own_ref.1, bf16[8192,128]{1,0:T(8,128)(2,1)} %bitcast.17, ...), custom_call_target="tpu_custom_call" | custom-call | tf_op jit(solution)/shard_map/attention_layer/pallas_call | solution.py:339
  154.8 12.2 %all_to_all.15 = f32[32,8,128]{2,1,0:T(8,128)S(1)} all-to-all(f32[32,8,128]{2,1,0:T(8,128)} %get-tuple-element.7), channel_id=1, replica_groups=mesh['dom'=32,'feat'=4] {'dom'}, dimensions={0} | all-to-all | bytes 262144 | tf_op jit(solution)/shard_map/all_to_all | solution.py:375
  167.0 11.3 %all_to_all.16 = f32[32,8,128]{2,1,0:T(8,128)S(1)} all-to-all(f32[32,8,128]{2,1,0:T(8,128)S(1)} %broadcast_in_dim.20), channel_id=1, replica_groups=mesh['dom'=32,'feat'=4] {'dom'}, dimensions={0} | all-to-all | bytes 262144 | tf_op jit(solution)/shard_map/all_to_all | solution.py:376
  178.3 0.1 copy.36
  178.3 0.6 slice.14
  178.9 0.5 slice_bitcast_fusion
  179.4 0.6 slice.16
  (8 shorter events, 0.1 us)
Async XLA Ops:
  0.6 0.7 copy-start
  18.8 10.9 %copy-start.2 = (s32[64,5,128]{2,0,1:T(8,128)S(1)}, s32[64,5,128]{2,0,1:T(8,128)}, u32[]{:S(2)}) copy-start(s32[64,5,128]{2,0,1:T(8,128)} %param.17) | copy-start | bytes 491524
  18.8 11.7 %copy-start.3 = (s32[64,3,128]{2,0,1:T(8,128)S(1)}, s32[64,3,128]{2,0,1:T(8,128)}, u32[]{:S(2)}) copy-start(s32[64,3,128]{2,0,1:T(8,128)} %param.19) | copy-start | bytes 294916
  18.8 12.4 %copy-start.5 = (s32[64,5]{0,1:T(8,128)S(1)}, s32[64,5]{0,1:T(8,128)}, u32[]{:S(2)}) copy-start(s32[64,5]{0,1:T(8,128)} %param.16) | copy-start | bytes 3844
  18.8 13.1 %copy-start.6 = (s32[64,3]{0,1:T(4,128)S(1)}, s32[64,3]{0,1:T(4,128)}, u32[]{:S(2)}) copy-start(s32[64,3]{0,1:T(4,128)} %param.18) | copy-start | bytes 2308
  18.8 13.8 %copy-start.4 = (bf16[128,64]{0,1:T(8,128)(2,1)S(1)}, bf16[128,64]{0,1:T(8,128)(2,1)}, u32[]{:S(2)}) copy-start(bf16[128,64]{0,1:T(8,128)(2,1)} %param.12) | copy-start | bytes 49156
  18.9 15.2 %copy-start.7 = (f32[2,1,64]{2,1,0:T(1,128)S(1)}, f32[2,1,64]{2,1,0:T(1,128)}, u32[]{:S(2)}) copy-start(f32[2,1,64]{2,1,0:T(1,128)} %param.13) | copy-start | bytes 1540
  18.9 15.2 %copy-start.8 = (f32[64]{0:T(128)S(1)}, f32[64]{0:T(128)}, u32[]{:S(2)}) copy-start(f32[64]{0:T(128)} %param.14) | copy-start | bytes 772
  18.9 39.1 %all-to-all-start = ((bf16[32,256,128]{2,1,0:T(8,128)(2,1)}), bf16[32,256,128]{2,1,0:T(8,128)(2,1)S(1)}, u32[]{:S(2)}, u32[]{:S(2)}) async-start(bf16[32,256,128]{2,1,0:T(8,128)(2,1)} %bitcast.18), calls=%async_computation | async-start | bytes 4194304 | tf_op jit(solution)/shard_map/all_to_all | solution.py:333
  58.0 1.4 copy-start.1

commit v2 on v1

v2 whole, which is shorter than its diff:
```python
import jax
import jax.numpy as jnp
from jax import lax
from jax.experimental import pallas as pl
from jax.experimental.pallas import tpu as pltpu
from jax.sharding import PartitionSpec as P

BLK = 128
PEER_BLOCKS = 2
SUB = 8
LOW = jnp.bfloat16
WIDE = jnp.float32
VMEM_LIMIT = 32 * 1024 * 1024
SCRATCH_TURNS = 4
NEAR_GROUP = 4
GATHER_STEP = 32


def gather_kernel(rows_ref, live_ref, features_ref, out_ref, wide_ref, stage_ref):
    node_count = features_ref.shape[0]
    peer_count = live_ref.shape[0]
    capacity = rows_ref.shape[0] // peer_count
    step_count = capacity // GATHER_STEP

    def widen(turn, carry):
        lead = pl.multiple_of(turn * BLK, BLK)
        wide_ref[pl.ds(lead, BLK), :] = features_ref[pl.ds(lead, BLK), :].astype(WIDE)
        return carry

    lax.fori_loop(0, node_count // BLK, widen, 0, unroll=4)

    def one_peer(peer, carry):
        busy = (live_ref[peer] + GATHER_STEP - 1) // GATHER_STEP

        def fetch(step, inner):
            lead = pl.multiple_of(peer * capacity + step * GATHER_STEP, GATHER_STEP)
            for slot in range(GATHER_STEP):
                row = rows_ref[lead + slot]
                stage_ref[pl.ds(lead + slot, 1), :] = wide_ref[pl.ds(row, 1), :]
            return inner

        def blank(step, inner):
            lead = pl.multiple_of(peer * capacity + step * GATHER_STEP, GATHER_STEP)
            stage_ref[pl.ds(lead, GATHER_STEP), :] = jnp.zeros((GATHER_STEP, stage_ref.shape[1]), WIDE)
            return inner

        lax.fori_loop(0, busy, fetch, 0)
        lax.fori_loop(busy, step_count, blank, 0)
        return carry

    lax.fori_loop(0, peer_count, one_peer, 0)

    def narrow(turn, carry):
        lead = pl.multiple_of(turn * BLK, BLK)
        out_ref[pl.ds(lead, BLK), :] = stage_ref[pl.ds(lead, BLK), :].astype(LOW)
        return carry

    lax.fori_loop(0, peer_count * capacity // BLK, narrow, 0, unroll=4)


def spread(row):
    return jnp.broadcast_to(row, (SUB, BLK))


def leaky(values):
    return jnp.maximum(values, 0.2 * values)


def slope_of(values):
    return jnp.where(values > 0, 1.0, 0.2)


def at_block(index, blocks=1):
    return pl.ds(pl.multiple_of(index * blocks * BLK, BLK), blocks * BLK)


def column_sum(values):
    return jnp.sum(values, axis=0, keepdims=True)


def tile_steps():
    sub_index = lax.broadcasted_iota(jnp.int32, (SUB, BLK), 0)
    lane_index = lax.broadcasted_iota(jnp.int32, (SUB, BLK), 1)
    return (sub_index - lane_index) & (SUB - 1), lane_index


def tile_home():
    sub_index = lax.broadcasted_iota(jnp.int32, (SUB, BLK), 0)
    lane_index = lax.broadcasted_iota(jnp.int32, (SUB, BLK), 1)
    return (lane_index & (SUB - 1)) == sub_index


def skew(row):
    placed = jnp.where(tile_home(), spread(row), 0.0)
    placed = placed + pltpu.roll(placed, BLK - 1, 1)
    placed = placed + pltpu.roll(placed, BLK - 2, 1)
    return placed + pltpu.roll(placed, BLK - 4, 1)


def unskew(tile):
    tile = tile + pltpu.roll(tile, 1, 1)
    tile = tile + pltpu.roll(tile, 2, 1)
    tile = tile + pltpu.roll(tile, 4, 1)
    return column_sum(jnp.where(tile_home(), tile, 0.0))


def band_of(product):
    step_index, lane_index = tile_steps()
    tile_index = ((lane_index + step_index) & (BLK - 1)) // SUB
    band = product[:SUB]
    for part in range(1, BLK // SUB):
        band = jnp.where(tile_index == part, product[part * SUB : (part + 1) * SUB], band)
    return band


def project_into(rows, weight, weight_turned, proj_ref, projt_ref, index):
    proj_ref[index] = jnp.dot(rows, weight, preferred_element_type=WIDE).astype(LOW)
    turned = lax.dot_general(
        weight_turned, rows, (((1,), (1,)), ((), ())), preferred_element_type=WIDE
    ).astype(LOW)
    projt_ref[index] = turned
    return turned.astype(WIDE)


def own_kernel(
    local_pairs_ref,
    own_ref,
    weight_ref,
    consts_ref,
    cotangent_ref,
    projt_ref,
    score_ref,
    stats_ref,
    band_ref,
    bias_ref,
    proj_ref,
):
    block_count = own_ref.shape[0] // BLK
    local_count = local_pairs_ref.shape[1]
    weight = weight_ref[...]
    weight_turned = weight.astype(WIDE).T.astype(LOW)

    def one_table(block, grad_bias):
        nodes = at_block(block)
        turned = project_into(own_ref[nodes, :], weight, weight_turned, proj_ref, projt_ref, block)
        source = column_sum(turned * consts_ref[0])
        score_ref[block] = skew(source)
        upstream = cotangent_ref[:, nodes].astype(WIDE)
        stats_ref[block, 0:1, :] = source
        stats_ref[block, 1:2, :] = column_sum(turned * consts_ref[1])
        stats_ref[block, 2:3, :] = column_sum(upstream * turned)
        return grad_bias + upstream

    zero = jnp.zeros((weight.shape[1], BLK), WIDE)
    bias_ref[...] = lax.fori_loop(0, block_count, one_table, zero, unroll=8)

    def one_block(block, carry):
        upstream = cotangent_ref[:, at_block(block)]
        for pair in range(local_count):
            rows = proj_ref[local_pairs_ref[block, pair]]
            band_ref[block, pair] = band_of(jnp.dot(rows, upstream, preferred_element_type=WIDE))
        return carry

    lax.fori_loop(0, block_count, one_block, 0, unroll=2)


def layer_kernel(
    incoming_ref,
    local_pairs_ref,
    remote_pairs_ref,
    own_ref,
    halo_ref,
    weight_ref,
    consts_ref,
    cotangent_ref,
    local_counts_ref,
    remote_counts_ref,
    own_projt_ref,
    own_score_ref,
    stats_ref,
    band_ref,
    bias_ref,
    out_ref,
    shares_ref,
    halo_proj_ref,
    halo_projt_ref,
    halo_score_ref,
    own_grad_ref,
    halo_grad_ref,
    own_src_ref,
    halo_src_ref,
    own_rows_ref,
    mask_ref,
    weights_ref,
    share_ref,
):
    block_count = own_ref.shape[0] // BLK
    halo_count = halo_ref.shape[0] // BLK
    local_count = local_pairs_ref.shape[1]
    remote_count = remote_pairs_ref.shape[1]
    pair_count = local_count + remote_count
    head_width = weight_ref.shape[1]
    step_index, lane_index = tile_steps()
    row_all = lax.broadcasted_iota(jnp.int32, (BLK, BLK), 0)
    lane_all = lax.broadcasted_iota(jnp.int32, (BLK, BLK), 1)
    mask_ref[...] = jnp.where(((row_all - lane_all) & (BLK - 1)) < SUB, 1.0, 0.0).astype(LOW)
    weight = weight_ref[...]
    weight_turned = weight.astype(WIDE).T.astype(LOW)

    own_grad_ref[...] = jnp.zeros(own_grad_ref.shape, WIDE)
    halo_grad_ref[...] = jnp.zeros(halo_grad_ref.shape, WIDE)
    own_src_ref[...] = jnp.zeros(own_src_ref.shape, WIDE)
    halo_src_ref[...] = jnp.zeros(halo_src_ref.shape, WIDE)

    def halo_table(block, carry):
        rows = halo_ref[at_block(block), :]
        turned = project_into(
            rows, weight, weight_turned, halo_proj_ref, halo_projt_ref, block
        )
        source = column_sum(turned * consts_ref[0])
        slot = (block % PEER_BLOCKS) * BLK + lane_index[:1]
        live = slot < incoming_ref[block // PEER_BLOCKS]
        halo_score_ref[block] = skew(jnp.where(live, source, -jnp.inf))
        return carry

    lax.fori_loop(0, halo_count, halo_table, 0, unroll=16)

    def widen_band(tile, target_ref, turn, pair):
        doubled = jnp.concatenate([tile, tile], 0).astype(LOW)
        for part in range(BLK // (2 * SUB)):
            lead = pair * BLK + part * 2 * SUB
            target_ref[turn, lead : lead + 2 * SUB, :] = (
                doubled * mask_ref[part * 2 * SUB : (part + 1) * 2 * SUB, :]
            )

    def one_block(block, turn):
        nodes = at_block(block)
        upstream = cotangent_ref[:, nodes]
        upstream_wide = upstream.astype(WIDE)
        near = [local_pairs_ref[block, k] for k in range(local_count)]
        far = [remote_pairs_ref[block, k] for k in range(remote_count)]
        counts = [local_counts_ref[block, k : k + 1, :] for k in range(local_count)]
        counts += [remote_counts_ref[block, k : k + 1, :] for k in range(remote_count)]
        target_score = spread(stats_ref[block, 1:2, :])
        pre_self = target_score + spread(stats_ref[block, 0:1, :])
        logit_self = leaky(pre_self)
        pre = [target_score + own_score_ref[index] for index in near]
        pre += [target_score + halo_score_ref[index] for index in far]
        logits = [
            jnp.where(step_index < spread(count), leaky(value), -jnp.inf)
            for value, count in zip(pre, counts)
        ]
        top = logits[0]
        for logit in logits[1:]:
            top = jnp.maximum(top, logit)
        top = jnp.maximum(spread(jnp.max(top, axis=0, keepdims=True)), logit_self)
        raised = [jnp.exp(logit - top) for logit in logits]
        raised_self = jnp.exp(logit_self - top)
        denom = raised[0]
        for value in raised[1:]:
            denom = denom + value
        denom = spread(column_sum(denom)) + raised_self
        scale = 1.0 / denom
        share = [value * scale for value in raised]
        share_self = raised_self * scale
        for pair in range(pair_count):
            widen_band(raised[pair], weights_ref, turn, pair)
            widen_band(share[pair], share_ref, turn, pair)
        sources = [own_projt_ref[index] for index in near]
        sources = jnp.concatenate(sources + [halo_projt_ref[index] for index in far], 1)
        summed = jnp.dot(sources, weights_ref[turn], preferred_element_type=WIDE)
        self_wide = own_projt_ref[block].astype(WIDE)
        aggregate = (summed + raised_self[:1] * self_wide) * scale[:1]
        out_ref[:, nodes] = (aggregate + consts_ref[2]).astype(LOW)
        inner = spread(column_sum(upstream_wide * aggregate))
        grad_self = share_self * (spread(stats_ref[block, 2:3, :]) - inner) * slope_of(pre_self)
        total = None
        for pair in range(pair_count):
            if pair < local_count:
                grad_share = band_ref[block, pair]
            else:
                rows = halo_proj_ref[far[pair - local_count]]
                grad_share = band_of(jnp.dot(rows, upstream, preferred_element_type=WIDE))
            grad_pre = share[pair] * (grad_share - inner) * slope_of(pre[pair])
            if pair < local_count:
                own_src_ref[near[pair]] += grad_pre
            else:
                halo_src_ref[far[pair - local_count]] += grad_pre
            total = grad_pre if total is None else total + grad_pre
        own_rows_ref[block, 0:1, :] = grad_self[:1]
        own_rows_ref[block, 1:2, :] = column_sum(total) + grad_self[:1]
        grad_sources = lax.dot_general(
            upstream, share_ref[turn], (((1,), (1,)), ((), ())), preferred_element_type=WIDE
        )
        for pair in range(pair_count):
            if pair < local_count:
                own_grad_ref[near[pair]] += grad_sources[:, pair * BLK : (pair + 1) * BLK]
            else:
                index = far[pair - local_count]
                halo_grad_ref[index] += grad_sources[:, pair * BLK : (pair + 1) * BLK]
        own_grad_ref[block] += share_self[:1] * upstream_wide

    def one_turn(turn, carry):
        for part in range(SCRATCH_TURNS):
            one_block(turn * SCRATCH_TURNS + part, part)
        return carry

    lax.fori_loop(0, block_count // SCRATCH_TURNS, one_turn, 0)

    def finish(index, rows, own, carry):
        grad_weight, from_src, from_dst = carry
        parts = []
        for part in range(2):
            at = index * 2 + part
            if own:
                turned = own_projt_ref[at].astype(WIDE)
                source = unskew(own_src_ref[at]) + own_rows_ref[at, 0:1, :]
                target = own_rows_ref[at, 1:2, :]
                grad = own_grad_ref[at] + consts_ref[0] * source + consts_ref[1] * target
                from_dst = from_dst + turned * target
            else:
                turned = halo_projt_ref[at].astype(WIDE)
                source = unskew(halo_src_ref[at])
                grad = halo_grad_ref[at] + consts_ref[0] * source
            from_src = from_src + turned * source
            high = grad.astype(LOW)
            low = (grad - high.astype(WIDE)).astype(LOW)
            parts.append(jnp.concatenate([high, low], 0))
        grad_weight = grad_weight + jnp.dot(
            jnp.concatenate(parts, 1), rows, preferred_element_type=WIDE
        )
        return grad_weight, from_src, from_dst

    def finish_own(index, carry):
        return finish(index, own_ref[at_block(index, 2), :], True, carry)

    def finish_halo(index, carry):
        return finish(index, halo_ref[at_block(index, 2), :], False, carry)

    zero = jnp.zeros((head_width, BLK), WIDE)
    carry = (jnp.zeros((2 * head_width, own_ref.shape[1]), WIDE), zero, zero)
    carry = lax.fori_loop(0, block_count // 2, finish_own, carry, unroll=8)
    carry = lax.fori_loop(0, halo_count // 2, finish_halo, carry, unroll=8)
    grad_weight, from_src, from_dst = carry
    grad_weight = grad_weight[:head_width] + grad_weight[head_width:]
    lanes = lax.broadcasted_iota(jnp.int32, (head_width, BLK), 1)
    extra = jnp.zeros((head_width, BLK), WIDE)
    for place, value in enumerate((from_src, from_dst, bias_ref[...])):
        extra = jnp.where(lanes == place, jnp.sum(value, axis=1, keepdims=True), extra)
    extra = jnp.concatenate([extra, jnp.zeros((BLK - head_width, BLK), WIDE)], 0).T
    for copy in range(shares_ref.shape[0]):
        shares_ref[copy, :head_width, :] = grad_weight
        shares_ref[copy, head_width:, :] = extra[:SUB]


def relay_kernel(parts_ref, out_ref):
    total = parts_ref[0]
    for part in range(1, parts_ref.shape[0]):
        total = total + parts_ref[part]
    for copy in range(out_ref.shape[0]):
        out_ref[copy] = total


def last_kernel(parts_ref, weight_ref, attention_ref, bias_ref):
    total = parts_ref[0]
    for part in range(1, parts_ref.shape[0]):
        total = total + parts_ref[part]
    head_width = weight_ref.shape[1]
    weight_ref[...] = total[:head_width].T
    attention_ref[0] = total[head_width : head_width + 1, :head_width]
    attention_ref[1] = total[head_width + 1 : head_width + 2, :head_width]
    bias_ref[...] = total[head_width + 2 : head_width + 3, :head_width]


def vmem():
    return pl.BlockSpec(memory_space=pltpu.VMEM)


def smem():
    return pl.BlockSpec(memory_space=pltpu.SMEM)


def gather_rows(rows, live, features):
    slots = rows.shape[0]
    node_count, in_width = features.shape
    return pl.pallas_call(
        gather_kernel,
        out_shape=jax.ShapeDtypeStruct((slots, in_width), LOW),
        in_specs=[smem(), smem(), vmem()],
        out_specs=vmem(),
        scratch_shapes=[
            pltpu.VMEM((node_count, in_width), WIDE),
            pltpu.VMEM((slots, in_width), WIDE),
        ],
        compiler_params=pltpu.CompilerParams(vmem_limit_bytes=VMEM_LIMIT),
        name="gather_rows",
    )(rows, live, features)


def own_part(*operands):
    local_pairs, features, weight = operands[:3]
    head_width = weight.shape[1]
    block_count = features.shape[0] // BLK
    local_count = local_pairs.shape[1]
    tiles = jax.ShapeDtypeStruct((block_count, SUB, BLK), WIDE)
    return pl.pallas_call(
        own_kernel,
        out_shape=(
            jax.ShapeDtypeStruct((block_count, head_width, BLK), LOW),
            tiles,
            tiles,
            jax.ShapeDtypeStruct((block_count, local_count, SUB, BLK), WIDE),
            jax.ShapeDtypeStruct((head_width, BLK), WIDE),
        ),
        in_specs=[smem()] + [vmem()] * 4,
        out_specs=(vmem(),) * 5,
        scratch_shapes=[pltpu.VMEM((block_count, BLK, head_width), LOW)],
        compiler_params=pltpu.CompilerParams(vmem_limit_bytes=VMEM_LIMIT),
        cost_estimate=pl.CostEstimate(flops=10**10, bytes_accessed=8 * 10**6, transcendentals=0),
        name="own_part",
    )(*operands)


def attention_layer(*operands):
    local_pairs, remote_pairs, features, halo, weight = operands[1:6]
    node_count, in_width = features.shape
    head_width = weight.shape[1]
    block_count = node_count // BLK
    halo_count = halo.shape[0] // BLK
    pair_rows = (local_pairs.shape[1] + remote_pairs.shape[1]) * BLK
    return pl.pallas_call(
        layer_kernel,
        out_shape=(
            jax.ShapeDtypeStruct((head_width, node_count), LOW),
            jax.ShapeDtypeStruct((NEAR_GROUP, head_width + SUB, in_width), WIDE),
        ),
        in_specs=[smem(), smem(), smem()] + [vmem()] * 12,
        out_specs=(vmem(), vmem()),
        scratch_shapes=[
            pltpu.VMEM((halo_count, BLK, head_width), LOW),
            pltpu.VMEM((halo_count, head_width, BLK), LOW),
            pltpu.VMEM((halo_count, SUB, BLK), WIDE),
            pltpu.VMEM((block_count, head_width, BLK), WIDE),
            pltpu.VMEM((halo_count, head_width, BLK), WIDE),
            pltpu.VMEM((block_count, SUB, BLK), WIDE),
            pltpu.VMEM((halo_count, SUB, BLK), WIDE),
            pltpu.VMEM((block_count, SUB, BLK), WIDE),
            pltpu.VMEM((BLK, BLK), LOW),
            pltpu.VMEM((SCRATCH_TURNS, pair_rows, BLK), LOW),
            pltpu.VMEM((SCRATCH_TURNS, pair_rows, BLK), LOW),
        ],
        compiler_params=pltpu.CompilerParams(vmem_limit_bytes=VMEM_LIMIT),
        cost_estimate=pl.CostEstimate(flops=10**10, bytes_accessed=10**7, transcendentals=0),
        name="attention_layer",
    )(*operands)


def per_device(
    features,
    weight,
    attention,
    bias,
    cotangent,
    local_pairs,
    local_counts,
    remote_pairs,
    remote_counts,
    send_rows,
    send_counts,
):
    node_count, in_width = features.shape
    head_width = weight.shape[1]
    peer_count = lax.axis_size("dom")
    capacity = PEER_BLOCKS * BLK
    slots = peer_count * capacity
    me = lax.axis_index("dom")
    outgoing_live = lax.dynamic_index_in_dim(send_counts, me, 0, False)
    incoming_live = lax.dynamic_index_in_dim(send_counts, me, 1, False)
    outgoing = gather_rows(send_rows.reshape(-1), outgoing_live, features)
    halo = lax.all_to_all(
        outgoing.reshape(peer_count, capacity, in_width), "dom", 0, 0, tiled=True
    ).reshape(slots, in_width)
    consts = jnp.broadcast_to(
        jnp.concatenate([attention[:, 0], bias[None]], 0)[:, :, None], (3, head_width, BLK)
    )
    own = own_part(local_pairs, features, weight, consts, cotangent)
    output, shares = attention_layer(
        incoming_live,
        local_pairs,
        remote_pairs,
        features,
        halo,
        weight,
        consts,
        cotangent,
        local_counts,
        remote_counts,
        *own,
    )
    near = [
        [base + step for step in range(NEAR_GROUP)] for base in range(0, peer_count, NEAR_GROUP)
    ]
    far = [list(range(base, peer_count, NEAR_GROUP)) for base in range(NEAR_GROUP)]
    shares = exchange(shares, near)
    relayed = pl.pallas_call(
        relay_kernel,
        out_shape=jax.ShapeDtypeStruct((peer_count // NEAR_GROUP,) + shares.shape[1:], WIDE),
        in_specs=[vmem()],
        out_specs=vmem(),
        name="relay_sums",
    )(shares)
    grad_weight, grad_attention, grad_bias = pl.pallas_call(
        last_kernel,
        out_shape=(
            jax.ShapeDtypeStruct((in_width, head_width), WIDE),
            jax.ShapeDtypeStruct((2, 1, head_width), WIDE),
            jax.ShapeDtypeStruct((1, head_width), WIDE),
        ),
        in_specs=[vmem()],
        out_specs=(vmem(), vmem(), vmem()),
        name="last_sums",
    )(exchange(relayed, far))
    return output, grad_weight, grad_attention, grad_bias[0]


def exchange(values, groups):
    return lax.all_to_all(values, "dom", 0, 0, tiled=True, axis_index_groups=groups)


def solution(mesh):
    return jax.shard_map(
        per_device,
        mesh=mesh,
        in_specs=(
            P("dom", None),
            P(None, "feat"),
            P(None, "feat", None),
            P("feat"),
            P("feat", "dom"),
            P("dom", None),
            P("dom", None, None),
            P("dom", None),
            P("dom", None, None),
            P("dom", None, None),
            P(),
        ),
        out_specs=(P("feat", "dom"), P(None, "feat"), P(None, "feat", None), P("feat")),
        check_vma=False,
    )
```

time: 181 us -> 106 us (0.59)
  Pallas kernels: 112 us -> 51 us
  waiting for transfers between devices: 23.9 us -> 10.7 us
  local copies, waits for them, and re-layouts: 8.84 us -> 11.8 us
  blocking collectives: 23.4 us -> 20.8 us
    pallas_call x2 -> x5, Pallas kernels: 112 us -> 51 us  [the longest x1 25.3 us: attention_layer(): pl.pallas_call(layer_kernel, out_shape=(jax.ShapeDtypeStruct((head_width,...]
    all_to_all x1, waiting for transfers between devices: 23.9 us -> 10.7 us  [per_device(): lax.all_to_all(outgoing.reshape(peer_count, capacity, in_width), 'dom', 0...]
    unnamed x23 -> x39, local copies, waits for them, and re-layouts: 4.95 us -> 11.5 us
    all_to_all x2, blocking collectives: 23.4 us -> 20.8 us  [exchange(): lax.all_to_all(values, 'dom', 0, 0, tiled=True, axis_index_groups=groups)]
  transfers between devices with their start and end apart: 1 -> 1, of which waited for: 1 -> 1; matrix products, arithmetic and copies ran while one was open for 2% -> 1% of each run, Pallas kernels for 0% -> 13%
where the time goes in v2:
time: 106 us; the launch traced here: 104 us
  Pallas kernels  51 us (48%)
  blocking collectives  20.8 us (20%)
  local copies, waits for them, and re-layouts  11.8 us (11%)
  waiting for transfers between devices  10.7 us (10%)
  starting transfers between devices  9.4 us (9%)
    pallas_call x1, Pallas kernels, attention_layer(): pl.pallas_call(layer_kernel, out_shape=(jax.ShapeDtypeStruct((head_width,...  25.3 us
    all_to_all x2, blocking collectives, exchange(): lax.all_to_all(values, 'dom', 0, 0, tiled=True, axis_index_groups=groups)  20.8 us
    pallas_call x1, Pallas kernels, own_part(): pl.pallas_call(own_kernel, out_shape=(jax.ShapeDtypeStruct((block_count,...  13.5 us
    unnamed x39, local copies, waits for them, and re-layouts  11.5 us
    all_to_all x1, waiting for transfers between devices, per_device(): lax.all_to_all(outgoing.reshape(peer_count, capacity, in_width), 'dom', 0...  10.7 us
    all_to_all x1, starting transfers between devices, per_device(): lax.all_to_all(outgoing.reshape(peer_count, capacity, in_width), 'dom', 0...  9.4 us
    pallas_call x1, Pallas kernels, gather_rows(): pl.pallas_call(gather_kernel, out_shape=jax.ShapeDtypeStruct((slots, in_w...  8.88 us
  transfers between devices with their start and end apart: 1, of which 1 were waited for; matrix products, arithmetic and copies ran while one was open for 1% of the time, Pallas kernels for 13%

profile of v2, /device:TPU:1, one launch (start us, length us, event | category | flops | bytes accessed | tf_op | source)
XLA Modules:
  0.0 104.5 jit_solution(11003764750573089595)
XLA Ops:
  0.6 0.0 copy-start
  0.7 0.8 copy.31
  1.5 0.0 copy-start.1
  1.5 1.6 %copy-done.1 = bf16[8192,128]{1,0:T(8,128)(2,1)S(1)} copy-done((bf16[8192,128]{1,0:T(8,128)(2,1)S(1)}, bf16[8192,128]{1,0:T(8,128)(2,1)}, u32[]{:S(2)}) %copy-start.1) | copy-done | bytes 2097176
  3.1 8.9 %gather_rows.1 = bf16[8192,128]{1,0:T(8,128)(2,1)} custom-call(s32[8192]{0:T(1024)S(1)} %bitcast.9, s32[32]{0:T(128)S(1)} %dynamic-slice_bitcast_fusion.live_ref, bf16[8192,128]{1,0:T(8,128)(2,1)S(1)} %copy-done.1), custom_call_target="tpu_custom_call" | custom-call | tf_op jit(solution)/shard_map/gather_rows/pallas_call | solution.py:386
  11.9 0.0 copy-start.9
  12.0 0.0 copy-start.14
  12.0 0.0 copy-start.15
  12.0 0.0 copy-start.2
  12.0 9.4 %all-to-all-start = ((bf16[32,256,128]{2,1,0:T(8,128)(2,1)}), bf16[32,256,128]{2,1,0:T(8,128)(2,1)}, u32[]{:S(2)}, u32[]{:S(2)}) async-start(bf16[32,256,128]{2,1,0:T(8,128)(2,1)} %bitcast.1), calls=%async_computation | async-start | bytes 4194304 | tf_op jit(solution)/shard_map/all_to_all | solution.py:480
  21.4 0.1 copy.27.weight_ref
  21.5 0.1 copy.25.local_pairs_ref
  21.6 0.1 copy.26.remote_pairs_ref
  21.7 0.1 copy.29.remote_counts_ref
  21.8 0.1 copy.28.local_counts_ref
  21.9 0.2 dynamic-slice_reduce_fusion.incoming_ref
  22.2 0.1 broadcast_in_dim.10.consts_ref
  22.3 0.0 copy-start.3
  22.3 1.2 %copy-done.3 = bf16[64,8192]{1,0:T(8,128)(2,1)S(1)} copy-done((bf16[64,8192]{1,0:T(8,128)(2,1)S(1)}, bf16[64,8192]{1,0:T(8,128)(2,1)}, u32[]{:S(2)}) %copy-start.3) | copy-done | bytes 1048600
  23.5 13.5 %own_part.1 = (bf16[64,64,128]{2,1,0:T(8,128)(2,1)S(1)}, f32[64,8,128]{2,1,0:T(8,128)S(1)}, f32[64,8,128]{2,1,0:T(8,128)S(1)}, f32[64,5,8,128]{3,2,1,0:T(8,128)S(1)}, f32[64,128]{1,0:T(8,128)S(1)}) custom-call(s32[64,5]{1,0:T(8,128)S(1)} %copy.25.local_pairs_ref, bf16[8192,128]{1,0:T(8,128)(2,1)S(1)} %copy-done.2, bf16[128,64]{1,0:T(8,128)(2,1)S(1)} %copy.27.weight_ref, ...), custom_call_target="tpu_custom_call" | custom-call | flops 10000000000 | bytes 8000000 | tf_op jit(solution)/shard_map/own_part/pallas_call | solution.py:406
  37.0 1.1 %copy-done.5 = f32[64,5,8,128]{3,2,1,0:T(8,128)} copy-done((f32[64,5,8,128]{3,2,1,0:T(8,128)}, f32[64,5,8,128]{3,2,1,0:T(8,128)S(1)}, u32[]{:S(2)}) %copy-start.5) | copy-done | bytes 1310744
  38.1 1.0 copy-done.7
  39.1 10.7 %all-to-all-done = bf16[32,256,128]{2,1,0:T(8,128)(2,1)} async-done(((bf16[32,256,128]{2,1,0:T(8,128)(2,1)}), bf16[32,256,128]{2,1,0:T(8,128)(2,1)}, u32[]{:S(2)}, u32[]{:S(2)}) %all-to-all-start) | async-done | bytes 2097184 | tf_op jit(solution)/shard_map/all_to_all | solution.py:480
  49.8 1.2 %copy-done.4 = bf16[64,8192]{1,0:T(8,128)(2,1)S(1)} copy-done((bf16[64,8192]{1,0:T(8,128)(2,1)S(1)}, bf16[64,8192]{1,0:T(8,128)(2,1)}, u32[]{:S(2)}) %copy-start.4) | copy-done | bytes 1048600
  51.0 1.3 %copy-done.6 = f32[64,5,8,128]{3,2,1,0:T(8,128)S(1)} copy-done((f32[64,5,8,128]{3,2,1,0:T(8,128)S(1)}, f32[64,5,8,128]{3,2,1,0:T(8,128)}, u32[]{:S(2)}) %copy-start.6) | copy-done | bytes 1310744
  52.3 1.2 %copy-done.8 = bf16[64,64,128]{2,1,0:T(8,128)(2,1)S(1)} copy-done((bf16[64,64,128]{2,1,0:T(8,128)(2,1)S(1)}, bf16[64,64,128]{2,1,0:T(8,128)(2,1)}, u32[]{:S(2)}) %copy-start.8) | copy-done | bytes 1048600
  53.5 25.3 %attention_layer.1 = (bf16[64,8192]{1,0:T(8,128)(2,1)}, f32[4,72,128]{2,1,0:T(8,128)S(1)}) custom-call(s32[32]{0:T(128)S(1)} %dynamic-slice_reduce_fusion.incoming_ref, s32[64,5]{1,0:T(8,128)S(1)} %copy.25.local_pairs_ref, s32[64,3]{1,0:T(8,128)S(1)} %copy.26.remote_pairs_ref, bf16[8192,128]{1,0:T(8,128)(2,1)S(1)} %copy-done.2, ...), custom_call_target="tpu_custom_call" | custom-call | flops 10000000000 | bytes 10000000 | tf_op jit(solution)/shard_map/attention_layer/pallas_call | solution.py:431
  78.8 8.2 %all_to_all.15.parts_ref = f32[4,72,128]{2,1,0:T(8,128)} all-to-all(f32[4,72,128]{2,1,0:T(8,128)S(1)} %get-tuple-element.20), channel_id=1, replica_groups={{0,4,8,12},{16,20,24,28},{32,36,40,44},{48,52,56,60},{64,68,72,76},{80,..., dimensions={0} | all-to-all | bytes 294912 | tf_op jit(solution)/shard_map/all_to_all | solution.py:527
  87.0 1.6 %relay_sums.1 = f32[8,72,128]{2,1,0:T(8,128)} custom-call(f32[4,72,128]{2,1,0:T(8,128)} %all_to_all.15.parts_ref), custom_call_target="tpu_custom_call" | custom-call | tf_op jit(solution)/shard_map/relay_sums/pallas_call | solution.py:505
  88.7 12.5 %all_to_all.16.parts_ref = f32[8,72,128]{2,1,0:T(8,128)} all-to-all(f32[8,72,128]{2,1,0:T(8,128)} %relay_sums.1), channel_id=1, replica_groups={{0,16,32,48,64,80,96,112},{4,20,36,52,68,84,100,116},{8,24,40,56,72,88,..., dimensions={0} | all-to-all | bytes 589824 | tf_op jit(solution)/shard_map/all_to_all | solution.py:527
  101.2 1.7 %last_sums.1 = (f32[128,64]{1,0:T(8,128)}, f32[2,1,64]{2,1,0:T(1,128)}, f32[1,64]{1,0:T(1,128)}) custom-call(f32[8,72,128]{2,1,0:T(8,128)} %all_to_all.16.parts_ref), custom_call_target="tpu_custom_call" | custom-call | tf_op jit(solution)/shard_map/last_sums/pallas_call | solution.py:512
  102.9 1.5 %copy.30 = f32[128,64]{0,1:T(8,128)} copy(f32[128,64]{1,0:T(8,128)} %get-tuple-element.29) | data formatting | bytes 65536
  (20 shorter events, 0.1 us)
Async XLA Ops:
  0.6 0.8 copy-start
  1.5 1.6 %copy-start.1 = (bf16[8192,128]{1,0:T(8,128)(2,1)S(1)}, bf16[8192,128]{1,0:T(8,128)(2,1)}, u32[]{:S(2)}) copy-start(bf16[8192,128]{1,0:T(8,128)(2,1)} %own_ref.3) | copy-start | bytes 6291460
  11.9 9.5 %copy-start.11 = (bf16[128,64]{0,1:T(8,128)(2,1)S(1)}, bf16[128,64]{0,1:T(8,128)(2,1)}, u32[]{:S(2)}) copy-start(bf16[128,64]{0,1:T(8,128)(2,1)} %param.12) | copy-start | bytes 49156
  11.9 9.6 %copy-start.12 = (s32[64,5]{0,1:T(8,128)S(1)}, s32[64,5]{0,1:T(8,128)}, u32[]{:S(2)}) copy-start(s32[64,5]{0,1:T(8,128)} %param.16) | copy-start | bytes 3844
  11.9 9.7 %copy-start.13 = (s32[64,3]{0,1:T(4,128)S(1)}, s32[64,3]{0,1:T(4,128)}, u32[]{:S(2)}) copy-start(s32[64,3]{0,1:T(4,128)} %param.18) | copy-start | bytes 2308
  11.9 9.8 %copy-start.10 = (s32[64,3,128]{2,0,1:T(8,128)S(1)}, s32[64,3,128]{2,0,1:T(8,128)}, u32[]{:S(2)}) copy-start(s32[64,3,128]{2,0,1:T(8,128)} %param.19) | copy-start | bytes 294916
  11.9 9.9 %copy-start.9 = (s32[64,5,128]{2,0,1:T(8,128)S(1)}, s32[64,5,128]{2,0,1:T(8,128)}, u32[]{:S(2)}) copy-start(s32[64,5,128]{2,0,1:T(8,128)} %param.17) | copy-start | bytes 491524
  12.0 10.2 %copy-start.14 = (f32[2,1,64]{2,1,0:T(1,128)S(1)}, f32[2,1,64]{2,1,0:T(1,128)}, u32[]{:S(2)}) copy-start(f32[2,1,64]{2,1,0:T(1,128)} %param.13) | copy-start | bytes 1540
  12.0 10.2 %copy-start.15 = (f32[64]{0:T(128)S(1)}, f32[64]{0:T(128)}, u32[]{:S(2)}) copy-start(f32[64]{0:T(128)} %param.14) | copy-start | bytes 772
  12.0 10.3 %copy-start.2 = (bf16[8192,128]{1,0:T(8,128)(2,1)S(1)}, bf16[8192,128]{1,0:T(8,128)(2,1)}, u32[]{:S(2)}) copy-start(bf16[8192,128]{1,0:T(8,128)(2,1)} %own_ref.3) | copy-start | bytes 6291460
  12.0 37.8 %all-to-all-start = ((bf16[32,256,128]{2,1,0:T(8,128)(2,1)}), bf16[32,256,128]{2,1,0:T(8,128)(2,1)}, u32[]{:S(2)}, u32[]{:S(2)}) async-start(bf16[32,256,128]{2,1,0:T(8,128)(2,1)} %bitcast.1), calls=%async_computation | async-start | bytes 4194304 | tf_op jit(solution)/shard_map/all_to_all | solution.py:480
  22.3 1.2 %copy-start.3 = (bf16[64,8192]{1,0:T(8,128)(2,1)S(1)}, bf16[64,8192]{1,0:T(8,128)(2,1)}, u32[]{:S(2)}) copy-start(bf16[64,8192]{1,0:T(8,128)(2,1)} %cotangent_ref.3) | copy-start | bytes 3145732
  37.0 1.1 %copy-start.5 = (f32[64,5,8,128]{3,2,1,0:T(8,128)}, f32[64,5,8,128]{3,2,1,0:T(8,128)S(1)}, u32[]{:S(2)}) copy-start(f32[64,5,8,128]{3,2,1,0:T(8,128)S(1)} %get-tuple-element.17.band_ref) | copy-start | bytes 3932164
  38.1 1.0 copy-start.7
  49.8 1.2 %copy-start.4 = (bf16[64,8192]{1,0:T(8,128)(2,1)S(1)}, bf16[64,8192]{1,0:T(8,128)(2,1)}, u32[]{:S(2)}) copy-start(bf16[64,8192]{1,0:T(8,128)(2,1)} %cotangent_ref.3) | copy-start | bytes 3145732
  51.0 1.3 %copy-start.6 = (f32[64,5,8,128]{3,2,1,0:T(8,128)S(1)}, f32[64,5,8,128]{3,2,1,0:T(8,128)}, u32[]{:S(2)}) copy-start(f32[64,5,8,128]{3,2,1,0:T(8,128)} %copy-done.5) | copy-start | bytes 3932164
  52.3 1.2 %copy-start.8 = (bf16[64,64,128]{2,1,0:T(8,128)(2,1)S(1)}, bf16[64,64,128]{2,1,0:T(8,128)(2,1)}, u32[]{:S(2)}) copy-start(bf16[64,64,128]{2,1,0:T(8,128)(2,1)} %copy-done.7) | copy-start | bytes 3145732

commit v3 on v2

--- a/solution.py
+++ b/solution.py
@@ -11,8 +11,11 @@
 LOW = jnp.bfloat16
 WIDE = jnp.float32
 VMEM_LIMIT = 32 * 1024 * 1024
-SCRATCH_TURNS = 4
-NEAR_GROUP = 4
+OWN_LIMIT = 56 * 1024 * 1024
+LAYER_LIMIT = 58 * 1024 * 1024
+TURN_BLOCKS = 8
+WEIGHT_GROUP = 8
+SHARE_GROUP = 2
 GATHER_STEP = 32
 
 
@@ -168,19 +171,19 @@
     incoming_ref,
     local_pairs_ref,
     remote_pairs_ref,
-    own_ref,
-    halo_ref,
     weight_ref,
     consts_ref,
-    cotangent_ref,
-    local_counts_ref,
-    remote_counts_ref,
-    own_projt_ref,
-    own_score_ref,
-    stats_ref,
-    band_ref,
     bias_ref,
-    out_ref,
+    halo_hbm,
+    own_projt_hbm,
+    own_score_hbm,
+    stats_hbm,
+    cotangent_hbm,
+    local_counts_hbm,
+    remote_counts_hbm,
+    band_hbm,
+    own_hbm,
+    out_hbm,
     shares_ref,
     halo_proj_ref,
     halo_projt_ref,
@@ -191,9 +194,35 @@
     halo_src_ref,
     own_rows_ref,
     mask_ref,
-    weights_ref,
-    share_ref,
+    halo_ref,
+    own_projt_ref,
+    own_score_ref,
+    stats_ref,
+    cotangent_ref,
+    local_counts_ref,
+    remote_counts_ref,
+    band_ref,
+    own_ref,
+    out_ref,
+    copy_sem,
 ):
+    fetches = []
+    for place, (source, target) in enumerate(
+        (
+            (halo_hbm, halo_ref),
+            (own_projt_hbm, own_projt_ref),
+            (own_score_hbm, own_score_ref),
+            (stats_hbm, stats_ref),
+            (cotangent_hbm, cotangent_ref),
+            (local_counts_hbm, local_counts_ref),
+            (remote_counts_hbm, remote_counts_ref),
+            (band_hbm, band_ref),
+            (own_hbm, own_ref),
+        )
+    ):
+        fetches.append(pltpu.make_async_copy(source, target, copy_sem.at[place]))
+    for fetch in fetches:
+        fetch.start()
     block_count = own_ref.shape[0] // BLK
     halo_count = halo_ref.shape[0] // BLK
     local_count = local_pairs_ref.shape[1]
@@ -212,6 +241,8 @@
     own_src_ref[...] = jnp.zeros(own_src_ref.shape, WIDE)
     halo_src_ref[...] = jnp.zeros(halo_src_ref.shape, WIDE)
 
+    fetches[0].wait()
+
     def halo_table(block, carry):
         rows = halo_ref[at_block(block), :]
         turned = project_into(
@@ -225,15 +256,15 @@
 
     lax.fori_loop(0, halo_count, halo_table, 0, unroll=16)
 
-    def widen_band(tile, target_ref, turn, pair):
-        doubled = jnp.concatenate([tile, tile], 0).astype(LOW)
-        for part in range(BLK // (2 * SUB)):
-            lead = pair * BLK + part * 2 * SUB
-            target_ref[turn, lead : lead + 2 * SUB, :] = (
-                doubled * mask_ref[part * 2 * SUB : (part + 1) * 2 * SUB, :]
-            )
-
-    def one_block(block, turn):
+    def band_values(tiles):
+        parts = []
+        for tile in tiles:
+            doubled = jnp.concatenate([tile, tile], 0).astype(LOW)
+            for lead in range(0, BLK, 2 * SUB):
+                parts.append(doubled * mask_ref[lead : lead + 2 * SUB, :])
+        return jnp.concatenate(parts, 0)
+
+    def one_block(block):
         nodes = at_block(block)
         upstream = cotangent_ref[:, nodes]
         upstream_wide = upstream.astype(WIDE)
@@ -263,12 +294,17 @@
         scale = 1.0 / denom
         share = [value * scale for value in raised]
         share_self = raised_self * scale
-        for pair in range(pair_count):
-            widen_band(raised[pair], weights_ref, turn, pair)
-            widen_band(share[pair], share_ref, turn, pair)
         sources = [own_projt_ref[index] for index in near]
-        sources = jnp.concatenate(sources + [halo_projt_ref[index] for index in far], 1)
-        summed = jnp.dot(sources, weights_ref[turn], preferred_element_type=WIDE)
+        sources += [halo_projt_ref[index] for index in far]
+        summed = None
+        for lead in range(0, pair_count, WEIGHT_GROUP):
+            group = slice(lead, lead + WEIGHT_GROUP)
+            part = jnp.dot(
+                jnp.concatenate(sources[group], 1),
+                band_values(raised[group]),
+                preferred_element_type=WIDE,
+            )
+            summed = part if summed is None else summed + part
         self_wide = own_projt_ref[block].astype(WIDE)
         aggregate = (summed + raised_self[:1] * self_wide) * scale[:1]
         out_ref[:, nodes] = (aggregate + consts_ref[2]).astype(LOW)
@@ -289,23 +325,32 @@
             total = grad_pre if total is None else total + grad_pre
         own_rows_ref[block, 0:1, :] = grad_self[:1]
         own_rows_ref[block, 1:2, :] = column_sum(total) + grad_self[:1]
-        grad_sources = lax.dot_general(
-            upstream, share_ref[turn], (((1,), (1,)), ((), ())), preferred_element_type=WIDE
-        )
-        for pair in range(pair_count):
-            if pair < local_count:
-                own_grad_ref[near[pair]] += grad_sources[:, pair * BLK : (pair + 1) * BLK]
-            else:
-                index = far[pair - local_count]
-                halo_grad_ref[index] += grad_sources[:, pair * BLK : (pair + 1) * BLK]
+        for lead in range(0, pair_count, SHARE_GROUP):
+            grad_sources = lax.dot_general(
+                upstream,
+                band_values(share[lead : lead + SHARE_GROUP]),
+                (((1,), (1,)), ((), ())),
+                preferred_element_type=WIDE,
+            )
+            for pair in range(lead, min(lead + SHARE_GROUP, pair_count)):
+                grad = grad_sources[:, (pair - lead) * BLK : (pair - lead + 1) * BLK]
+                if pair < local_count:
+                    own_grad_ref[near[pair]] += grad
+                else:
+                    halo_grad_ref[far[pair - local_count]] += grad
         own_grad_ref[block] += share_self[:1] * upstream_wide
 
     def one_turn(turn, carry):
-        for part in range(SCRATCH_TURNS):
-            one_block(turn * SCRATCH_TURNS + part, part)
+        for part in range(TURN_BLOCKS):
+            one_block(turn * TURN_BLOCKS + part)
         return carry
 
-    lax.fori_loop(0, block_count // SCRATCH_TURNS, one_turn, 0)
+    for fetch in fetches[1:-1]:
+        fetch.wait()
+    lax.fori_loop(0, block_count // TURN_BLOCKS, one_turn, 0)
+    store = pltpu.make_async_copy(out_ref, out_hbm, copy_sem.at[len(fetches)])
+    store.start()
+    fetches[-1].wait()
 
     def finish(index, rows, own, carry):
         grad_weight, from_src, from_dst = carry
@@ -351,22 +396,15 @@
     for copy in range(shares_ref.shape[0]):
         shares_ref[copy, :head_width, :] = grad_weight
         shares_ref[copy, head_width:, :] = extra[:SUB]
-
-
-def relay_kernel(parts_ref, out_ref):
-    total = parts_ref[0]
-    for part in range(1, parts_ref.shape[0]):
-        total = total + parts_ref[part]
-    for copy in range(out_ref.shape[0]):
-        out_ref[copy] = total
+    store.wait()
 
 
 def last_kernel(parts_ref, weight_ref, attention_ref, bias_ref):
     total = parts_ref[0]
     for part in range(1, parts_ref.shape[0]):
         total = total + parts_ref[part]
-    head_width = weight_ref.shape[1]
-    weight_ref[...] = total[:head_width].T
+    head_width = weight_ref.shape[0]
+    weight_ref[...] = total[:head_width]
     attention_ref[0] = total[head_width : head_width + 1, :head_width]
     attention_ref[1] = total[head_width + 1 : head_width + 2, :head_width]
     bias_ref[...] = total[head_width + 2 : head_width + 3, :head_width]
@@ -374,6 +412,10 @@
 
 def vmem():
     return pl.BlockSpec(memory_space=pltpu.VMEM)
+
+
+def anywhere():
+    return pl.BlockSpec(memory_space=pl.ANY)
 
 
 def smem():
@@ -415,27 +457,29 @@
         in_specs=[smem()] + [vmem()] * 4,
         out_specs=(vmem(),) * 5,
         scratch_shapes=[pltpu.VMEM((block_count, BLK, head_width), LOW)],
-        compiler_params=pltpu.CompilerParams(vmem_limit_bytes=VMEM_LIMIT),
+        compiler_params=pltpu.CompilerParams(vmem_limit_bytes=OWN_LIMIT),
         cost_estimate=pl.CostEstimate(flops=10**10, bytes_accessed=8 * 10**6, transcendentals=0),
         name="own_part",
     )(*operands)
 
 
 def attention_layer(*operands):
-    local_pairs, remote_pairs, features, halo, weight = operands[1:6]
-    node_count, in_width = features.shape
-    head_width = weight.shape[1]
+    incoming, local_pairs, remote_pairs, weight = operands[:4]
+    streamed = operands[6:]
+    halo, cotangent = streamed[0], streamed[4]
+    peer_count = incoming.shape[0]
+    in_width = halo.shape[1]
+    head_width, node_count = cotangent.shape
     block_count = node_count // BLK
     halo_count = halo.shape[0] // BLK
-    pair_rows = (local_pairs.shape[1] + remote_pairs.shape[1]) * BLK
     return pl.pallas_call(
         layer_kernel,
         out_shape=(
             jax.ShapeDtypeStruct((head_width, node_count), LOW),
-            jax.ShapeDtypeStruct((NEAR_GROUP, head_width + SUB, in_width), WIDE),
+            jax.ShapeDtypeStruct((peer_count, head_width + SUB, in_width), WIDE),
         ),
-        in_specs=[smem(), smem(), smem()] + [vmem()] * 12,
-        out_specs=(vmem(), vmem()),
+        in_specs=[smem()] * 3 + [vmem()] * 3 + [anywhere()] * len(streamed),
+        out_specs=(anywhere(), vmem()),
         scratch_shapes=[
             pltpu.VMEM((halo_count, BLK, head_width), LOW),
             pltpu.VMEM((halo_count, head_width, BLK), LOW),
@@ -446,10 +490,13 @@
             pltpu.VMEM((halo_count, SUB, BLK), WIDE),
             pltpu.VMEM((block_count, SUB, BLK), WIDE),
             pltpu.VMEM((BLK, BLK), LOW),
-            pltpu.VMEM((SCRATCH_TURNS, pair_rows, BLK), LOW),
-            pltpu.VMEM((SCRATCH_TURNS, pair_rows, BLK), LOW),
+        ]
+        + [pltpu.VMEM(value.shape, value.dtype) for value in streamed]
+        + [
+            pltpu.VMEM((head_width, node_count), LOW),
+            pltpu.SemaphoreType.DMA((len(streamed) + 1,)),
         ],
-        compiler_params=pltpu.CompilerParams(vmem_limit_bytes=VMEM_LIMIT),
+        compiler_params=pltpu.CompilerParams(vmem_limit_bytes=LAYER_LIMIT),
         cost_estimate=pl.CostEstimate(flops=10**10, bytes_accessed=10**7, transcendentals=0),
         name="attention_layer",
     )(*operands)
@@ -483,48 +530,39 @@
     consts = jnp.broadcast_to(
         jnp.concatenate([attention[:, 0], bias[None]], 0)[:, :, None], (3, head_width, BLK)
     )
-    own = own_part(local_pairs, features, weight, consts, cotangent)
+    projt, score, stats, band, grad_bias = own_part(
+        local_pairs, features, weight, consts, cotangent
+    )
     output, shares = attention_layer(
         incoming_live,
         local_pairs,
         remote_pairs,
-        features,
-        halo,
         weight,
         consts,
+        grad_bias,
+        halo,
+        projt,
+        score,
+        stats,
         cotangent,
         local_counts,
         remote_counts,
-        *own,
+        band,
+        features,
     )
-    near = [
-        [base + step for step in range(NEAR_GROUP)] for base in range(0, peer_count, NEAR_GROUP)
-    ]
-    far = [list(range(base, peer_count, NEAR_GROUP)) for base in range(NEAR_GROUP)]
-    shares = exchange(shares, near)
-    relayed = pl.pallas_call(
-        relay_kernel,
-        out_shape=jax.ShapeDtypeStruct((peer_count // NEAR_GROUP,) + shares.shape[1:], WIDE),
-        in_specs=[vmem()],
-        out_specs=vmem(),
-        name="relay_sums",
-    )(shares)
+    gathered = lax.all_to_all(shares, "dom", 0, 0, tiled=True)
     grad_weight, grad_attention, grad_bias = pl.pallas_call(
         last_kernel,
         out_shape=(
-            jax.ShapeDtypeStruct((in_width, head_width), WIDE),
+            jax.ShapeDtypeStruct((head_width, in_width), WIDE),
             jax.ShapeDtypeStruct((2, 1, head_width), WIDE),
             jax.ShapeDtypeStruct((1, head_width), WIDE),
         ),
         in_specs=[vmem()],
         out_specs=(vmem(), vmem(), vmem()),
         name="last_sums",
-    )(exchange(relayed, far))
-    return output, grad_weight, grad_attention, grad_bias[0]
-
-
-def exchange(values, groups):
-    return lax.all_to_all(values, "dom", 0, 0, tiled=True, axis_index_groups=groups)
+    )(gathered)
+    return output, grad_weight.T, grad_attention, grad_bias[0]
 
 
 def solution(mesh):

time: 106 us -> 102 us (0.962); the launches traced: 104 us -> 102 us
  blocking collectives: 20.8 us -> 24.2 us
  waiting for transfers between devices: 10.7 us -> 7.33 us
  local copies, waits for them, and re-layouts: 11.8 us -> 8.85 us
  starting transfers between devices: 9.4 us -> 10.7 us
  Pallas kernels: 51 us -> 49.9 us
    unnamed x39 -> x26, local copies, waits for them, and re-layouts: 11.5 us -> 7.42 us
    all_to_all x2 -> x1, blocking collectives: 20.8 us -> 24.2 us  [per_device(): gathered = lax.all_to_all(shares, 'dom', 0, 0, tiled=True)]
    all_to_all x1, waiting for transfers between devices: 10.7 us -> 7.33 us  [per_device(): lax.all_to_all(outgoing.reshape(peer_count, capacity, in_width), 'dom', 0...]
    pallas_call x1, Pallas kernels: 13.5 us -> 15.8 us  [own_part(): pl.pallas_call(own_kernel, out_shape=(jax.ShapeDtypeStruct((block_count,...]
    pallas_call x2 -> x1, Pallas kernels: 3.35 us -> 1.96 us  [per_device(): pl.pallas_call(last_kernel, out_shape=(jax.ShapeDtypeStruct((head_width,...]
    all_to_all x1, starting transfers between devices: 9.4 us -> 10.7 us  [per_device(): lax.all_to_all(outgoing.reshape(peer_count, capacity, in_width), 'dom', 0...]
    pallas_call x1, Pallas kernels: 25.3 us -> 24 us  [attention_layer(): pl.pallas_call(layer_kernel, out_shape=(jax.ShapeDtypeStruct((head_width,...]
  transfers between devices with their start and end apart: 1 -> 1, of which waited for: 1 -> 1; matrix products, arithmetic and copies ran while one was open for 1% -> 5% of each run, Pallas kernels for 13% -> 16%
where the time goes in v3:
time: 102 us
  Pallas kernels  49.9 us (49%)
  blocking collectives  24.2 us (24%)
  starting transfers between devices  10.7 us (10%)
  local copies, waits for them, and re-layouts  8.85 us (9%)
  waiting for transfers between devices  7.33 us (7%)
    all_to_all x1, blocking collectives, per_device(): gathered = lax.all_to_all(shares, 'dom', 0, 0, tiled=True)  24.2 us
    pallas_call x1, Pallas kernels, attention_layer(): pl.pallas_call(layer_kernel, out_shape=(jax.ShapeDtypeStruct((head_width,...  24 us
    pallas_call x1, Pallas kernels, own_part(): pl.pallas_call(own_kernel, out_shape=(jax.ShapeDtypeStruct((block_count,...  15.8 us
    all_to_all x1, starting transfers between devices, per_device(): lax.all_to_all(outgoing.reshape(peer_count, capacity, in_width), 'dom', 0...  10.7 us
    pallas_call x1, Pallas kernels, gather_rows(): pl.pallas_call(gather_kernel, out_shape=jax.ShapeDtypeStruct((slots, in_w...  8.2 us
    unnamed x26, local copies, waits for them, and re-layouts  7.42 us
    all_to_all x1, waiting for transfers between devices, per_device(): lax.all_to_all(outgoing.reshape(peer_count, capacity, in_width), 'dom', 0...  7.33 us
  transfers between devices with their start and end apart: 1, of which 1 were waited for; matrix products, arithmetic and copies ran while one was open for 5% of the time, Pallas kernels for 16%

profile of v3, /device:TPU:1, one launch (start us, length us, event | category | flops | bytes accessed | tf_op | source)
XLA Modules:
  0.0 101.8 jit_solution(13671937772473322685)
XLA Ops:
  0.6 0.0 copy-start
  0.7 0.8 copy.29
  1.4 0.0 copy-done
  1.5 0.0 copy-start.1
  1.5 1.6 %copy-done.1 = bf16[8192,128]{1,0:T(8,128)(2,1)S(1)} copy-done((bf16[8192,128]{1,0:T(8,128)(2,1)S(1)}, bf16[8192,128]{1,0:T(8,128)(2,1)}, u32[]{:S(2)}) %copy-start.1) | copy-done | bytes 2097176
  3.1 8.2 %gather_rows.1 = bf16[8192,128]{1,0:T(8,128)(2,1)} custom-call(s32[8192]{0:T(1024)S(1)} %bitcast.10, s32[32]{0:T(128)S(1)} %dynamic-slice_bitcast_fusion.live_ref, bf16[8192,128]{1,0:T(8,128)(2,1)S(1)} %copy-done.1), custom_call_target="tpu_custom_call" | custom-call | tf_op jit(solution)/shard_map/gather_rows/pallas_call | solution.py:428
  11.3 0.0 copy-start.5
  11.3 0.0 copy-start.6
  11.3 0.0 copy-start.3
  11.3 0.0 copy-start.8
  11.3 0.0 copy-start.9
  11.3 10.7 %all-to-all-start = ((bf16[32,256,128]{2,1,0:T(8,128)(2,1)}), bf16[32,256,128]{2,1,0:T(8,128)(2,1)S(1)}, u32[]{:S(2)}, u32[]{:S(2)}) async-start(bf16[32,256,128]{2,1,0:T(8,128)(2,1)} %bitcast.3), calls=%async_computation | async-start | bytes 4194304 | tf_op jit(solution)/shard_map/all_to_all | solution.py:527
  22.1 0.0 copy-done.5
  22.1 0.7 copy.26.weight_ref
  22.8 0.0 copy-done.6
  22.8 0.7 copy.24.local_pairs_ref
  23.5 0.0 copy-done.7
  23.5 0.7 copy.25.remote_pairs_ref
  24.2 0.0 copy-done.4
  24.2 0.7 copy.28.remote_counts_hbm
  25.0 0.0 copy-done.3
  25.0 0.8 copy.27.local_counts_hbm
  25.8 0.7 dynamic-slice_reduce_fusion.incoming_ref
  26.5 0.0 copy-done.8
  26.5 0.0 copy-done.9
  26.5 0.7 broadcast_in_dim.10.consts_ref
  27.2 15.8 %own_part.1 = (bf16[64,64,128]{2,1,0:T(8,128)(2,1)}, f32[64,8,128]{2,1,0:T(8,128)}, f32[64,8,128]{2,1,0:T(8,128)}, f32[64,5,8,128]{3,2,1,0:T(8,128)}, f32[64,128]{1,0:T(8,128)}) custom-call(s32[64,5]{1,0:T(8,128)} %copy.24.local_pairs_ref, bf16[8192,128]{1,0:T(8,128)(2,1)} %own_hbm.1, bf16[128,64]{1,0:T(8,128)(2,1)} %copy.26.weight_ref, ...), custom_call_target="tpu_custom_call" | custom-call | flops 10000000000 | bytes 8000000 | tf_op jit(solution)/shard_map/own_part/pallas_call | solution.py:448
  43.0 7.3 %all-to-all-done = bf16[32,256,128]{2,1,0:T(8,128)(2,1)S(1)} async-done(((bf16[32,256,128]{2,1,0:T(8,128)(2,1)}), bf16[32,256,128]{2,1,0:T(8,128)(2,1)S(1)}, u32[]{:S(2)}, u32[]{:S(2)}) %all-to-all-start) | async-done | bytes 2097184 | tf_op jit(solution)/shard_map/all_to_all | solution.py:527
  50.4 1.3 %copy-done.2 = bf16[32,256,128]{2,1,0:T(8,128)(2,1)} copy-done((bf16[32,256,128]{2,1,0:T(8,128)(2,1)}, bf16[32,256,128]{2,1,0:T(8,128)(2,1)S(1)}, u32[]{:S(2)}) %copy-start.2) | copy-done | bytes 2097176
  51.7 24.0 %attention_layer.1 = (bf16[64,8192]{1,0:T(8,128)(2,1)}, f32[32,72,128]{2,1,0:T(8,128)}) custom-call(s32[32]{0:T(128)} %dynamic-slice_reduce_fusion.incoming_ref, s32[64,5]{1,0:T(8,128)} %copy.24.local_pairs_ref, s32[64,3]{1,0:T(8,128)} %copy.25.remote_pairs_ref, bf16[128,64]{1,0:T(8,128)(2,1)} %copy.26.weight_ref, ...), custom_call_target="tpu_custom_call" | custom-call | flops 10000000000 | bytes 10000000 | tf_op jit(solution)/shard_map/attention_layer/pallas_call | solution.py:475
  75.7 24.2 %all_to_all.10.parts_ref = f32[32,72,128]{2,1,0:T(8,128)} all-to-all(f32[32,72,128]{2,1,0:T(8,128)} %get-tuple-element.20), channel_id=1, replica_groups=mesh['dom'=32,'feat'=4] {'dom'}, dimensions={0} | all-to-all | bytes 2359296 | tf_op jit(solution)/shard_map/all_to_all | solution.py:553
  99.9 2.0 %last_sums.1 = (f32[64,128]{1,0:T(8,128)}, f32[2,1,64]{2,1,0:T(1,128)}, f32[1,64]{1,0:T(1,128)}) custom-call(f32[32,72,128]{2,1,0:T(8,128)} %all_to_all.10.parts_ref), custom_call_target="tpu_custom_call" | custom-call | tf_op jit(solution)/shard_map/last_sums/pallas_call | solution.py:554
  (5 shorter events, 0.0 us)
Async XLA Ops:
  0.6 0.8 copy-start
  1.5 1.6 %copy-start.1 = (bf16[8192,128]{1,0:T(8,128)(2,1)S(1)}, bf16[8192,128]{1,0:T(8,128)(2,1)}, u32[]{:S(2)}) copy-start(bf16[8192,128]{1,0:T(8,128)(2,1)} %own_hbm.1) | copy-start | bytes 6291460
  11.3 10.8 %copy-start.5 = (bf16[128,64]{0,1:T(8,128)(2,1)S(1)}, bf16[128,64]{0,1:T(8,128)(2,1)}, u32[]{:S(2)}) copy-start(bf16[128,64]{0,1:T(8,128)(2,1)} %param.12) | copy-start | bytes 49156
  11.3 11.5 %copy-start.6 = (s32[64,5]{0,1:T(8,128)S(1)}, s32[64,5]{0,1:T(8,128)}, u32[]{:S(2)}) copy-start(s32[64,5]{0,1:T(8,128)} %param.16) | copy-start | bytes 3844
  11.3 12.2 %copy-start.7 = (s32[64,3]{0,1:T(4,128)S(1)}, s32[64,3]{0,1:T(4,128)}, u32[]{:S(2)}) copy-start(s32[64,3]{0,1:T(4,128)} %param.18) | copy-start | bytes 2308
  11.3 13.0 %copy-start.4 = (s32[64,3,128]{2,0,1:T(8,128)S(1)}, s32[64,3,128]{2,0,1:T(8,128)}, u32[]{:S(2)}) copy-start(s32[64,3,128]{2,0,1:T(8,128)} %param.19) | copy-start | bytes 294916
  11.3 13.7 %copy-start.3 = (s32[64,5,128]{2,0,1:T(8,128)S(1)}, s32[64,5,128]{2,0,1:T(8,128)}, u32[]{:S(2)}) copy-start(s32[64,5,128]{2,0,1:T(8,128)} %param.17) | copy-start | bytes 491524
  11.3 15.2 %copy-start.8 = (f32[2,1,64]{2,1,0:T(1,128)S(1)}, f32[2,1,64]{2,1,0:T(1,128)}, u32[]{:S(2)}) copy-start(f32[2,1,64]{2,1,0:T(1,128)} %param.13) | copy-start | bytes 1540
  11.3 15.2 %copy-start.9 = (f32[64]{0:T(128)S(1)}, f32[64]{0:T(128)}, u32[]{:S(2)}) copy-start(f32[64]{0:T(128)} %param.14) | copy-start | bytes 772
  11.3 39.0 %all-to-all-start = ((bf16[32,256,128]{2,1,0:T(8,128)(2,1)}), bf16[32,256,128]{2,1,0:T(8,128)(2,1)S(1)}, u32[]{:S(2)}, u32[]{:S(2)}) async-start(bf16[32,256,128]{2,1,0:T(8,128)(2,1)} %bitcast.3), calls=%async_computation | async-start | bytes 4194304 | tf_op jit(solution)/shard_map/all_to_all | solution.py:527
  50.4 1.3 %copy-start.2 = (bf16[32,256,128]{2,1,0:T(8,128)(2,1)}, bf16[32,256,128]{2,1,0:T(8,128)(2,1)S(1)}, u32[]{:S(2)}) copy-start(bf16[32,256,128]{2,1,0:T(8,128)(2,1)S(1)} %all-to-all-done) | copy-start | bytes 6291460

commit v4 on v3

--- a/solution.py
+++ b/solution.py
@@ -11,8 +11,9 @@
 LOW = jnp.bfloat16
 WIDE = jnp.float32
 VMEM_LIMIT = 32 * 1024 * 1024
-OWN_LIMIT = 56 * 1024 * 1024
-LAYER_LIMIT = 58 * 1024 * 1024
+OWN_LIMIT = 62 * 1024 * 1024
+SMALL_LIMIT = 4 * 1024 * 1024
+LAYER_LIMIT = 60 * 1024 * 1024
 TURN_BLOCKS = 8
 WEIGHT_GROUP = 8
 SHARE_GROUP = 2
@@ -307,7 +308,7 @@
             summed = part if summed is None else summed + part
         self_wide = own_projt_ref[block].astype(WIDE)
         aggregate = (summed + raised_self[:1] * self_wide) * scale[:1]
-        out_ref[:, nodes] = (aggregate + consts_ref[2]).astype(LOW)
+        out_ref[block] = (aggregate + consts_ref[2]).astype(LOW)
         inner = spread(column_sum(upstream_wide * aggregate))
         grad_self = share_self * (spread(stats_ref[block, 2:3, :]) - inner) * slope_of(pre_self)
         total = None
@@ -392,22 +393,42 @@
     extra = jnp.zeros((head_width, BLK), WIDE)
     for place, value in enumerate((from_src, from_dst, bias_ref[...])):
         extra = jnp.where(lanes == place, jnp.sum(value, axis=1, keepdims=True), extra)
-    extra = jnp.concatenate([extra, jnp.zeros((BLK - head_width, BLK), WIDE)], 0).T
-    for copy in range(shares_ref.shape[0]):
-        shares_ref[copy, :head_width, :] = grad_weight
-        shares_ref[copy, head_width:, :] = extra[:SUB]
+    peers = shares_ref.shape[0]
+    each = head_width // peers
+    shares_ref[...] = jnp.zeros(shares_ref.shape, WIDE)
+    for peer in range(peers):
+        shares_ref[peer, :each, :] = grad_weight[peer * each : (peer + 1) * each]
+        shares_ref[peer, each : 2 * each, :] = extra[peer * each : (peer + 1) * each]
     store.wait()
 
 
-def last_kernel(parts_ref, weight_ref, attention_ref, bias_ref):
+def relay_kernel(parts_ref, out_ref):
     total = parts_ref[0]
     for part in range(1, parts_ref.shape[0]):
         total = total + parts_ref[part]
+    for copy in range(out_ref.shape[0]):
+        out_ref[copy] = total
+
+
+def keep_kernel(sums_ref, out_ref):
+    out_ref[...] = sums_ref[0]
+
+
+def last_kernel(me_ref, parts_ref, kept_ref, weight_ref, attention_ref, bias_ref, extra_ref):
+    peers = parts_ref.shape[0]
     head_width = weight_ref.shape[0]
-    weight_ref[...] = total[:head_width]
-    attention_ref[0] = total[head_width : head_width + 1, :head_width]
-    attention_ref[1] = total[head_width + 1 : head_width + 2, :head_width]
-    bias_ref[...] = total[head_width + 2 : head_width + 3, :head_width]
+    each = head_width // peers
+    extra_ref[...] = jnp.zeros(extra_ref.shape, WIDE)
+    for peer in range(peers):
+        weight_ref[peer * each : (peer + 1) * each, :] = parts_ref[peer, :each]
+        extra_ref[peer * each : (peer + 1) * each, :] = parts_ref[peer, each : 2 * each]
+    mine = pl.ds(me_ref[0] * each, each)
+    weight_ref[mine, :] = kept_ref[:each]
+    extra_ref[mine, :] = kept_ref[each : 2 * each]
+    turned = extra_ref[...].T
+    attention_ref[0] = turned[0:1, :head_width]
+    attention_ref[1] = turned[1:2, :head_width]
+    bias_ref[...] = turned[2:3, :head_width]
 
 
 def vmem():
@@ -475,8 +496,8 @@
     return pl.pallas_call(
         layer_kernel,
         out_shape=(
-            jax.ShapeDtypeStruct((head_width, node_count), LOW),
-            jax.ShapeDtypeStruct((peer_count, head_width + SUB, in_width), WIDE),
+            jax.ShapeDtypeStruct((block_count, head_width, BLK), LOW),
+            jax.ShapeDtypeStruct((peer_count, SUB, in_width), WIDE),
         ),
         in_specs=[smem()] * 3 + [vmem()] * 3 + [anywhere()] * len(streamed),
         out_specs=(anywhere(), vmem()),
@@ -493,7 +514,7 @@
         ]
         + [pltpu.VMEM(value.shape, value.dtype) for value in streamed]
         + [
-            pltpu.VMEM((head_width, node_count), LOW),
+            pltpu.VMEM((block_count, head_width, BLK), LOW),
             pltpu.SemaphoreType.DMA((len(streamed) + 1,)),
         ],
         compiler_params=pltpu.CompilerParams(vmem_limit_bytes=LAYER_LIMIT),
@@ -533,7 +554,7 @@
     projt, score, stats, band, grad_bias = own_part(
         local_pairs, features, weight, consts, cotangent
     )
-    output, shares = attention_layer(
+    output_blocks, shares = attention_layer(
         incoming_live,
         local_pairs,
         remote_pairs,
@@ -550,7 +571,24 @@
         band,
         features,
     )
-    gathered = lax.all_to_all(shares, "dom", 0, 0, tiled=True)
+    output = output_blocks.transpose(1, 0, 2).reshape(head_width, node_count)
+    partial_sums, output = lax.optimization_barrier((exchange(shares), output))
+    chunk_sums = pl.pallas_call(
+        relay_kernel,
+        out_shape=jax.ShapeDtypeStruct(shares.shape, WIDE),
+        in_specs=[vmem()],
+        out_specs=vmem(),
+        compiler_params=pltpu.CompilerParams(vmem_limit_bytes=SMALL_LIMIT),
+        name="relay_sums",
+    )(partial_sums)
+    kept = pl.pallas_call(
+        keep_kernel,
+        out_shape=jax.ShapeDtypeStruct(shares.shape[1:], WIDE),
+        in_specs=[vmem()],
+        out_specs=vmem(),
+        compiler_params=pltpu.CompilerParams(vmem_limit_bytes=SMALL_LIMIT),
+        name="keep_own",
+    )(chunk_sums)
     grad_weight, grad_attention, grad_bias = pl.pallas_call(
         last_kernel,
         out_shape=(
@@ -558,11 +596,17 @@
             jax.ShapeDtypeStruct((2, 1, head_width), WIDE),
             jax.ShapeDtypeStruct((1, head_width), WIDE),
         ),
-        in_specs=[vmem()],
+        in_specs=[smem(), vmem(), vmem()],
         out_specs=(vmem(), vmem(), vmem()),
+        scratch_shapes=[pltpu.VMEM((in_width, in_width), WIDE)],
+        compiler_params=pltpu.CompilerParams(vmem_limit_bytes=SMALL_LIMIT),
         name="last_sums",
-    )(gathered)
+    )(me[None], exchange(chunk_sums), kept)
     return output, grad_weight.T, grad_attention, grad_bias[0]
+
+
+def exchange(values):
+    return lax.all_to_all(values, "dom", 0, 0, tiled=True)
 
 
 def solution(mesh):

time: 102 us -> 99.5 us (0.975)
  blocking collectives: 24.2 us -> 0 us
  waiting for transfers between devices: 7.33 us -> 19.8 us
  starting transfers between devices: 10.7 us -> 18.6 us
    all_to_all x1 -> x0, blocking collectives: 24.2 us -> none  [per_device(): gathered = lax.all_to_all(shares, 'dom', 0, 0, tiled=True)]
    all_to_all x0 -> x2, waiting for transfers between devices: none -> 12.4 us  [exchange(): return lax.all_to_all(values, 'dom', 0, 0, tiled=True)]
    all_to_all x0 -> x2, starting transfers between devices: none -> 8.25 us  [exchange(): return lax.all_to_all(values, 'dom', 0, 0, tiled=True)]
    reshape x0 -> x1, local copies, waits for them, and re-layouts: none -> 2.33 us  [per_device(): output = output_blocks.transpose(1, 0, 2).reshape(head_width, node_count)]
    unnamed x26 -> x24, local copies, waits for them, and re-layouts: 7.42 us -> 6.05 us
    pallas_call x1, Pallas kernels: 1.96 us -> 0.65 us  [per_device(): pl.pallas_call(last_kernel, out_shape=(jax.ShapeDtypeStruct((head_width,...]
    pallas_call x1 -> x3, Pallas kernels: 24 us -> 25.2 us  [the longest x1 23.5 us: attention_layer(): pl.pallas_call(layer_kernel, out_shape=(jax.ShapeDtypeStruct((block_count...]
  transfers between devices with their start and end apart: 1 -> 3, of which waited for: 1 -> 3; matrix products, arithmetic and copies ran while one was open for 5% -> 7% of each run, Pallas kernels for 16% -> 17%
where the time goes in v4:
time: 99.5 us; the launch traced here: 99 us
  Pallas kernels  50.1 us (50%)
  waiting for transfers between devices  19.8 us (20%)
  starting transfers between devices  18.6 us (19%)
  local copies, waits for them, and re-layouts  9.81 us (10%)
    pallas_call x1, Pallas kernels, attention_layer(): pl.pallas_call(layer_kernel, out_shape=(jax.ShapeDtypeStruct((block_count...  23.5 us
    pallas_call x1, Pallas kernels, own_part(): pl.pallas_call(own_kernel, out_shape=(jax.ShapeDtypeStruct((block_count,...  15.8 us
    all_to_all x2, waiting for transfers between devices, exchange(): return lax.all_to_all(values, 'dom', 0, 0, tiled=True)  12.4 us
    all_to_all x1, starting transfers between devices, per_device(): lax.all_to_all(outgoing.reshape(peer_count, capacity, in_width), 'dom', 0...  10.4 us
    pallas_call x1, Pallas kernels, gather_rows(): pl.pallas_call(gather_kernel, out_shape=jax.ShapeDtypeStruct((slots, in_w...  8.46 us
    all_to_all x2, starting transfers between devices, exchange(): return lax.all_to_all(values, 'dom', 0, 0, tiled=True)  8.25 us
    all_to_all x1, waiting for transfers between devices, per_device(): lax.all_to_all(outgoing.reshape(peer_count, capacity, in_width), 'dom', 0...  7.44 us
    unnamed x24, local copies, waits for them, and re-layouts  6.05 us
  transfers between devices with their start and end apart: 3, of which 3 were waited for; matrix products, arithmetic and copies ran while one was open for 7% of the time, Pallas kernels for 17%

profile of v4, /device:TPU:1, one launch (start us, length us, event | category | flops | bytes accessed | tf_op | source)
XLA Modules:
  0.0 99.0 jit_solution(2222773444472771304)
XLA Ops:
  0.6 0.0 copy-start
  0.7 0.8 copy.31
  1.4 0.0 copy-done
  1.5 0.0 copy-start.1
  1.5 1.6 %copy-done.1 = bf16[8192,128]{1,0:T(8,128)(2,1)S(1)} copy-done((bf16[8192,128]{1,0:T(8,128)(2,1)S(1)}, bf16[8192,128]{1,0:T(8,128)(2,1)}, u32[]{:S(2)}) %copy-start.1) | copy-done | bytes 2097176
  3.1 8.5 %gather_rows.1 = bf16[8192,128]{1,0:T(8,128)(2,1)} custom-call(s32[8192]{0:T(1024)S(1)} %bitcast.17, s32[32]{0:T(128)S(1)} %dynamic-slice_bitcast_fusion.live_ref, bf16[8192,128]{1,0:T(8,128)(2,1)S(1)} %copy-done.1), custom_call_target="tpu_custom_call" | custom-call | tf_op jit(solution)/shard_map/gather_rows/pallas_call | solution.py:449
  11.5 0.0 copy-start.2
  11.5 0.0 copy-start.7
  11.5 0.0 copy-start.8
  11.6 10.4 %all-to-all-start = ((bf16[32,256,128]{2,1,0:T(8,128)(2,1)}), bf16[32,256,128]{2,1,0:T(8,128)(2,1)}, u32[]{:S(2)}, u32[]{:S(2)}) async-start(bf16[32,256,128]{2,1,0:T(8,128)(2,1)} %bitcast.3), calls=%async_computation | async-start | bytes 4194304 | tf_op jit(solution)/shard_map/all_to_all | solution.py:548
  21.9 0.0 copy-done.4
  21.9 0.7 copy.26.weight_ref
  22.6 0.7 copy.24.local_pairs_ref
  23.4 0.0 copy-done.6
  23.4 0.7 copy.25.remote_pairs_ref
  24.1 0.7 copy.28.remote_counts_hbm
  24.8 0.0 copy-done.2
  24.8 0.8 copy.27.local_counts_hbm
  25.6 0.7 dynamic-slice_reduce_fusion.incoming_ref
  26.3 0.0 copy-done.7
  26.3 0.7 broadcast_in_dim.13.consts_ref
  27.0 15.8 %own_part.1 = (bf16[64,64,128]{2,1,0:T(8,128)(2,1)}, f32[64,8,128]{2,1,0:T(8,128)}, f32[64,8,128]{2,1,0:T(8,128)}, f32[64,5,8,128]{3,2,1,0:T(8,128)}, f32[64,128]{1,0:T(8,128)}) custom-call(s32[64,5]{1,0:T(8,128)} %copy.24.local_pairs_ref, bf16[8192,128]{1,0:T(8,128)(2,1)} %own_hbm.1, bf16[128,64]{1,0:T(8,128)(2,1)} %copy.26.weight_ref, ...), custom_call_target="tpu_custom_call" | custom-call | flops 10000000000 | bytes 8000000 | tf_op jit(solution)/shard_map/own_part/pallas_call | solution.py:469
  42.8 7.4 %all-to-all-done = bf16[32,256,128]{2,1,0:T(8,128)(2,1)} async-done(((bf16[32,256,128]{2,1,0:T(8,128)(2,1)}), bf16[32,256,128]{2,1,0:T(8,128)(2,1)}, u32[]{:S(2)}, u32[]{:S(2)}) %all-to-all-start) | async-done | bytes 2097184 | tf_op jit(solution)/shard_map/all_to_all | solution.py:548
  50.3 23.5 %attention_layer.1 = (bf16[64,64,128]{2,1,0:T(8,128)(2,1)}, f32[32,8,128]{2,1,0:T(8,128)}) custom-call(s32[32]{0:T(128)} %dynamic-slice_reduce_fusion.incoming_ref, s32[64,5]{1,0:T(8,128)} %copy.24.local_pairs_ref, s32[64,3]{1,0:T(8,128)} %copy.25.remote_pairs_ref, bf16[128,64]{1,0:T(8,128)(2,1)} %copy.26.weight_ref, ...), custom_call_target="tpu_custom_call" | custom-call | flops 10000000000 | bytes 10000000 | tf_op jit(solution)/shard_map/attention_layer/pallas_call | solution.py:496
  73.8 4.4 %all-to-all-start.1 = ((f32[32,8,128]{2,1,0:T(8,128)}), f32[32,8,128]{2,1,0:T(8,128)S(1)}, u32[]{:S(2)}, u32[]{:S(2)}) async-start(f32[32,8,128]{2,1,0:T(8,128)} %get-tuple-element.21), calls=%async_computation.1 | async-start | bytes 262144 | tf_op jit(solution)/shard_map/all_to_all | solution.py:609
  78.2 2.3 %copy_bitcast_fusion = bf16[64,8192]{1,0:T(8,128)(2,1)} fusion(bf16[64,64,128]{2,1,0:T(8,128)(2,1)} %get-tuple-element.22), kind=kLoop, calls=%fused_computation | loop fusion | bytes 2097152 | tf_op jit(solution)/shard_map/reshape | solution.py:574
  80.5 5.5 %all-to-all-done.1.parts_ref = f32[32,8,128]{2,1,0:T(8,128)S(1)} async-done(((f32[32,8,128]{2,1,0:T(8,128)}), f32[32,8,128]{2,1,0:T(8,128)S(1)}, u32[]{:S(2)}, u32[]{:S(2)}) %all-to-all-start.1) | async-done | bytes 131104 | tf_op jit(solution)/shard_map/all_to_all | solution.py:609
  86.0 0.7 relay_sums.1.sums_ref
  86.7 3.9 %all-to-all-start.2 = ((f32[32,8,128]{2,1,0:T(8,128)}), f32[32,8,128]{2,1,0:T(8,128)S(1)}, u32[]{:S(2)}, u32[]{:S(2)}) async-start(f32[32,8,128]{2,1,0:T(8,128)} %relay_sums.1.sums_ref), calls=%async_computation.2 | async-start | bytes 262144 | tf_op jit(solution)/shard_map/all_to_all | solution.py:609
  90.6 0.9 keep_own.1.kept_ref
  91.5 6.9 %all-to-all-done.2.parts_ref = f32[32,8,128]{2,1,0:T(8,128)S(1)} async-done(((f32[32,8,128]{2,1,0:T(8,128)}), f32[32,8,128]{2,1,0:T(8,128)S(1)}, u32[]{:S(2)}, u32[]{:S(2)}) %all-to-all-start.2) | async-done | bytes 131104 | tf_op jit(solution)/shard_map/all_to_all | solution.py:609
  98.4 0.7 last_sums.1
  (9 shorter events, 0.0 us)
Async XLA Ops:
  0.6 0.8 copy-start
  1.5 1.6 %copy-start.1 = (bf16[8192,128]{1,0:T(8,128)(2,1)S(1)}, bf16[8192,128]{1,0:T(8,128)(2,1)}, u32[]{:S(2)}) copy-start(bf16[8192,128]{1,0:T(8,128)(2,1)} %own_hbm.1) | copy-start | bytes 6291460
  11.5 10.4 %copy-start.4 = (bf16[128,64]{0,1:T(8,128)(2,1)S(1)}, bf16[128,64]{0,1:T(8,128)(2,1)}, u32[]{:S(2)}) copy-start(bf16[128,64]{0,1:T(8,128)(2,1)} %param.12) | copy-start | bytes 49156
  11.5 11.1 %copy-start.5 = (s32[64,5]{0,1:T(8,128)S(1)}, s32[64,5]{0,1:T(8,128)}, u32[]{:S(2)}) copy-start(s32[64,5]{0,1:T(8,128)} %param.16) | copy-start | bytes 3844
  11.5 11.8 %copy-start.6 = (s32[64,3]{0,1:T(4,128)S(1)}, s32[64,3]{0,1:T(4,128)}, u32[]{:S(2)}) copy-start(s32[64,3]{0,1:T(4,128)} %param.18) | copy-start | bytes 2308
  11.5 12.5 %copy-start.3 = (s32[64,3,128]{2,0,1:T(8,128)S(1)}, s32[64,3,128]{2,0,1:T(8,128)}, u32[]{:S(2)}) copy-start(s32[64,3,128]{2,0,1:T(8,128)} %param.19) | copy-start | bytes 294916
  11.5 13.3 %copy-start.2 = (s32[64,5,128]{2,0,1:T(8,128)S(1)}, s32[64,5,128]{2,0,1:T(8,128)}, u32[]{:S(2)}) copy-start(s32[64,5,128]{2,0,1:T(8,128)} %param.17) | copy-start | bytes 491524
  11.5 14.7 %copy-start.7 = (f32[2,1,64]{2,1,0:T(1,128)S(1)}, f32[2,1,64]{2,1,0:T(1,128)}, u32[]{:S(2)}) copy-start(f32[2,1,64]{2,1,0:T(1,128)} %param.13) | copy-start | bytes 1540
  11.5 14.7 %copy-start.8 = (f32[64]{0:T(128)S(1)}, f32[64]{0:T(128)}, u32[]{:S(2)}) copy-start(f32[64]{0:T(128)} %param.14) | copy-start | bytes 772
  11.6 38.7 %all-to-all-start = ((bf16[32,256,128]{2,1,0:T(8,128)(2,1)}), bf16[32,256,128]{2,1,0:T(8,128)(2,1)}, u32[]{:S(2)}, u32[]{:S(2)}) async-start(bf16[32,256,128]{2,1,0:T(8,128)(2,1)} %bitcast.3), calls=%async_computation | async-start | bytes 4194304 | tf_op jit(solution)/shard_map/all_to_all | solution.py:548
  73.8 12.2 %all-to-all-start.1 = ((f32[32,8,128]{2,1,0:T(8,128)}), f32[32,8,128]{2,1,0:T(8,128)S(1)}, u32[]{:S(2)}, u32[]{:S(2)}) async-start(f32[32,8,128]{2,1,0:T(8,128)} %get-tuple-element.21), calls=%async_computation.1 | async-start | bytes 262144 | tf_op jit(solution)/shard_map/all_to_all | solution.py:609
  86.7 11.7 %all-to-all-start.2 = ((f32[32,8,128]{2,1,0:T(8,128)}), f32[32,8,128]{2,1,0:T(8,128)S(1)}, u32[]{:S(2)}, u32[]{:S(2)}) async-start(f32[32,8,128]{2,1,0:T(8,128)} %relay_sums.1.sums_ref), calls=%async_computation.2 | async-start | bytes 262144 | tf_op jit(solution)/shard_map/all_to_all | solution.py:609

commit v5 on v4

--- a/solution.py
+++ b/solution.py
@@ -14,7 +14,7 @@
 OWN_LIMIT = 62 * 1024 * 1024
 SMALL_LIMIT = 4 * 1024 * 1024
 LAYER_LIMIT = 60 * 1024 * 1024
-TURN_BLOCKS = 8
+TURN_BLOCKS = 16
 WEIGHT_GROUP = 8
 SHARE_GROUP = 2
 GATHER_STEP = 32
@@ -127,7 +127,7 @@
 
 
 def own_kernel(
-    local_pairs_ref,
+    pairs_ref,
     own_ref,
     weight_ref,
     consts_ref,
@@ -140,7 +140,8 @@
     proj_ref,
 ):
     block_count = own_ref.shape[0] // BLK
-    local_count = local_pairs_ref.shape[1]
+    local_count = band_ref.shape[1]
+    pair_count = pairs_ref.shape[0] // block_count
     weight = weight_ref[...]
     weight_turned = weight.astype(WIDE).T.astype(LOW)
 
@@ -161,7 +162,7 @@
     def one_block(block, carry):
         upstream = cotangent_ref[:, at_block(block)]
         for pair in range(local_count):
-            rows = proj_ref[local_pairs_ref[block, pair]]
+            rows = proj_ref[pairs_ref[block * pair_count + pair]]
             band_ref[block, pair] = band_of(jnp.dot(rows, upstream, preferred_element_type=WIDE))
         return carry
 
@@ -170,8 +171,7 @@
 
 def layer_kernel(
     incoming_ref,
-    local_pairs_ref,
-    remote_pairs_ref,
+    pairs_ref,
     weight_ref,
     consts_ref,
     bias_ref,
@@ -226,9 +226,9 @@
         fetch.start()
     block_count = own_ref.shape[0] // BLK
     halo_count = halo_ref.shape[0] // BLK
-    local_count = local_pairs_ref.shape[1]
-    remote_count = remote_pairs_ref.shape[1]
-    pair_count = local_count + remote_count
+    local_count = band_ref.shape[1]
+    pair_count = pairs_ref.shape[0] // block_count
+    remote_count = pair_count - local_count
     head_width = weight_ref.shape[1]
     step_index, lane_index = tile_steps()
     row_all = lax.broadcasted_iota(jnp.int32, (BLK, BLK), 0)
@@ -255,7 +255,7 @@
         halo_score_ref[block] = skew(jnp.where(live, source, -jnp.inf))
         return carry
 
-    lax.fori_loop(0, halo_count, halo_table, 0, unroll=16)
+    lax.fori_loop(0, halo_count, halo_table, 0, unroll=32)
 
     def band_values(tiles):
         parts = []
@@ -269,8 +269,8 @@
         nodes = at_block(block)
         upstream = cotangent_ref[:, nodes]
         upstream_wide = upstream.astype(WIDE)
-        near = [local_pairs_ref[block, k] for k in range(local_count)]
-        far = [remote_pairs_ref[block, k] for k in range(remote_count)]
+        near = [pairs_ref[block * pair_count + k] for k in range(local_count)]
+        far = [pairs_ref[block * pair_count + k] for k in range(local_count, pair_count)]
         counts = [local_counts_ref[block, k : k + 1, :] for k in range(local_count)]
         counts += [remote_counts_ref[block, k : k + 1, :] for k in range(remote_count)]
         target_score = spread(stats_ref[block, 1:2, :])
@@ -356,8 +356,8 @@
     def finish(index, rows, own, carry):
         grad_weight, from_src, from_dst = carry
         parts = []
-        for part in range(2):
-            at = index * 2 + part
+        for part in range(8):
+            at = index * 8 + part
             if own:
                 turned = own_projt_ref[at].astype(WIDE)
                 source = unskew(own_src_ref[at]) + own_rows_ref[at, 0:1, :]
@@ -378,15 +378,15 @@
         return grad_weight, from_src, from_dst
 
     def finish_own(index, carry):
-        return finish(index, own_ref[at_block(index, 2), :], True, carry)
+        return finish(index, own_ref[at_block(index, 8), :], True, carry)
 
     def finish_halo(index, carry):
-        return finish(index, halo_ref[at_block(index, 2), :], False, carry)
+        return finish(index, halo_ref[at_block(index, 8), :], False, carry)
 
     zero = jnp.zeros((head_width, BLK), WIDE)
     carry = (jnp.zeros((2 * head_width, own_ref.shape[1]), WIDE), zero, zero)
-    carry = lax.fori_loop(0, block_count // 2, finish_own, carry, unroll=8)
-    carry = lax.fori_loop(0, halo_count // 2, finish_halo, carry, unroll=8)
+    carry = lax.fori_loop(0, block_count // 8, finish_own, carry, unroll=8)
+    carry = lax.fori_loop(0, halo_count // 8, finish_halo, carry, unroll=8)
     grad_weight, from_src, from_dst = carry
     grad_weight = grad_weight[:head_width] + grad_weight[head_width:]
     lanes = lax.broadcasted_iota(jnp.int32, (head_width, BLK), 1)
@@ -460,11 +460,10 @@
     )(rows, live, features)
 
 
-def own_part(*operands):
-    local_pairs, features, weight = operands[:3]
+def own_part(local_count, *operands):
+    pairs, features, weight = operands[:3]
     head_width = weight.shape[1]
     block_count = features.shape[0] // BLK
-    local_count = local_pairs.shape[1]
     tiles = jax.ShapeDtypeStruct((block_count, SUB, BLK), WIDE)
     return pl.pallas_call(
         own_kernel,
@@ -485,8 +484,8 @@
 
 
 def attention_layer(*operands):
-    incoming, local_pairs, remote_pairs, weight = operands[:4]
-    streamed = operands[6:]
+    incoming, pairs, weight = operands[:3]
+    streamed = operands[5:]
     halo, cotangent = streamed[0], streamed[4]
     peer_count = incoming.shape[0]
     in_width = halo.shape[1]
@@ -499,7 +498,7 @@
             jax.ShapeDtypeStruct((block_count, head_width, BLK), LOW),
             jax.ShapeDtypeStruct((peer_count, SUB, in_width), WIDE),
         ),
-        in_specs=[smem()] * 3 + [vmem()] * 3 + [anywhere()] * len(streamed),
+        in_specs=[smem()] * 2 + [vmem()] * 3 + [anywhere()] * len(streamed),
         out_specs=(anywhere(), vmem()),
         scratch_shapes=[
             pltpu.VMEM((halo_count, BLK, head_width), LOW),
@@ -551,13 +550,13 @@
     consts = jnp.broadcast_to(
         jnp.concatenate([attention[:, 0], bias[None]], 0)[:, :, None], (3, head_width, BLK)
     )
+    pairs = jnp.concatenate([local_pairs, remote_pairs], 1).reshape(-1)
     projt, score, stats, band, grad_bias = own_part(
-        local_pairs, features, weight, consts, cotangent
+        local_pairs.shape[1], pairs, features, weight, consts, cotangent
     )
     output_blocks, shares = attention_layer(
         incoming_live,
-        local_pairs,
-        remote_pairs,
+        pairs,
         weight,
         consts,
         grad_bias,

time: 99.5 us -> 95.1 us (0.956)
  Pallas kernels: 50.1 us -> 46 us
    pallas_call x1, Pallas kernels: 23.5 us -> 19.2 us  [attention_layer(): pl.pallas_call(layer_kernel, out_shape=(jax.ShapeDtypeStruct((block_count...]
    unnamed x24 -> x22, local copies, waits for them, and re-layouts: 6.05 us -> 4.66 us
  transfers between devices with their start and end apart: 3 -> 3, of which waited for: 3 -> 3; matrix products, arithmetic and copies ran while one was open for 7% -> 7% of each run, Pallas kernels for 17% -> 18%
where the time goes in v5:
time: 95.1 us; the launch traced here: 94.7 us
  Pallas kernels  46 us (48%)
  waiting for transfers between devices  20.4 us (21%)
  starting transfers between devices  18.3 us (19%)
  local copies, waits for them, and re-layouts  9.19 us (10%)
    pallas_call x1, Pallas kernels, attention_layer(): pl.pallas_call(layer_kernel, out_shape=(jax.ShapeDtypeStruct((block_count...  19.2 us
    pallas_call x1, Pallas kernels, own_part(): pl.pallas_call(own_kernel, out_shape=(jax.ShapeDtypeStruct((block_count,...  15.8 us
    all_to_all x2, waiting for transfers between devices, exchange(): return lax.all_to_all(values, 'dom', 0, 0, tiled=True)  12.4 us
    all_to_all x1, starting transfers between devices, per_device(): lax.all_to_all(outgoing.reshape(peer_count, capacity, in_width), 'dom', 0...  10 us
    pallas_call x1, Pallas kernels, gather_rows(): pl.pallas_call(gather_kernel, out_shape=jax.ShapeDtypeStruct((slots, in_w...  8.68 us
    all_to_all x2, starting transfers between devices, exchange(): return lax.all_to_all(values, 'dom', 0, 0, tiled=True)  8.28 us
    all_to_all x1, waiting for transfers between devices, per_device(): lax.all_to_all(outgoing.reshape(peer_count, capacity, in_width), 'dom', 0...  8.01 us
    unnamed x22, local copies, waits for them, and re-layouts  4.66 us
  transfers between devices with their start and end apart: 3, of which 3 were waited for; matrix products, arithmetic and copies ran while one was open for 7% of the time, Pallas kernels for 18%

profile of v5, /device:TPU:1, one launch (start us, length us, event | category | flops | bytes accessed | tf_op | source)
XLA Modules:
  0.0 94.7 jit_solution(13980895558061115139)
XLA Ops:
  0.6 0.0 copy-start
  0.7 0.8 copy.26
  1.4 0.0 copy-done
  1.5 0.0 copy-start.1
  1.5 1.6 %copy-done.1 = bf16[8192,128]{1,0:T(8,128)(2,1)S(1)} copy-done((bf16[8192,128]{1,0:T(8,128)(2,1)S(1)}, bf16[8192,128]{1,0:T(8,128)(2,1)}, u32[]{:S(2)}) %copy-start.1) | copy-done | bytes 2097176
  3.1 8.7 %gather_rows.1 = bf16[8192,128]{1,0:T(8,128)(2,1)} custom-call(s32[8192]{0:T(1024)S(1)} %bitcast.17, s32[32]{0:T(128)S(1)} %dynamic-slice_bitcast_fusion.live_ref, bf16[8192,128]{1,0:T(8,128)(2,1)S(1)} %copy-done.1), custom_call_target="tpu_custom_call" | custom-call | tf_op jit(solution)/shard_map/gather_rows/pallas_call | solution.py:449
  11.7 0.0 copy-start.2
  11.8 0.0 copy-start.7
  11.8 0.0 copy-start.8
  11.8 10.0 %all-to-all-start = ((bf16[32,256,128]{2,1,0:T(8,128)(2,1)}), bf16[32,256,128]{2,1,0:T(8,128)(2,1)}, u32[]{:S(2)}, u32[]{:S(2)}) async-start(bf16[32,256,128]{2,1,0:T(8,128)(2,1)} %bitcast.3), calls=%async_computation | async-start | bytes 4194304 | tf_op jit(solution)/shard_map/all_to_all | solution.py:547
  21.8 0.0 copy-done.5
  21.9 0.1 copy.19
  21.9 0.7 reshape.24.pairs_ref
  22.6 0.0 copy-done.4
  22.6 0.7 copy.21.weight_ref
  23.4 0.0 copy-done.3
  23.4 0.7 copy.23.remote_counts_hbm
  24.1 0.8 copy.22.local_counts_hbm
  24.9 0.7 dynamic-slice_reduce_fusion.incoming_ref
  25.6 0.0 copy-done.8
  25.6 0.7 broadcast_in_dim.13.consts_ref
  26.3 15.8 %own_part.1 = (bf16[64,64,128]{2,1,0:T(8,128)(2,1)}, f32[64,8,128]{2,1,0:T(8,128)}, f32[64,8,128]{2,1,0:T(8,128)}, f32[64,5,8,128]{3,2,1,0:T(8,128)}, f32[64,128]{1,0:T(8,128)}) custom-call(s32[512]{0:T(512)} %reshape.24.pairs_ref, bf16[8192,128]{1,0:T(8,128)(2,1)} %own_hbm.1, bf16[128,64]{1,0:T(8,128)(2,1)} %copy.21.weight_ref, ...), custom_call_target="tpu_custom_call" | custom-call | flops 10000000000 | bytes 8000000 | tf_op jit(solution)/shard_map/own_part/pallas_call | solution.py:468
  42.2 8.0 %all-to-all-done = bf16[32,256,128]{2,1,0:T(8,128)(2,1)} async-done(((bf16[32,256,128]{2,1,0:T(8,128)(2,1)}), bf16[32,256,128]{2,1,0:T(8,128)(2,1)}, u32[]{:S(2)}, u32[]{:S(2)}) %all-to-all-start) | async-done | bytes 2097184 | tf_op jit(solution)/shard_map/all_to_all | solution.py:547
  50.2 19.2 %attention_layer.1 = (bf16[64,64,128]{2,1,0:T(8,128)(2,1)}, f32[32,8,128]{2,1,0:T(8,128)}) custom-call(s32[32]{0:T(128)} %dynamic-slice_reduce_fusion.incoming_ref, s32[512]{0:T(512)} %reshape.24.pairs_ref, bf16[128,64]{1,0:T(8,128)(2,1)} %copy.21.weight_ref, f32[3,64,128]{2,1,0:T(8,128)} %broadcast_in_dim.13.consts_ref, ...), custom_call_target="tpu_custom_call" | custom-call | flops 10000000000 | bytes 10000000 | tf_op jit(solution)/shard_map/attention_layer/pallas_call | solution.py:495
  69.4 4.4 %all-to-all-start.1 = ((f32[32,8,128]{2,1,0:T(8,128)}), f32[32,8,128]{2,1,0:T(8,128)S(1)}, u32[]{:S(2)}, u32[]{:S(2)}) async-start(f32[32,8,128]{2,1,0:T(8,128)} %get-tuple-element.21), calls=%async_computation.1 | async-start | bytes 262144 | tf_op jit(solution)/shard_map/all_to_all | solution.py:608
  73.8 2.3 %copy_bitcast_fusion = bf16[64,8192]{1,0:T(8,128)(2,1)} fusion(bf16[64,64,128]{2,1,0:T(8,128)(2,1)} %get-tuple-element.22), kind=kLoop, calls=%fused_computation | loop fusion | bytes 2097152 | tf_op jit(solution)/shard_map/reshape | solution.py:573
  76.1 5.5 %all-to-all-done.1.parts_ref = f32[32,8,128]{2,1,0:T(8,128)S(1)} async-done(((f32[32,8,128]{2,1,0:T(8,128)}), f32[32,8,128]{2,1,0:T(8,128)S(1)}, u32[]{:S(2)}, u32[]{:S(2)}) %all-to-all-start.1) | async-done | bytes 131104 | tf_op jit(solution)/shard_map/all_to_all | solution.py:608
  81.6 0.7 relay_sums.1.sums_ref
  82.3 3.9 %all-to-all-start.2 = ((f32[32,8,128]{2,1,0:T(8,128)}), f32[32,8,128]{2,1,0:T(8,128)S(1)}, u32[]{:S(2)}, u32[]{:S(2)}) async-start(f32[32,8,128]{2,1,0:T(8,128)} %relay_sums.1.sums_ref), calls=%async_computation.2 | async-start | bytes 262144 | tf_op jit(solution)/shard_map/all_to_all | solution.py:608
  86.2 0.9 keep_own.1.kept_ref
  87.1 6.9 %all-to-all-done.2.parts_ref = f32[32,8,128]{2,1,0:T(8,128)S(1)} async-done(((f32[32,8,128]{2,1,0:T(8,128)}), f32[32,8,128]{2,1,0:T(8,128)S(1)}, u32[]{:S(2)}, u32[]{:S(2)}) %all-to-all-start.2) | async-done | bytes 131104 | tf_op jit(solution)/shard_map/all_to_all | solution.py:608
  94.0 0.7 last_sums.1
  (10 shorter events, 0.0 us)
Async XLA Ops:
  0.6 0.8 copy-start
  1.5 1.6 %copy-start.1 = (bf16[8192,128]{1,0:T(8,128)(2,1)S(1)}, bf16[8192,128]{1,0:T(8,128)(2,1)}, u32[]{:S(2)}) copy-start(bf16[8192,128]{1,0:T(8,128)(2,1)} %own_hbm.1) | copy-start | bytes 6291460
  11.7 10.1 %copy-start.5 = (s32[64,5]{0,1:T(8,128)S(1)}, s32[64,5]{0,1:T(8,128)}, u32[]{:S(2)}) copy-start(s32[64,5]{0,1:T(8,128)} %param.16) | copy-start | bytes 3844
  11.7 10.1 %copy-start.6 = (s32[64,3]{0,1:T(4,128)S(1)}, s32[64,3]{0,1:T(4,128)}, u32[]{:S(2)}) copy-start(s32[64,3]{0,1:T(4,128)} %param.18) | copy-start | bytes 2308
  11.7 10.9 %copy-start.4 = (bf16[128,64]{0,1:T(8,128)(2,1)S(1)}, bf16[128,64]{0,1:T(8,128)(2,1)}, u32[]{:S(2)}) copy-start(bf16[128,64]{0,1:T(8,128)(2,1)} %param.12) | copy-start | bytes 49156
  11.7 11.6 %copy-start.3 = (s32[64,3,128]{2,0,1:T(8,128)S(1)}, s32[64,3,128]{2,0,1:T(8,128)}, u32[]{:S(2)}) copy-start(s32[64,3,128]{2,0,1:T(8,128)} %param.19) | copy-start | bytes 294916
  11.7 12.3 %copy-start.2 = (s32[64,5,128]{2,0,1:T(8,128)S(1)}, s32[64,5,128]{2,0,1:T(8,128)}, u32[]{:S(2)}) copy-start(s32[64,5,128]{2,0,1:T(8,128)} %param.17) | copy-start | bytes 491524
  11.8 13.8 %copy-start.7 = (f32[2,1,64]{2,1,0:T(1,128)S(1)}, f32[2,1,64]{2,1,0:T(1,128)}, u32[]{:S(2)}) copy-start(f32[2,1,64]{2,1,0:T(1,128)} %param.13) | copy-start | bytes 1540
  11.8 13.8 %copy-start.8 = (f32[64]{0:T(128)S(1)}, f32[64]{0:T(128)}, u32[]{:S(2)}) copy-start(f32[64]{0:T(128)} %param.14) | copy-start | bytes 772
  11.8 38.4 %all-to-all-start = ((bf16[32,256,128]{2,1,0:T(8,128)(2,1)}), bf16[32,256,128]{2,1,0:T(8,128)(2,1)}, u32[]{:S(2)}, u32[]{:S(2)}) async-start(bf16[32,256,128]{2,1,0:T(8,128)(2,1)} %bitcast.3), calls=%async_computation | async-start | bytes 4194304 | tf_op jit(solution)/shard_map/all_to_all | solution.py:547
  69.4 12.2 %all-to-all-start.1 = ((f32[32,8,128]{2,1,0:T(8,128)}), f32[32,8,128]{2,1,0:T(8,128)S(1)}, u32[]{:S(2)}, u32[]{:S(2)}) async-start(f32[32,8,128]{2,1,0:T(8,128)} %get-tuple-element.21), calls=%async_computation.1 | async-start | bytes 262144 | tf_op jit(solution)/shard_map/all_to_all | solution.py:608
  82.3 11.7 %all-to-all-start.2 = ((f32[32,8,128]{2,1,0:T(8,128)}), f32[32,8,128]{2,1,0:T(8,128)S(1)}, u32[]{:S(2)}, u32[]{:S(2)}) async-start(f32[32,8,128]{2,1,0:T(8,128)} %relay_sums.1.sums_ref), calls=%async_computation.2 | async-start | bytes 262144 | tf_op jit(solution)/shard_map/all_to_all | solution.py:608

commit v6 on v5

--- a/solution.py
+++ b/solution.py
@@ -15,6 +15,7 @@
 SMALL_LIMIT = 4 * 1024 * 1024
 LAYER_LIMIT = 60 * 1024 * 1024
 TURN_BLOCKS = 16
+NEAR_GROUP = 4
 WEIGHT_GROUP = 8
 SHARE_GROUP = 2
 GATHER_STEP = 32
@@ -393,12 +394,10 @@
     extra = jnp.zeros((head_width, BLK), WIDE)
     for place, value in enumerate((from_src, from_dst, bias_ref[...])):
         extra = jnp.where(lanes == place, jnp.sum(value, axis=1, keepdims=True), extra)
-    peers = shares_ref.shape[0]
-    each = head_width // peers
-    shares_ref[...] = jnp.zeros(shares_ref.shape, WIDE)
-    for peer in range(peers):
-        shares_ref[peer, :each, :] = grad_weight[peer * each : (peer + 1) * each]
-        shares_ref[peer, each : 2 * each, :] = extra[peer * each : (peer + 1) * each]
+    extra = jnp.concatenate([extra, jnp.zeros((BLK - head_width, BLK), WIDE)], 0).T
+    for copy in range(shares_ref.shape[0]):
+        shares_ref[copy, :head_width, :] = grad_weight
+        shares_ref[copy, head_width:, :] = extra[:SUB]
     store.wait()
 
 
@@ -414,21 +413,17 @@
     out_ref[...] = sums_ref[0]
 
 
-def last_kernel(me_ref, parts_ref, kept_ref, weight_ref, attention_ref, bias_ref, extra_ref):
-    peers = parts_ref.shape[0]
+def last_kernel(place_ref, parts_ref, kept_ref, weight_ref, attention_ref, bias_ref):
+    kept = kept_ref[...]
+    total = None
+    for part in range(parts_ref.shape[0]):
+        value = jnp.where(place_ref[0] == part, kept, parts_ref[part])
+        total = value if total is None else total + value
     head_width = weight_ref.shape[0]
-    each = head_width // peers
-    extra_ref[...] = jnp.zeros(extra_ref.shape, WIDE)
-    for peer in range(peers):
-        weight_ref[peer * each : (peer + 1) * each, :] = parts_ref[peer, :each]
-        extra_ref[peer * each : (peer + 1) * each, :] = parts_ref[peer, each : 2 * each]
-    mine = pl.ds(me_ref[0] * each, each)
-    weight_ref[mine, :] = kept_ref[:each]
-    extra_ref[mine, :] = kept_ref[each : 2 * each]
-    turned = extra_ref[...].T
-    attention_ref[0] = turned[0:1, :head_width]
-    attention_ref[1] = turned[1:2, :head_width]
-    bias_ref[...] = turned[2:3, :head_width]
+    weight_ref[...] = total[:head_width]
+    attention_ref[0] = total[head_width : head_width + 1, :head_width]
+    attention_ref[1] = total[head_width + 1 : head_width + 2, :head_width]
+    bias_ref[...] = total[head_width + 2 : head_width + 3, :head_width]
 
 
 def vmem():
@@ -487,7 +482,6 @@
     incoming, pairs, weight = operands[:3]
     streamed = operands[5:]
     halo, cotangent = streamed[0], streamed[4]
-    peer_count = incoming.shape[0]
     in_width = halo.shape[1]
     head_width, node_count = cotangent.shape
     block_count = node_count // BLK
@@ -496,7 +490,7 @@
         layer_kernel,
         out_shape=(
             jax.ShapeDtypeStruct((block_count, head_width, BLK), LOW),
-            jax.ShapeDtypeStruct((peer_count, SUB, in_width), WIDE),
+            jax.ShapeDtypeStruct((NEAR_GROUP, head_width + SUB, in_width), WIDE),
         ),
         in_specs=[smem()] * 2 + [vmem()] * 3 + [anywhere()] * len(streamed),
         out_specs=(anywhere(), vmem()),
@@ -570,11 +564,13 @@
         band,
         features,
     )
+    near = [list(range(base, base + NEAR_GROUP)) for base in range(0, peer_count, NEAR_GROUP)]
+    far = [list(range(base, peer_count, NEAR_GROUP)) for base in range(NEAR_GROUP)]
     output = output_blocks.transpose(1, 0, 2).reshape(head_width, node_count)
-    partial_sums, output = lax.optimization_barrier((exchange(shares), output))
-    chunk_sums = pl.pallas_call(
+    partial_sums, output = lax.optimization_barrier((exchange(shares, near), output))
+    group_sums = pl.pallas_call(
         relay_kernel,
-        out_shape=jax.ShapeDtypeStruct(shares.shape, WIDE),
+        out_shape=jax.ShapeDtypeStruct((peer_count // NEAR_GROUP,) + shares.shape[1:], WIDE),
         in_specs=[vmem()],
         out_specs=vmem(),
         compiler_params=pltpu.CompilerParams(vmem_limit_bytes=SMALL_LIMIT),
@@ -587,7 +583,7 @@
         out_specs=vmem(),
         compiler_params=pltpu.CompilerParams(vmem_limit_bytes=SMALL_LIMIT),
         name="keep_own",
-    )(chunk_sums)
+    )(group_sums)
     grad_weight, grad_attention, grad_bias = pl.pallas_call(
         last_kernel,
         out_shape=(
@@ -597,15 +593,14 @@
         ),
         in_specs=[smem(), vmem(), vmem()],
         out_specs=(vmem(), vmem(), vmem()),
-        scratch_shapes=[pltpu.VMEM((in_width, in_width), WIDE)],
         compiler_params=pltpu.CompilerParams(vmem_limit_bytes=SMALL_LIMIT),
         name="last_sums",
-    )(me[None], exchange(chunk_sums), kept)
+    )(me[None] // NEAR_GROUP, exchange(group_sums, far), kept)
     return output, grad_weight.T, grad_attention, grad_bias[0]
 
 
-def exchange(values):
-    return lax.all_to_all(values, "dom", 0, 0, tiled=True)
+def exchange(values, groups):
+    return lax.all_to_all(values, "dom", 0, 0, tiled=True, axis_index_groups=groups)
 
 
 def solution(mesh):

time: 95.1 us -> 91.4 us (0.961); the launches traced: 94.7 us -> 89.7 us
  waiting for transfers between devices: 20.4 us -> 15.9 us
    all_to_all x2, waiting for transfers between devices: 12.4 us -> 7.79 us  [exchange(): lax.all_to_all(values, 'dom', 0, 0, tiled=True, axis_index_groups=groups)]
  transfers between devices with their start and end apart: 3 -> 3, of which waited for: 3 -> 3; matrix products, arithmetic and copies ran while one was open for 7% -> 8% of each run, Pallas kernels for 18% -> 19%
where the time goes in v6:
time: 91.4 us; the launch traced here: 89.7 us
  Pallas kernels  46 us (50%)
  starting transfers between devices  17.8 us (19%)
  waiting for transfers between devices  15.9 us (17%)
  local copies, waits for them, and re-layouts  9.19 us (10%)
    pallas_call x1, Pallas kernels, attention_layer(): pl.pallas_call(layer_kernel, out_shape=(jax.ShapeDtypeStruct((block_count...  19.4 us
    pallas_call x1, Pallas kernels, own_part(): pl.pallas_call(own_kernel, out_shape=(jax.ShapeDtypeStruct((block_count,...  15.7 us
    all_to_all x1, starting transfers between devices, per_device(): lax.all_to_all(outgoing.reshape(peer_count, capacity, in_width), 'dom', 0...  10.2 us
    pallas_call x1, Pallas kernels, gather_rows(): pl.pallas_call(gather_kernel, out_shape=jax.ShapeDtypeStruct((slots, in_w...  8.56 us
    all_to_all x1, waiting for transfers between devices, per_device(): lax.all_to_all(outgoing.reshape(peer_count, capacity, in_width), 'dom', 0...  8.14 us
    all_to_all x2, waiting for transfers between devices, exchange(): lax.all_to_all(values, 'dom', 0, 0, tiled=True, axis_index_groups=groups)  7.79 us
    all_to_all x2, starting transfers between devices, exchange(): lax.all_to_all(values, 'dom', 0, 0, tiled=True, axis_index_groups=groups)  7.6 us
    unnamed x22, local copies, waits for them, and re-layouts  4.66 us
  transfers between devices with their start and end apart: 3, of which 3 were waited for; matrix products, arithmetic and copies ran while one was open for 8% of the time, Pallas kernels for 19%

profile of v6, /device:TPU:1, one launch (start us, length us, event | category | flops | bytes accessed | tf_op | source)
XLA Modules:
  0.0 89.7 jit_solution(2746590966744142337)
XLA Ops:
  0.6 0.0 copy-start
  0.7 0.8 copy.26
  1.4 0.0 copy-done
  1.5 0.0 copy-start.1
  1.5 1.6 %copy-done.1 = bf16[8192,128]{1,0:T(8,128)(2,1)S(1)} copy-done((bf16[8192,128]{1,0:T(8,128)(2,1)S(1)}, bf16[8192,128]{1,0:T(8,128)(2,1)}, u32[]{:S(2)}) %copy-start.1) | copy-done | bytes 2097176
  3.1 8.6 %gather_rows.1 = bf16[8192,128]{1,0:T(8,128)(2,1)} custom-call(s32[8192]{0:T(1024)S(1)} %bitcast.17, s32[32]{0:T(128)S(1)} %dynamic-slice_bitcast_fusion.live_ref, bf16[8192,128]{1,0:T(8,128)(2,1)S(1)} %copy-done.1), custom_call_target="tpu_custom_call" | custom-call | tf_op jit(solution)/shard_map/gather_rows/pallas_call | solution.py:444
  11.6 0.0 copy-start.2
  11.6 0.0 copy-start.7
  11.7 0.0 copy-start.8
  11.7 10.2 %all-to-all-start = ((bf16[32,256,128]{2,1,0:T(8,128)(2,1)}), bf16[32,256,128]{2,1,0:T(8,128)(2,1)}, u32[]{:S(2)}, u32[]{:S(2)}) async-start(bf16[32,256,128]{2,1,0:T(8,128)(2,1)} %bitcast.3), calls=%async_computation | async-start | bytes 4194304 | tf_op jit(solution)/shard_map/all_to_all | solution.py:541
  21.9 0.0 copy-done.5
  21.9 0.0 copy-done.6
  21.9 0.1 copy.19
  22.0 0.7 reshape.28.pairs_ref
  22.7 0.7 copy.21.weight_ref
  23.4 0.7 copy.23.remote_counts_hbm
  24.1 0.0 copy-done.2
  24.1 0.8 copy.22.local_counts_hbm
  24.9 0.7 dynamic-slice_reduce_fusion.incoming_ref
  25.6 0.0 copy-done.7
  25.6 0.7 broadcast_in_dim.13.consts_ref
  26.4 15.7 %own_part.1 = (bf16[64,64,128]{2,1,0:T(8,128)(2,1)}, f32[64,8,128]{2,1,0:T(8,128)}, f32[64,8,128]{2,1,0:T(8,128)}, f32[64,5,8,128]{3,2,1,0:T(8,128)}, f32[64,128]{1,0:T(8,128)}) custom-call(s32[512]{0:T(512)} %reshape.28.pairs_ref, bf16[8192,128]{1,0:T(8,128)(2,1)} %own_hbm.1, bf16[128,64]{1,0:T(8,128)(2,1)} %copy.21.weight_ref, ...), custom_call_target="tpu_custom_call" | custom-call | flops 10000000000 | bytes 8000000 | tf_op jit(solution)/shard_map/own_part/pallas_call | solution.py:463
  42.1 8.1 %all-to-all-done = bf16[32,256,128]{2,1,0:T(8,128)(2,1)} async-done(((bf16[32,256,128]{2,1,0:T(8,128)(2,1)}), bf16[32,256,128]{2,1,0:T(8,128)(2,1)}, u32[]{:S(2)}, u32[]{:S(2)}) %all-to-all-start) | async-done | bytes 2097184 | tf_op jit(solution)/shard_map/all_to_all | solution.py:541
  50.2 19.4 %attention_layer.1 = (bf16[64,64,128]{2,1,0:T(8,128)(2,1)}, f32[4,72,128]{2,1,0:T(8,128)}) custom-call(s32[32]{0:T(128)} %dynamic-slice_reduce_fusion.incoming_ref, s32[512]{0:T(512)} %reshape.28.pairs_ref, bf16[128,64]{1,0:T(8,128)(2,1)} %copy.21.weight_ref, f32[3,64,128]{2,1,0:T(8,128)} %broadcast_in_dim.13.consts_ref, ...), custom_call_target="tpu_custom_call" | custom-call | flops 10000000000 | bytes 10000000 | tf_op jit(solution)/shard_map/attention_layer/pallas_call | solution.py:489
  69.6 4.2 %all-to-all-start.1 = ((f32[4,72,128]{2,1,0:T(8,128)}), f32[4,72,128]{2,1,0:T(8,128)S(1)}, u32[]{:S(2)}, u32[]{:S(2)}) async-start(f32[4,72,128]{2,1,0:T(8,128)} %get-tuple-element.21), calls=%async_computation.1 | async-start | bytes 294912 | tf_op jit(solution)/shard_map/all_to_all | solution.py:603
  73.8 2.3 %copy_bitcast_fusion = bf16[64,8192]{1,0:T(8,128)(2,1)} fusion(bf16[64,64,128]{2,1,0:T(8,128)(2,1)} %get-tuple-element.22), kind=kLoop, calls=%fused_computation | loop fusion | bytes 2097152 | tf_op jit(solution)/shard_map/reshape | solution.py:569
  76.1 1.4 %all-to-all-done.1.parts_ref = f32[4,72,128]{2,1,0:T(8,128)S(1)} async-done(((f32[4,72,128]{2,1,0:T(8,128)}), f32[4,72,128]{2,1,0:T(8,128)S(1)}, u32[]{:S(2)}, u32[]{:S(2)}) %all-to-all-start.1) | async-done | bytes 147488 | tf_op jit(solution)/shard_map/all_to_all | solution.py:603
  77.5 0.7 relay_sums.1.sums_ref
  78.3 3.4 %all-to-all-start.2 = ((f32[8,72,128]{2,1,0:T(8,128)}), f32[8,72,128]{2,1,0:T(8,128)S(1)}, u32[]{:S(2)}, u32[]{:S(2)}) async-start(f32[8,72,128]{2,1,0:T(8,128)} %relay_sums.1.sums_ref), calls=%async_computation.2 | async-start | bytes 589824 | tf_op jit(solution)/shard_map/all_to_all | solution.py:603
  81.7 1.0 %keep_own.1.kept_ref = f32[72,128]{1,0:T(8,128)S(1)} custom-call(f32[8,72,128]{2,1,0:T(8,128)} %relay_sums.1.sums_ref), custom_call_target="tpu_custom_call" | custom-call | tf_op jit(solution)/shard_map/keep_own/pallas_call | solution.py:579
  82.7 6.4 %all-to-all-done.2.parts_ref = f32[8,72,128]{2,1,0:T(8,128)S(1)} async-done(((f32[8,72,128]{2,1,0:T(8,128)}), f32[8,72,128]{2,1,0:T(8,128)S(1)}, u32[]{:S(2)}, u32[]{:S(2)}) %all-to-all-start.2) | async-done | bytes 294944 | tf_op jit(solution)/shard_map/all_to_all | solution.py:603
  89.1 0.6 last_sums.1
  (10 shorter events, 0.0 us)
Async XLA Ops:
  0.6 0.8 copy-start
  1.5 1.6 %copy-start.1 = (bf16[8192,128]{1,0:T(8,128)(2,1)S(1)}, bf16[8192,128]{1,0:T(8,128)(2,1)}, u32[]{:S(2)}) copy-start(bf16[8192,128]{1,0:T(8,128)(2,1)} %own_hbm.1) | copy-start | bytes 6291460
  11.6 10.2 %copy-start.5 = (s32[64,5]{0,1:T(8,128)S(1)}, s32[64,5]{0,1:T(8,128)}, u32[]{:S(2)}) copy-start(s32[64,5]{0,1:T(8,128)} %param.16) | copy-start | bytes 3844
  11.6 10.3 %copy-start.6 = (s32[64,3]{0,1:T(4,128)S(1)}, s32[64,3]{0,1:T(4,128)}, u32[]{:S(2)}) copy-start(s32[64,3]{0,1:T(4,128)} %param.18) | copy-start | bytes 2308
  11.6 11.0 %copy-start.4 = (bf16[128,64]{0,1:T(8,128)(2,1)S(1)}, bf16[128,64]{0,1:T(8,128)(2,1)}, u32[]{:S(2)}) copy-start(bf16[128,64]{0,1:T(8,128)(2,1)} %param.12) | copy-start | bytes 49156
  11.6 11.8 %copy-start.3 = (s32[64,3,128]{2,0,1:T(8,128)S(1)}, s32[64,3,128]{2,0,1:T(8,128)}, u32[]{:S(2)}) copy-start(s32[64,3,128]{2,0,1:T(8,128)} %param.19) | copy-start | bytes 294916
  11.6 12.5 %copy-start.2 = (s32[64,5,128]{2,0,1:T(8,128)S(1)}, s32[64,5,128]{2,0,1:T(8,128)}, u32[]{:S(2)}) copy-start(s32[64,5,128]{2,0,1:T(8,128)} %param.17) | copy-start | bytes 491524
  11.6 14.0 %copy-start.7 = (f32[2,1,64]{2,1,0:T(1,128)S(1)}, f32[2,1,64]{2,1,0:T(1,128)}, u32[]{:S(2)}) copy-start(f32[2,1,64]{2,1,0:T(1,128)} %param.13) | copy-start | bytes 1540
  11.7 14.0 %copy-start.8 = (f32[64]{0:T(128)S(1)}, f32[64]{0:T(128)}, u32[]{:S(2)}) copy-start(f32[64]{0:T(128)} %param.14) | copy-start | bytes 772
  11.7 38.5 %all-to-all-start = ((bf16[32,256,128]{2,1,0:T(8,128)(2,1)}), bf16[32,256,128]{2,1,0:T(8,128)(2,1)}, u32[]{:S(2)}, u32[]{:S(2)}) async-start(bf16[32,256,128]{2,1,0:T(8,128)(2,1)} %bitcast.3), calls=%async_computation | async-start | bytes 4194304 | tf_op jit(solution)/shard_map/all_to_all | solution.py:541
  69.6 7.9 %all-to-all-start.1 = ((f32[4,72,128]{2,1,0:T(8,128)}), f32[4,72,128]{2,1,0:T(8,128)S(1)}, u32[]{:S(2)}, u32[]{:S(2)}) async-start(f32[4,72,128]{2,1,0:T(8,128)} %get-tuple-element.21), calls=%async_computation.1 | async-start | bytes 294912 | tf_op jit(solution)/shard_map/all_to_all | solution.py:603
  78.3 10.8 %all-to-all-start.2 = ((f32[8,72,128]{2,1,0:T(8,128)}), f32[8,72,128]{2,1,0:T(8,128)S(1)}, u32[]{:S(2)}, u32[]{:S(2)}) async-start(f32[8,72,128]{2,1,0:T(8,128)} %relay_sums.1.sums_ref), calls=%async_computation.2 | async-start | bytes 589824 | tf_op jit(solution)/shard_map/all_to_all | solution.py:603

commit v7 on v6

--- a/solution.py
+++ b/solution.py
@@ -16,12 +16,16 @@
 LAYER_LIMIT = 60 * 1024 * 1024
 TURN_BLOCKS = 16
 NEAR_GROUP = 4
+FAR_GROUP = 8
+GATHER_PARTS = 4
 WEIGHT_GROUP = 8
 SHARE_GROUP = 2
 GATHER_STEP = 32
 
 
-def gather_kernel(rows_ref, live_ref, features_ref, out_ref, wide_ref, stage_ref):
+def gather_kernel(
+    rows_ref, live_ref, features_hbm, out_hbm, features_ref, wide_ref, stage_ref, in_sem, out_sem
+):
     node_count = features_ref.shape[0]
     peer_count = live_ref.shape[0]
     capacity = rows_ref.shape[0] // peer_count
@@ -32,7 +36,18 @@
         wide_ref[pl.ds(lead, BLK), :] = features_ref[pl.ds(lead, BLK), :].astype(WIDE)
         return carry
 
-    lax.fori_loop(0, node_count // BLK, widen, 0, unroll=4)
+    part_nodes = node_count // GATHER_PARTS
+    fetches = []
+    for part in range(GATHER_PARTS):
+        nodes = pl.ds(part * part_nodes, part_nodes)
+        fetches.append(
+            pltpu.make_async_copy(features_hbm.at[nodes], features_ref.at[nodes], in_sem.at[part])
+        )
+        fetches[part].start()
+    blocks = part_nodes // BLK
+    for part in range(GATHER_PARTS):
+        fetches[part].wait()
+        lax.fori_loop(part * blocks, (part + 1) * blocks, widen, 0, unroll=4)
 
     def one_peer(peer, carry):
         busy = (live_ref[peer] + GATHER_STEP - 1) // GATHER_STEP
@@ -53,14 +68,25 @@
         lax.fori_loop(busy, step_count, blank, 0)
         return carry
 
-    lax.fori_loop(0, peer_count, one_peer, 0)
-
     def narrow(turn, carry):
         lead = pl.multiple_of(turn * BLK, BLK)
-        out_ref[pl.ds(lead, BLK), :] = stage_ref[pl.ds(lead, BLK), :].astype(LOW)
+        features_ref[pl.ds(lead, BLK), :] = stage_ref[pl.ds(lead, BLK), :].astype(LOW)
         return carry
 
-    lax.fori_loop(0, peer_count * capacity // BLK, narrow, 0, unroll=4)
+    part_peers = peer_count // GATHER_PARTS
+    part_slots = part_peers * capacity
+    stores = []
+    for part in range(GATHER_PARTS):
+        lax.fori_loop(part * part_peers, (part + 1) * part_peers, one_peer, 0)
+        blocks = part_slots // BLK
+        lax.fori_loop(part * blocks, (part + 1) * blocks, narrow, 0, unroll=4)
+        slots = pl.ds(part * part_slots, part_slots)
+        stores.append(
+            pltpu.make_async_copy(features_ref.at[slots], out_hbm.at[slots], out_sem.at[part])
+        )
+        stores[part].start()
+    for store in stores:
+        store.wait()
 
 
 def spread(row):
@@ -444,13 +470,16 @@
     return pl.pallas_call(
         gather_kernel,
         out_shape=jax.ShapeDtypeStruct((slots, in_width), LOW),
-        in_specs=[smem(), smem(), vmem()],
-        out_specs=vmem(),
+        in_specs=[smem(), smem(), anywhere()],
+        out_specs=anywhere(),
         scratch_shapes=[
+            pltpu.VMEM((max(node_count, slots), in_width), LOW),
             pltpu.VMEM((node_count, in_width), WIDE),
             pltpu.VMEM((slots, in_width), WIDE),
+            pltpu.SemaphoreType.DMA((GATHER_PARTS,)),
+            pltpu.SemaphoreType.DMA((GATHER_PARTS,)),
         ],
-        compiler_params=pltpu.CompilerParams(vmem_limit_bytes=VMEM_LIMIT),
+        compiler_params=pltpu.CompilerParams(vmem_limit_bytes=LAYER_LIMIT),
         name="gather_rows",
     )(rows, live, features)
 
@@ -490,7 +519,7 @@
         layer_kernel,
         out_shape=(
             jax.ShapeDtypeStruct((block_count, head_width, BLK), LOW),
-            jax.ShapeDtypeStruct((NEAR_GROUP, head_width + SUB, in_width), WIDE),
+            jax.ShapeDtypeStruct((FAR_GROUP, head_width + SUB, in_width), WIDE),
         ),
         in_specs=[smem()] * 2 + [vmem()] * 3 + [anywhere()] * len(streamed),
         out_specs=(anywhere(), vmem()),
@@ -567,10 +596,10 @@
     near = [list(range(base, base + NEAR_GROUP)) for base in range(0, peer_count, NEAR_GROUP)]
     far = [list(range(base, peer_count, NEAR_GROUP)) for base in range(NEAR_GROUP)]
     output = output_blocks.transpose(1, 0, 2).reshape(head_width, node_count)
-    partial_sums, output = lax.optimization_barrier((exchange(shares, near), output))
+    partial_sums, output = lax.optimization_barrier((exchange(shares, far), output))
     group_sums = pl.pallas_call(
         relay_kernel,
-        out_shape=jax.ShapeDtypeStruct((peer_count // NEAR_GROUP,) + shares.shape[1:], WIDE),
+        out_shape=jax.ShapeDtypeStruct((NEAR_GROUP,) + shares.shape[1:], WIDE),
         in_specs=[vmem()],
         out_specs=vmem(),
         compiler_params=pltpu.CompilerParams(vmem_limit_bytes=SMALL_LIMIT),
@@ -595,7 +624,7 @@
         out_specs=(vmem(), vmem(), vmem()),
         compiler_params=pltpu.CompilerParams(vmem_limit_bytes=SMALL_LIMIT),
         name="last_sums",
-    )(me[None] // NEAR_GROUP, exchange(group_sums, far), kept)
+    )(me[None] % NEAR_GROUP, exchange(group_sums, near), kept)
     return output, grad_weight.T, grad_attention, grad_bias[0]
 
 

time: 91.4 us -> 92.2 us (level); the launches traced: 89.7 us -> 91.8 us
  starting transfers between devices: 17.8 us -> 19.7 us
    all_to_all x2, starting transfers between devices: 7.6 us -> 9.09 us  [exchange(): lax.all_to_all(values, 'dom', 0, 0, tiled=True, axis_index_groups=groups)]
    unnamed x22 -> x20, local copies, waits for them, and re-layouts: 4.66 us -> 3.69 us
  transfers between devices with their start and end apart: 3 -> 3, of which waited for: 3 -> 3; matrix products, arithmetic and copies ran while one was open for 8% -> 7% of each run, Pallas kernels for 19% -> 18%
where the time goes in v7:
time: 92.2 us; the launch traced here: 91.8 us
  Pallas kernels  46.7 us (51%)
  starting transfers between devices  19.7 us (21%)
  waiting for transfers between devices  15.9 us (17%)
  local copies, waits for them, and re-layouts  8.71 us (9%)
    pallas_call x1, Pallas kernels, attention_layer(): pl.pallas_call(layer_kernel, out_shape=(jax.ShapeDtypeStruct((block_count...  19.5 us
    pallas_call x1, Pallas kernels, own_part(): pl.pallas_call(own_kernel, out_shape=(jax.ShapeDtypeStruct((block_count,...  15.8 us
    all_to_all x1, starting transfers between devices, per_device(): lax.all_to_all(outgoing.reshape(peer_count, capacity, in_width), 'dom', 0...  10.6 us
    pallas_call x1, Pallas kernels, gather_rows(): pl.pallas_call(gather_kernel, out_shape=jax.ShapeDtypeStruct((slots, in_w...  9.18 us
    all_to_all x2, starting transfers between devices, exchange(): lax.all_to_all(values, 'dom', 0, 0, tiled=True, axis_index_groups=groups)  9.09 us
    all_to_all x1, waiting for transfers between devices, per_device(): lax.all_to_all(outgoing.reshape(peer_count, capacity, in_width), 'dom', 0...  8.05 us
    all_to_all x2, waiting for transfers between devices, exchange(): lax.all_to_all(values, 'dom', 0, 0, tiled=True, axis_index_groups=groups)  7.86 us
    unnamed x20, local copies, waits for them, and re-layouts  3.69 us
  transfers between devices with their start and end apart: 3, of which 3 were waited for; matrix products, arithmetic and copies ran while one was open for 7% of the time, Pallas kernels for 18%

profile of v7, /device:TPU:1, one launch (start us, length us, event | category | flops | bytes accessed | tf_op | source)
XLA Modules:
  0.0 91.8 jit_solution(543712761581880364)
XLA Ops:
  0.6 0.0 copy-start
  0.7 1.4 %copy.26 = s32[4,2,8,128]{3,1,2,0:T(2,128)} copy(s32[4,2,8,128]{3,2,1,0:T(8,128)} %bitcast.19) | data formatting | bytes 65536
  2.0 0.0 copy-done
  2.0 0.5 dynamic-slice_bitcast_fusion.live_ref
  2.6 9.2 %gather_rows.1 = bf16[8192,128]{1,0:T(8,128)(2,1)} custom-call(s32[8192]{0:T(1024)} %bitcast.18, s32[32]{0:T(128)} %dynamic-slice_bitcast_fusion.live_ref, bf16[8192,128]{1,0:T(8,128)(2,1)} %own_hbm.1), custom_call_target="tpu_custom_call" | custom-call | tf_op jit(solution)/shard_map/gather_rows/pallas_call | solution.py:470
  11.7 0.0 copy-start.4
  11.8 0.0 copy-start.5
  11.8 0.0 copy-start.3
  11.8 0.0 copy-start.2
  11.8 0.0 copy-start.1
  11.8 0.0 copy-start.6
  11.8 0.0 copy-start.7
  11.8 10.6 %all-to-all-start = ((bf16[32,256,128]{2,1,0:T(8,128)(2,1)}), bf16[32,256,128]{2,1,0:T(8,128)(2,1)}, u32[]{:S(2)}, u32[]{:S(2)}) async-start(bf16[32,256,128]{2,1,0:T(8,128)(2,1)} %bitcast.17), calls=%async_computation | async-start | bytes 4194304 | tf_op jit(solution)/shard_map/all_to_all | solution.py:570
  22.5 0.1 copy.19
  22.6 0.7 reshape.26.pairs_ref
  23.2 0.7 copy.21.weight_ref
  24.0 0.7 copy.23.remote_counts_hbm
  24.7 0.0 copy-done.1
  24.7 0.8 copy.22.local_counts_hbm
  25.5 0.7 dynamic-slice_reduce_fusion.incoming_ref
  26.2 0.7 broadcast_in_dim.13.consts_ref
  26.9 15.8 %own_part.1 = (bf16[64,64,128]{2,1,0:T(8,128)(2,1)}, f32[64,8,128]{2,1,0:T(8,128)}, f32[64,8,128]{2,1,0:T(8,128)}, f32[64,5,8,128]{3,2,1,0:T(8,128)}, f32[64,128]{1,0:T(8,128)}) custom-call(s32[512]{0:T(512)} %reshape.26.pairs_ref, bf16[8192,128]{1,0:T(8,128)(2,1)} %own_hbm.1, bf16[128,64]{1,0:T(8,128)(2,1)} %copy.21.weight_ref, ...), custom_call_target="tpu_custom_call" | custom-call | flops 10000000000 | bytes 8000000 | tf_op jit(solution)/shard_map/own_part/pallas_call | solution.py:492
  42.7 8.1 %all-to-all-done = bf16[32,256,128]{2,1,0:T(8,128)(2,1)} async-done(((bf16[32,256,128]{2,1,0:T(8,128)(2,1)}), bf16[32,256,128]{2,1,0:T(8,128)(2,1)}, u32[]{:S(2)}, u32[]{:S(2)}) %all-to-all-start) | async-done | bytes 2097184 | tf_op jit(solution)/shard_map/all_to_all | solution.py:570
  50.8 19.5 %attention_layer.1 = (bf16[64,64,128]{2,1,0:T(8,128)(2,1)}, f32[8,72,128]{2,1,0:T(8,128)}) custom-call(s32[32]{0:T(128)} %dynamic-slice_reduce_fusion.incoming_ref, s32[512]{0:T(512)} %reshape.26.pairs_ref, bf16[128,64]{1,0:T(8,128)(2,1)} %copy.21.weight_ref, f32[3,64,128]{2,1,0:T(8,128)} %broadcast_in_dim.13.consts_ref, ...), custom_call_target="tpu_custom_call" | custom-call | flops 10000000000 | bytes 10000000 | tf_op jit(solution)/shard_map/attention_layer/pallas_call | solution.py:518
  70.3 3.4 %all-to-all-start.1 = ((f32[8,72,128]{2,1,0:T(8,128)}), f32[8,72,128]{2,1,0:T(8,128)S(1)}, u32[]{:S(2)}, u32[]{:S(2)}) async-start(f32[8,72,128]{2,1,0:T(8,128)} %get-tuple-element.21), calls=%async_computation.1 | async-start | bytes 589824 | tf_op jit(solution)/shard_map/all_to_all | solution.py:632
  73.7 2.3 %copy_bitcast_fusion = bf16[64,8192]{1,0:T(8,128)(2,1)} fusion(bf16[64,64,128]{2,1,0:T(8,128)(2,1)} %get-tuple-element.22), kind=kLoop, calls=%fused_computation | loop fusion | bytes 2097152 | tf_op jit(solution)/shard_map/reshape | solution.py:598
  76.0 5.1 %all-to-all-done.1.parts_ref = f32[8,72,128]{2,1,0:T(8,128)S(1)} async-done(((f32[8,72,128]{2,1,0:T(8,128)}), f32[8,72,128]{2,1,0:T(8,128)S(1)}, u32[]{:S(2)}, u32[]{:S(2)}) %all-to-all-start.1) | async-done | bytes 294944 | tf_op jit(solution)/shard_map/all_to_all | solution.py:632
  81.1 0.7 relay_sums.1.sums_ref
  81.8 5.7 %all-to-all-start.2 = ((f32[4,72,128]{2,1,0:T(8,128)}), f32[4,72,128]{2,1,0:T(8,128)S(1)}, u32[]{:S(2)}, u32[]{:S(2)}) async-start(f32[4,72,128]{2,1,0:T(8,128)} %relay_sums.1.sums_ref), calls=%async_computation.2 | async-start | bytes 294912 | tf_op jit(solution)/shard_map/all_to_all | solution.py:632
  87.4 0.9 %keep_own.1.kept_ref = f32[72,128]{1,0:T(8,128)S(1)} custom-call(f32[4,72,128]{2,1,0:T(8,128)} %relay_sums.1.sums_ref), custom_call_target="tpu_custom_call" | custom-call | tf_op jit(solution)/shard_map/keep_own/pallas_call | solution.py:608
  88.4 2.8 %all-to-all-done.2.parts_ref = f32[4,72,128]{2,1,0:T(8,128)S(1)} async-done(((f32[4,72,128]{2,1,0:T(8,128)}), f32[4,72,128]{2,1,0:T(8,128)S(1)}, u32[]{:S(2)}, u32[]{:S(2)}) %all-to-all-start.2) | async-done | bytes 147488 | tf_op jit(solution)/shard_map/all_to_all | solution.py:632
  91.2 0.6 last_sums.1
  (8 shorter events, 0.0 us)
Async XLA Ops:
  0.6 1.4 %copy-start = (s32[32,32]{1,0:T(8,128)S(1)}, s32[32,32]{1,0:T(8,128)}, u32[]{:S(2)}) copy-start(s32[32,32]{1,0:T(8,128)} %param.21) | copy-start | bytes 12292
  11.7 10.7 %copy-start.4 = (s32[64,5]{0,1:T(8,128)S(1)}, s32[64,5]{0,1:T(8,128)}, u32[]{:S(2)}) copy-start(s32[64,5]{0,1:T(8,128)} %param.16) | copy-start | bytes 3844
  11.8 10.7 %copy-start.5 = (s32[64,3]{0,1:T(4,128)S(1)}, s32[64,3]{0,1:T(4,128)}, u32[]{:S(2)}) copy-start(s32[64,3]{0,1:T(4,128)} %param.18) | copy-start | bytes 2308
  11.8 11.5 %copy-start.3 = (bf16[128,64]{0,1:T(8,128)(2,1)S(1)}, bf16[128,64]{0,1:T(8,128)(2,1)}, u32[]{:S(2)}) copy-start(bf16[128,64]{0,1:T(8,128)(2,1)} %param.12) | copy-start | bytes 49156
  11.8 12.2 %copy-start.2 = (s32[64,3,128]{2,0,1:T(8,128)S(1)}, s32[64,3,128]{2,0,1:T(8,128)}, u32[]{:S(2)}) copy-start(s32[64,3,128]{2,0,1:T(8,128)} %param.19) | copy-start | bytes 294916
  11.8 12.9 %copy-start.1 = (s32[64,5,128]{2,0,1:T(8,128)S(1)}, s32[64,5,128]{2,0,1:T(8,128)}, u32[]{:S(2)}) copy-start(s32[64,5,128]{2,0,1:T(8,128)} %param.17) | copy-start | bytes 491524
  11.8 14.4 %copy-start.6 = (f32[2,1,64]{2,1,0:T(1,128)S(1)}, f32[2,1,64]{2,1,0:T(1,128)}, u32[]{:S(2)}) copy-start(f32[2,1,64]{2,1,0:T(1,128)} %param.13) | copy-start | bytes 1540
  11.8 14.4 %copy-start.7 = (f32[64]{0:T(128)S(1)}, f32[64]{0:T(128)}, u32[]{:S(2)}) copy-start(f32[64]{0:T(128)} %param.14) | copy-start | bytes 772
  11.8 39.0 %all-to-all-start = ((bf16[32,256,128]{2,1,0:T(8,128)(2,1)}), bf16[32,256,128]{2,1,0:T(8,128)(2,1)}, u32[]{:S(2)}, u32[]{:S(2)}) async-start(bf16[32,256,128]{2,1,0:T(8,128)(2,1)} %bitcast.17), calls=%async_computation | async-start | bytes 4194304 | tf_op jit(solution)/shard_map/all_to_all | solution.py:570
  70.3 10.8 %all-to-all-start.1 = ((f32[8,72,128]{2,1,0:T(8,128)}), f32[8,72,128]{2,1,0:T(8,128)S(1)}, u32[]{:S(2)}, u32[]{:S(2)}) async-start(f32[8,72,128]{2,1,0:T(8,128)} %get-tuple-element.21), calls=%async_computation.1 | async-start | bytes 589824 | tf_op jit(solution)/shard_map/all_to_all | solution.py:632
  81.8 9.4 %all-to-all-start.2 = ((f32[4,72,128]{2,1,0:T(8,128)}), f32[4,72,128]{2,1,0:T(8,128)S(1)}, u32[]{:S(2)}, u32[]{:S(2)}) async-start(f32[4,72,128]{2,1,0:T(8,128)} %relay_sums.1.sums_ref), calls=%async_computation.2 | async-start | bytes 294912 | tf_op jit(solution)/shard_map/all_to_all | solution.py:632

commit v8 on v6

--- a/solution.py
+++ b/solution.py
@@ -401,24 +401,24 @@
     store.wait()
 
 
-def relay_kernel(parts_ref, out_ref):
-    total = parts_ref[0]
-    for part in range(1, parts_ref.shape[0]):
-        total = total + parts_ref[part]
-    for copy in range(out_ref.shape[0]):
-        out_ref[copy] = total
-
-
-def keep_kernel(sums_ref, out_ref):
-    out_ref[...] = sums_ref[0]
-
-
-def last_kernel(place_ref, parts_ref, kept_ref, weight_ref, attention_ref, bias_ref):
+def relay_kernel(place_ref, parts_ref, kept_ref, out_ref):
     kept = kept_ref[...]
     total = None
     for part in range(parts_ref.shape[0]):
         value = jnp.where(place_ref[0] == part, kept, parts_ref[part])
         total = value if total is None else total + value
+    for copy in range(out_ref.shape[0]):
+        out_ref[copy] = total
+
+
+def keep_kernel(sums_ref, out_ref):
+    out_ref[...] = sums_ref[0]
+
+
+def last_kernel(parts_ref, weight_ref, attention_ref, bias_ref):
+    total = parts_ref[0]
+    for part in range(1, parts_ref.shape[0]):
+        total = total + parts_ref[part]
     head_width = weight_ref.shape[0]
     weight_ref[...] = total[:head_width]
     attention_ref[0] = total[head_width : head_width + 1, :head_width]
@@ -566,16 +566,6 @@
     )
     near = [list(range(base, base + NEAR_GROUP)) for base in range(0, peer_count, NEAR_GROUP)]
     far = [list(range(base, peer_count, NEAR_GROUP)) for base in range(NEAR_GROUP)]
-    output = output_blocks.transpose(1, 0, 2).reshape(head_width, node_count)
-    partial_sums, output = lax.optimization_barrier((exchange(shares, near), output))
-    group_sums = pl.pallas_call(
-        relay_kernel,
-        out_shape=jax.ShapeDtypeStruct((peer_count // NEAR_GROUP,) + shares.shape[1:], WIDE),
-        in_specs=[vmem()],
-        out_specs=vmem(),
-        compiler_params=pltpu.CompilerParams(vmem_limit_bytes=SMALL_LIMIT),
-        name="relay_sums",
-    )(partial_sums)
     kept = pl.pallas_call(
         keep_kernel,
         out_shape=jax.ShapeDtypeStruct(shares.shape[1:], WIDE),
@@ -583,7 +573,17 @@
         out_specs=vmem(),
         compiler_params=pltpu.CompilerParams(vmem_limit_bytes=SMALL_LIMIT),
         name="keep_own",
-    )(group_sums)
+    )(shares)
+    group_sums = pl.pallas_call(
+        relay_kernel,
+        out_shape=jax.ShapeDtypeStruct((peer_count // NEAR_GROUP,) + shares.shape[1:], WIDE),
+        in_specs=[smem(), vmem(), vmem()],
+        out_specs=vmem(),
+        compiler_params=pltpu.CompilerParams(vmem_limit_bytes=SMALL_LIMIT),
+        name="relay_sums",
+    )(me[None] % NEAR_GROUP, exchange(shares, near), kept)
+    group_sums, output_blocks = lax.optimization_barrier((group_sums, output_blocks))
+    output = output_blocks.transpose(1, 0, 2).reshape(head_width, node_count)
     grad_weight, grad_attention, grad_bias = pl.pallas_call(
         last_kernel,
         out_shape=(
@@ -591,11 +591,11 @@
             jax.ShapeDtypeStruct((2, 1, head_width), WIDE),
             jax.ShapeDtypeStruct((1, head_width), WIDE),
         ),
-        in_specs=[smem(), vmem(), vmem()],
+        in_specs=[vmem()],
         out_specs=(vmem(), vmem(), vmem()),
         compiler_params=pltpu.CompilerParams(vmem_limit_bytes=SMALL_LIMIT),
         name="last_sums",
-    )(me[None] // NEAR_GROUP, exchange(group_sums, far), kept)
+    )(exchange(group_sums, far))
     return output, grad_weight.T, grad_attention, grad_bias[0]
 
 

time: 91.4 us -> 91 us (level)
  starting transfers between devices: 17.8 us -> 16.7 us
  local copies, waits for them, and re-layouts: 9.19 us -> 10.2 us
    all_to_all x1, starting transfers between devices: 10.2 us -> 9.14 us  [per_device(): lax.all_to_all(outgoing.reshape(peer_count, capacity, in_width), 'dom', 0...]
    pallas_call x1, Pallas kernels: 1 us -> 0.01 us  [per_device(): pl.pallas_call(keep_kernel, out_shape=jax.ShapeDtypeStruct(shares.shape[1...]
    unnamed x22 -> x24, local copies, waits for them, and re-layouts: 4.66 us -> 5.61 us
  transfers between devices with their start and end apart: 3 -> 3, of which waited for: 3 -> 3; matrix products, arithmetic and copies ran while one was open for 8% -> 8% of each run, Pallas kernels for 19% -> 18%
where the time goes in v8:
time: 91 us; the launch traced here: 89.3 us
  Pallas kernels  45.7 us (50%)
  starting transfers between devices  16.7 us (18%)
  waiting for transfers between devices  16 us (18%)
  local copies, waits for them, and re-layouts  10.2 us (11%)
    pallas_call x1, Pallas kernels, attention_layer(): pl.pallas_call(layer_kernel, out_shape=(jax.ShapeDtypeStruct((block_count...  19.4 us
    pallas_call x1, Pallas kernels, own_part(): pl.pallas_call(own_kernel, out_shape=(jax.ShapeDtypeStruct((block_count,...  15.7 us
    pallas_call x1, Pallas kernels, gather_rows(): pl.pallas_call(gather_kernel, out_shape=jax.ShapeDtypeStruct((slots, in_w...  9.19 us
    all_to_all x1, starting transfers between devices, per_device(): lax.all_to_all(outgoing.reshape(peer_count, capacity, in_width), 'dom', 0...  9.14 us
    all_to_all x1, waiting for transfers between devices, per_device(): lax.all_to_all(outgoing.reshape(peer_count, capacity, in_width), 'dom', 0...  8.13 us
    all_to_all x2, waiting for transfers between devices, exchange(): lax.all_to_all(values, 'dom', 0, 0, tiled=True, axis_index_groups=groups)  7.86 us
    all_to_all x2, starting transfers between devices, exchange(): lax.all_to_all(values, 'dom', 0, 0, tiled=True, axis_index_groups=groups)  7.57 us
    unnamed x24, local copies, waits for them, and re-layouts  5.61 us
  transfers between devices with their start and end apart: 3, of which 3 were waited for; matrix products, arithmetic and copies ran while one was open for 8% of the time, Pallas kernels for 18%

profile of v8, /device:TPU:1, one launch (start us, length us, event | category | flops | bytes accessed | tf_op | source)
XLA Modules:
  0.0 89.3 jit_solution(8525790238941434824)
XLA Ops:
  0.6 0.0 copy-start
  0.7 0.8 copy.26
  1.4 0.0 copy-done
  1.5 0.0 copy-start.1
  1.5 1.6 %copy-done.1 = bf16[8192,128]{1,0:T(8,128)(2,1)S(1)} copy-done((bf16[8192,128]{1,0:T(8,128)(2,1)S(1)}, bf16[8192,128]{1,0:T(8,128)(2,1)}, u32[]{:S(2)}) %copy-start.1) | copy-done | bytes 2097176
  3.1 9.2 %gather_rows.1 = bf16[8192,128]{1,0:T(8,128)(2,1)} custom-call(s32[8192]{0:T(1024)S(1)} %bitcast.17, s32[32]{0:T(128)S(1)} %dynamic-slice_bitcast_fusion.live_ref, bf16[8192,128]{1,0:T(8,128)(2,1)S(1)} %copy-done.1), custom_call_target="tpu_custom_call" | custom-call | tf_op jit(solution)/shard_map/gather_rows/pallas_call | solution.py:444
  12.3 0.0 copy-start.3
  12.3 0.0 copy-start.8
  12.3 0.0 copy-start.9
  12.3 9.1 %all-to-all-start = ((bf16[32,256,128]{2,1,0:T(8,128)(2,1)}), bf16[32,256,128]{2,1,0:T(8,128)(2,1)}, u32[]{:S(2)}, u32[]{:S(2)}) async-start(bf16[32,256,128]{2,1,0:T(8,128)(2,1)} %bitcast.4), calls=%async_computation | async-start | bytes 4194304 | tf_op jit(solution)/shard_map/all_to_all | solution.py:541
  21.4 0.0 copy-done.6
  21.4 0.0 copy-done.7
  21.5 0.1 copy.19
  21.6 0.7 reshape.26.pairs_ref
  22.2 0.0 copy-done.5
  22.2 0.7 copy.21.weight_ref
  23.0 0.0 copy-done.4
  23.0 0.7 copy.23.remote_counts_hbm
  23.7 0.8 copy.22.local_counts_hbm
  24.5 0.7 dynamic-slice_reduce_fusion.incoming_ref
  25.2 0.7 broadcast_in_dim.14.consts_ref
  26.0 15.7 %own_part.1 = (bf16[64,64,128]{2,1,0:T(8,128)(2,1)}, f32[64,8,128]{2,1,0:T(8,128)}, f32[64,8,128]{2,1,0:T(8,128)}, f32[64,5,8,128]{3,2,1,0:T(8,128)}, f32[64,128]{1,0:T(8,128)}) custom-call(s32[512]{0:T(512)} %reshape.26.pairs_ref, bf16[8192,128]{1,0:T(8,128)(2,1)} %own_hbm.1, bf16[128,64]{1,0:T(8,128)(2,1)} %copy.21.weight_ref, ...), custom_call_target="tpu_custom_call" | custom-call | flops 10000000000 | bytes 8000000 | tf_op jit(solution)/shard_map/own_part/pallas_call | solution.py:463
  41.7 8.1 %all-to-all-done = bf16[32,256,128]{2,1,0:T(8,128)(2,1)} async-done(((bf16[32,256,128]{2,1,0:T(8,128)(2,1)}), bf16[32,256,128]{2,1,0:T(8,128)(2,1)}, u32[]{:S(2)}, u32[]{:S(2)}) %all-to-all-start) | async-done | bytes 2097184 | tf_op jit(solution)/shard_map/all_to_all | solution.py:541
  49.8 19.4 %attention_layer.1 = (bf16[64,64,128]{2,1,0:T(8,128)(2,1)}, f32[4,72,128]{2,1,0:T(8,128)}) custom-call(s32[32]{0:T(128)} %dynamic-slice_reduce_fusion.incoming_ref, s32[512]{0:T(512)} %reshape.26.pairs_ref, bf16[128,64]{1,0:T(8,128)(2,1)} %copy.21.weight_ref, f32[3,64,128]{2,1,0:T(8,128)} %broadcast_in_dim.14.consts_ref, ...), custom_call_target="tpu_custom_call" | custom-call | flops 10000000000 | bytes 10000000 | tf_op jit(solution)/shard_map/attention_layer/pallas_call | solution.py:489
  69.2 4.2 %all-to-all-start.1 = ((f32[4,72,128]{2,1,0:T(8,128)}), f32[4,72,128]{2,1,0:T(8,128)S(1)}, u32[]{:S(2)}, u32[]{:S(2)}) async-start(f32[4,72,128]{2,1,0:T(8,128)} %get-tuple-element.21.sums_ref), calls=%async_computation.1 | async-start | bytes 294912 | tf_op jit(solution)/shard_map/all_to_all | solution.py:603
  73.4 0.9 %copy-done.2 = f32[4,72,128]{2,1,0:T(8,128)S(1)} copy-done((f32[4,72,128]{2,1,0:T(8,128)S(1)}, f32[4,72,128]{2,1,0:T(8,128)}, u32[]{:S(2)}) %copy-start.2) | copy-done | bytes 147480
  74.3 2.8 %all-to-all-done.1.parts_ref = f32[4,72,128]{2,1,0:T(8,128)S(1)} async-done(((f32[4,72,128]{2,1,0:T(8,128)}), f32[4,72,128]{2,1,0:T(8,128)S(1)}, u32[]{:S(2)}, u32[]{:S(2)}) %all-to-all-start.1) | async-done | bytes 147488 | tf_op jit(solution)/shard_map/all_to_all | solution.py:603
  77.1 0.7 relay_sums.1
  77.8 3.4 %all-to-all-start.2 = ((f32[8,72,128]{2,1,0:T(8,128)}), f32[8,72,128]{2,1,0:T(8,128)S(1)}, u32[]{:S(2)}, u32[]{:S(2)}) async-start(f32[8,72,128]{2,1,0:T(8,128)} %relay_sums.1), calls=%async_computation.2 | async-start | bytes 589824 | tf_op jit(solution)/shard_map/all_to_all | solution.py:603
  81.3 2.3 %copy_bitcast_fusion = bf16[64,8192]{1,0:T(8,128)(2,1)} fusion(bf16[64,64,128]{2,1,0:T(8,128)(2,1)} %get-tuple-element.23), kind=kLoop, calls=%fused_computation | loop fusion | bytes 2097152 | tf_op jit(solution)/shard_map/reshape | solution.py:586
  83.6 5.1 %all-to-all-done.2.parts_ref = f32[8,72,128]{2,1,0:T(8,128)S(1)} async-done(((f32[8,72,128]{2,1,0:T(8,128)}), f32[8,72,128]{2,1,0:T(8,128)S(1)}, u32[]{:S(2)}, u32[]{:S(2)}) %all-to-all-start.2) | async-done | bytes 294944 | tf_op jit(solution)/shard_map/all_to_all | solution.py:603
  88.7 0.6 last_sums.1
  (12 shorter events, 0.0 us)
Async XLA Ops:
  0.6 0.8 copy-start
  1.5 1.6 %copy-start.1 = (bf16[8192,128]{1,0:T(8,128)(2,1)S(1)}, bf16[8192,128]{1,0:T(8,128)(2,1)}, u32[]{:S(2)}) copy-start(bf16[8192,128]{1,0:T(8,128)(2,1)} %own_hbm.1) | copy-start | bytes 6291460
  12.2 9.2 %copy-start.6 = (s32[64,5]{0,1:T(8,128)S(1)}, s32[64,5]{0,1:T(8,128)}, u32[]{:S(2)}) copy-start(s32[64,5]{0,1:T(8,128)} %param.16) | copy-start | bytes 3844
  12.2 9.2 %copy-start.7 = (s32[64,3]{0,1:T(4,128)S(1)}, s32[64,3]{0,1:T(4,128)}, u32[]{:S(2)}) copy-start(s32[64,3]{0,1:T(4,128)} %param.18) | copy-start | bytes 2308
  12.2 10.0 %copy-start.5 = (bf16[128,64]{0,1:T(8,128)(2,1)S(1)}, bf16[128,64]{0,1:T(8,128)(2,1)}, u32[]{:S(2)}) copy-start(bf16[128,64]{0,1:T(8,128)(2,1)} %param.12) | copy-start | bytes 49156
  12.2 10.7 %copy-start.4 = (s32[64,3,128]{2,0,1:T(8,128)S(1)}, s32[64,3,128]{2,0,1:T(8,128)}, u32[]{:S(2)}) copy-start(s32[64,3,128]{2,0,1:T(8,128)} %param.19) | copy-start | bytes 294916
  12.3 11.4 %copy-start.3 = (s32[64,5,128]{2,0,1:T(8,128)S(1)}, s32[64,5,128]{2,0,1:T(8,128)}, u32[]{:S(2)}) copy-start(s32[64,5,128]{2,0,1:T(8,128)} %param.17) | copy-start | bytes 491524
  12.3 12.9 %copy-start.8 = (f32[2,1,64]{2,1,0:T(1,128)S(1)}, f32[2,1,64]{2,1,0:T(1,128)}, u32[]{:S(2)}) copy-start(f32[2,1,64]{2,1,0:T(1,128)} %param.13) | copy-start | bytes 1540
  12.3 12.9 %copy-start.9 = (f32[64]{0:T(128)S(1)}, f32[64]{0:T(128)}, u32[]{:S(2)}) copy-start(f32[64]{0:T(128)} %param.14) | copy-start | bytes 772
  12.3 37.5 %all-to-all-start = ((bf16[32,256,128]{2,1,0:T(8,128)(2,1)}), bf16[32,256,128]{2,1,0:T(8,128)(2,1)}, u32[]{:S(2)}, u32[]{:S(2)}) async-start(bf16[32,256,128]{2,1,0:T(8,128)(2,1)} %bitcast.4), calls=%async_computation | async-start | bytes 4194304 | tf_op jit(solution)/shard_map/all_to_all | solution.py:541
  69.2 7.9 %all-to-all-start.1 = ((f32[4,72,128]{2,1,0:T(8,128)}), f32[4,72,128]{2,1,0:T(8,128)S(1)}, u32[]{:S(2)}, u32[]{:S(2)}) async-start(f32[4,72,128]{2,1,0:T(8,128)} %get-tuple-element.21.sums_ref), calls=%async_computation.1 | async-start | bytes 294912 | tf_op jit(solution)/shard_map/all_to_all | solution.py:603
  73.4 0.9 %copy-start.2 = (f32[4,72,128]{2,1,0:T(8,128)S(1)}, f32[4,72,128]{2,1,0:T(8,128)}, u32[]{:S(2)}) copy-start(f32[4,72,128]{2,1,0:T(8,128)} %get-tuple-element.21.sums_ref) | copy-start | bytes 442372
  77.8 10.8 %all-to-all-start.2 = ((f32[8,72,128]{2,1,0:T(8,128)}), f32[8,72,128]{2,1,0:T(8,128)S(1)}, u32[]{:S(2)}, u32[]{:S(2)}) async-start(f32[8,72,128]{2,1,0:T(8,128)} %relay_sums.1), calls=%async_computation.2 | async-start | bytes 589824 | tf_op jit(solution)/shard_map/all_to_all | solution.py:603
